TPU v7x, 32 devices: a whole 2x2x4 slice. The times are simulated.
32 devices in a mesh: row: 2 (over y), col: 4 (over z), depth: 4 (over x, core).
Axes of the slice: x: 2, y: 2, z: 4, core: 2. Of those that a mesh axis runs over, the one named last changes fastest.
Arguments:
- a_blocks: bfloat16 [2, 4, 4, 16, 64, 256], P('row', 'col', 'depth'), may hold values from -0.5 to 0.5
- a_columns: int32 [2, 4, 4, 16, 4], P('row', 'col', 'depth'), may hold values from 0 to 127, as said below
- a_counts: int32 [2, 4, 4, 16], P('row', 'col', 'depth'), may hold values from 1 to 4, as said below
- b_blocks: bfloat16 [2, 4, 4, 128, 64, 128], P('row', 'col', 'depth'), may hold values from -6 to 6
- b_columns: int32 [2, 4, 4, 128, 2], P('row', 'col', 'depth'), may hold values from 0 to 191, as said below
- b_counts: int32 [2, 4, 4, 128], P('row', 'col', 'depth'), may hold values from 1 to 2, as said below
- c_columns: int32 [2, 4, 16, 4], P('row', 'col'), may hold values from 0 to 191, as said below
- c_counts: int32 [2, 4, 16], P('row', 'col'), may hold values from 1 to 4, as said below
Outputs:
- c_blocks: bfloat16 [2, 4, 16, 64, 256], P('row', 'col', 'depth')
Inputs may be any that keep to these rules, and one draw needn't show every extreme that they name: `a_columns`: within one block row the listed inner blocks are distinct. `a_counts`: every A panel has a block row with 4 live slots. `b_columns`: within one block row the listed block columns are distinct. `b_counts`: the counts of every B panel sum to exactly 160. `c_columns`: within one block row the listed block columns are distinct. `c_counts`: every grid position has a block row with 4 live slots.
All inputs are finite; a program needn't handle non-finite values.
Results may differ from a plain program's by a relative error of at most 0.0065.
Values may be sent and summed in bfloat16 or wider, within the bound.
No kernel may reach another device: no remote copies, remote signals or barrier semaphores. Data moves between devices by JAX's collectives and lax.ppermute only.
A program may use at most 64 MiB of HBM per device.

v0:
```python
import jax
import jax.numpy as jnp
from jax import lax
from jax.sharding import PartitionSpec as P


def shifted(value, axis, steps):
    count = lax.axis_size(axis)
    pairs = [(source, (source + steps) % count) for source in range(count)]
    return lax.ppermute(value, axis, pairs)


def block_product(
    a_panel, a_cols, a_live_counts, b_panel, b_cols, b_live_counts, c_cols, c_live_counts
):
    row_count, block_size, a_width = a_panel.shape
    a_slots = a_cols.shape[1]
    b_slots = b_cols.shape[1]
    c_slots = c_cols.shape[1]
    a_split = a_panel.reshape(row_count, block_size, a_slots, block_size)
    b_rows = b_panel[a_cols]
    products = jnp.einsum("ipak,iakq->iapq", a_split, b_rows, preferred_element_type=jnp.float32)
    products = products.reshape(row_count, a_slots, block_size, b_slots, block_size)
    a_live = jnp.arange(a_slots, dtype=jnp.int32)[None, :] < a_live_counts[:, None]
    b_live = (jnp.arange(b_slots, dtype=jnp.int32)[None, :] < b_live_counts[:, None])[a_cols]
    b_target = b_cols[a_cols]
    c_live = jnp.arange(c_slots, dtype=jnp.int32)[None, :] < c_live_counts[:, None]
    matched = (
        (b_target[:, :, :, None] == c_cols[:, None, None, :])
        & a_live[:, :, None, None]
        & b_live[:, :, :, None]
        & c_live[:, None, None, :]
    )
    summed = jnp.einsum(
        "iapjq,iajm->ipmq", products, matched.astype(jnp.float32), precision=lax.Precision.HIGHEST
    )
    return summed.reshape(row_count, block_size, c_slots * block_size)


def local(a_blocks, a_columns, a_counts, b_blocks, b_columns, b_counts, c_columns, c_counts):
    a_panel = a_blocks[0, 0, 0]
    a_cols = a_columns[0, 0, 0]
    a_live_counts = a_counts[0, 0, 0]
    b_panel = b_blocks[0, 0, 0]
    b_cols = b_columns[0, 0, 0]
    b_live_counts = b_counts[0, 0, 0]
    c_cols = c_columns[0, 0]
    c_live_counts = c_counts[0, 0]
    partial_value = block_product(
        a_panel, a_cols, a_live_counts, b_panel, b_cols, b_live_counts, c_cols, c_live_counts
    )
    moved_a = shifted(
        (a_panel, a_cols.astype(jnp.bfloat16), a_live_counts.astype(jnp.bfloat16)), "row", -1
    )
    a_panel = moved_a[0]
    a_cols = moved_a[1].astype(jnp.int32)
    a_live_counts = moved_a[2].astype(jnp.int32)
    moved_b = shifted(
        (b_panel, b_cols.astype(jnp.bfloat16), b_live_counts.astype(jnp.bfloat16)), "col", -1
    )
    b_panel = moved_b[0]
    b_cols = moved_b[1].astype(jnp.int32)
    b_live_counts = moved_b[2].astype(jnp.int32)
    partial_value = partial_value + block_product(
        a_panel, a_cols, a_live_counts, b_panel, b_cols, b_live_counts, c_cols, c_live_counts
    )
    summed = lax.psum_scatter(
        partial_value.astype(jnp.bfloat16), "depth", scatter_dimension=0, tiled=True
    )
    return summed[None, None]


def solution(mesh):
    placed = (
        P("row", "col", "depth", None, None, None),
        P("row", "col", "depth", None, None),
        P("row", "col", "depth", None),
        P("row", "col", "depth", None, None, None),
        P("row", "col", "depth", None, None),
        P("row", "col", "depth", None),
        P("row", "col", None, None),
        P("row", "col", None),
    )
    return jax.shard_map(
        local,
        mesh=mesh,
        in_specs=placed,
        out_specs=P("row", "col", "depth", None, None),
        check_vma=False,
    )
```

profile of v0, /device:TPU:0, one launch (start us, length us, event | category | flops | bytes accessed | tf_op | source)
XLA Modules:
  0.0 117.7 jit_solution(5379786672126675195)
XLA Ops:
  6.5 0.0 reduce-scatter.2.cloned.1.call-start
  6.5 0.7 convert_bitcast_fusion
  7.2 3.0 %collective-permute-start.1 = (bf16[16,4]{0,1:T(4,128)(2,1)S(1)}, bf16[16,4]{0,1:T(4,128)(2,1)S(1)}, u32[]{:S(2)}, u32[]{:S(2)}) collective-permute-start(bf16[16,4]{0,1:T(4,128)(2,1)S(1)} %convert_bitcast_fusion), channel_id=1, source_target_pairs={{0,16},{16,0},{1,17},{17,1},{2,18},{18,2},{3,19},{19,3},{4,20},{20... | collective-permute-start | bytes 392 | tf_op jit(solution)/shard_map/ppermute | solution.py:10
  10.2 3.6 %collective-permute-start.4 = (bf16[128,64,128]{2,1,0:T(8,128)(2,1)}, bf16[128,64,128]{2,1,0:T(8,128)(2,1)}, u32[]{:S(2)}, u32[]{:S(2)}) collective-permute-start(bf16[128,64,128]{2,1,0:T(8,128)(2,1)} %bitcast.63), channel_id=1, source_target_pairs={{0,12},{4,0},{8,4},{12,8},{1,13},{5,1},{9,5},{13,9},{2,14},{6,2},{... | collective-permute-start | bytes 6291464 | tf_op jit(solution)/shard_map/ppermute | solution.py:10
  13.8 0.5 collective-permute-start.5
  14.3 0.8 copy.24
  15.1 0.5 collective-permute-start
  15.6 0.7 bitcast_convert_fusion.1
  16.3 1.5 %collective-permute-start.2 = (bf16[16]{0:T(256)(128)(2,1)S(1)}, bf16[16]{0:T(256)(128)(2,1)S(1)}, u32[]{:S(2)}, u32[]{:S(2)}) collective-permute-start(bf16[16]{0:T(256)(128)(2,1)S(1)} %bitcast_convert_fusion.1), channel_id=1, source_target_pairs={{0,16},{16,0},{1,17},{17,1},{2,18},{18,2},{3,19},{19,3},{4,20},{20... | collective-permute-start | bytes 104 | tf_op jit(solution)/shard_map/ppermute | solution.py:10
  17.8 2.0 %reshape_squeeze.3 = bf16[16,64,4,64]{3,2,1,0:T(4,128)(2,1)S(1)} reshape(bf16[1,1,1,16,64,256]{5,4,3,2,1,0:T(8,128)(2,1)} %param.8) | data formatting | bytes 1048576 | tf_op jit(solution)/shard_map/reshape;squeeze | solution.py:20
  19.8 0.8 copy.28
  20.6 0.7 compare_select_fusion.1
  21.3 0.1 copy.25
  21.3 0.1 reshape.119
  21.4 3.2 %gather_fusion.2 = bf16[64,64,128]{2,1,0:T(8,128)(2,1)} fusion(bf16[128,64,128]{2,1,0:T(8,128)(2,1)} %bitcast.64, s32[1024]{0:T(1024)S(1)} %pad_clamp_fusion.1), kind=kCustom, calls=%fused_computation.2 | custom fusion | bytes 2097408 | tf_op jit(solution)/shard_map/gather | solution.py:21
  24.7 1.6 %convolution_bitcast_fusion.1 = f32[16,4,64,128]{3,2,1,0:T(8,128)S(1)} fusion(bf16[16,4,64,128]{3,2,1,0:T(8,128)(2,1)} %bitcast.60, bf16[16,64,4,64]{3,2,1,0:T(4,128)(2,1)S(1)} %reshape_squeeze.3), kind=kOutput, calls=%fused_computation.13 | convolution fusion | flops 67108864 | bytes 3670016 | tf_op jit(solution)/shard_map/ipak,iakq->iapq/dot_general | solution.py:22
  26.3 0.0 copy-start.1
  26.3 0.0 copy-start.2
  26.4 0.0 copy-start.3
  26.4 3.7 %reshape.114 = f32[16,4,64,2,64]{4,3,2,1,0:T(2,128)} reshape(f32[16,4,64,128]{3,2,1,0:T(8,128)S(1)} %convolution_bitcast_fusion.1) | data formatting | bytes 4194304 | tf_op jit(solution)/shard_map/reshape | solution.py:23
  30.1 0.6 gather_fusion
  30.6 0.2 copy.27
  30.9 0.0 copy-done.1
  30.9 0.1 iota_compare_fusion.1
  30.9 0.6 gather_fusion.1
  31.6 0.2 copy.30
  31.8 0.0 copy-done.2
  31.8 0.1 iota_compare_fusion.4
  31.9 0.0 collective-permute-done.2
  31.9 0.7 collective-permute-start.3
  32.5 0.0 copy-done.3
  32.5 0.1 iota_compare_fusion.2
  32.6 0.0 collective-permute-done.1
  32.6 0.1 copy.33
  32.7 0.1 reshape.143
  32.8 26.5 %collective-permute-done.3 = bf16[128]{0:T(256)(128)(2,1)S(1)} collective-permute-done((bf16[128]{0:T(256)(128)(2,1)S(1)}, bf16[128]{0:T(256)(128)(2,1)S(1)}, u32[]{:S(2)}, u32[]{:S(2)}) %collective-permute-start.3) | collective-permute-done | bytes 288 | tf_op jit(solution)/shard_map/ppermute | solution.py:10
  59.4 0.1 iota_compare_fusion
  59.5 0.6 gather_fusion.4
  60.1 0.2 copy.37
  60.3 0.0 collective-permute-done
  60.3 0.6 gather_fusion.3
  60.9 0.2 copy.35
  61.1 0.0 collective-permute-done.5
  61.1 2.0 %reshape.115 = bf16[16,64,4,64]{3,2,1,0:T(4,128)(2,1)S(1)} reshape(bf16[16,64,256]{2,1,0:T(8,128)(2,1)} %collective-permute-done.5) | data formatting | bytes 1048576 | tf_op jit(solution)/shard_map/reshape | solution.py:20
  63.2 0.0 collective-permute-done.4
  63.2 3.3 %gather_fusion.5 = bf16[64,64,128]{2,1,0:T(8,128)(2,1)} fusion(bf16[128,64,128]{2,1,0:T(8,128)(2,1)} %collective-permute-done.4, s32[1024]{0:T(1024)S(1)} %pad_clamp_fusion), kind=kCustom, calls=%fused_computation.5 | custom fusion | bytes 2097408 | tf_op jit(solution)/shard_map/gather | solution.py:21
  66.4 1.6 %convolution_bitcast_fusion = f32[16,4,64,128]{3,2,1,0:T(8,128)S(1)} fusion(bf16[16,4,64,128]{3,2,1,0:T(8,128)(2,1)} %bitcast.59, bf16[16,64,4,64]{3,2,1,0:T(4,128)(2,1)S(1)} %reshape.115), kind=kOutput, calls=%fused_computation.12 | convolution fusion | flops 67108864 | bytes 3670016 | tf_op jit(solution)/shard_map/ipak,iakq->iapq/dot_general | solution.py:22
  68.1 3.7 %reshape.116 = f32[16,4,64,2,64]{4,3,2,1,0:T(2,128)} reshape(f32[16,4,64,128]{3,2,1,0:T(8,128)S(1)} %convolution_bitcast_fusion) | data formatting | bytes 4194304 | tf_op jit(solution)/shard_map/reshape | solution.py:23
  71.8 0.0 copy-start
  71.8 8.9 %fusion = f32[16,4,64,64,1]{3,1,4,2,0:T(4,128)S(1)} fusion(f32[16,4,64,2,64]{4,3,2,1,0:T(2,128)} %reshape.116, s32[16,4,2]{1,2,0:T(2,128)S(1)} %copy.35, s32[16,4]{1,0:T(8,128)S(1)} %copy.28, pred[16,4,2]{1,2,0:T(4,128)(4,1)S(1)} %copy.37, pred[16,4]{1,0:T(8,128)(4,1)S(1)} %get-tuple-element.5, pred[16,4]{1,0:T(8,128)(4,1)S(1)} %get-tuple-element.6), kind=kOutput, calls=%fused_computation.6 | convolution fusion | flops 25167872 | bytes 3146752 | tf_op jit(solution)/shard_map/iapjq,iajm->ipmq/dot_general | solution.py:34
  80.7 0.0 copy-done
  80.7 5.9 %fusion.7 = bf16[16,64,4,64]{3,2,1,0:T(4,128)(2,1)S(1)} fusion(f32[16,4,64,64,1]{3,1,4,2,0:T(4,128)S(1)} %fusion, f32[16,4,64,2,64]{4,3,2,1,0:T(2,128)S(1)} %copy-done, s32[16,4]{1,0:T(8,128)S(1)} %copy.28, s32[16,4,2]{1,2,0:T(2,128)S(1)} %copy.27, pred[16,4]{1,0:T(8,128)(4,1)S(1)} %get-tuple-element.6, pred[16,4,2]{1,2,0:T(4,128)(4,1)S(1)} %copy.30, ...), kind=kOutput, calls=%fused_computation.14 | convolution fusion | flops 25692160 | bytes 3671040 | tf_op jit(solution)/shard_map/iapjq,iajm->ipmq/dot_general | solution.py:34
  86.6 1.5 %convert_element_type.49 = bf16[16,64,256]{2,1,0:T(8,128)(2,1)} reshape(bf16[16,64,4,64]{3,2,1,0:T(4,128)(2,1)S(1)} %fusion.7) | data formatting | bytes 1048576 | tf_op jit(solution)/shard_map/convert_element_type | solution.py:68
  88.0 0.0 reduce-scatter.2.cloned.1.call-update
  88.1 22.8 %reduce-scatter.2.cloned.1.call-done = bf16[4,64,256]{2,1,0:T(8,128)(2,1)} async-done(((bf16[16,64,256]{2,1,0:T(8,128)(2,1)}), bf16[4,64,256]{2,1,0:T(8,128)(2,1)}) %reduce-scatter.2.cloned.1.call-update) | async-done | bytes 131088 | tf_op jit(solution)/shard_map/reduce_scatter | solution.py:67
  (8 shorter events, 0.0 us)
Async XLA Ops:
  6.5 104.3 %reduce-scatter.2.cloned.1.call-start = ((), (), s32[]{:S(2)}) async-start(), calls=%async_computation.1 | async-start | bytes 655360 | tf_op jit(solution)/shard_map/reduce_scatter | solution.py:67
  7.2 25.4 %collective-permute-start.1 = (bf16[16,4]{0,1:T(4,128)(2,1)S(1)}, bf16[16,4]{0,1:T(4,128)(2,1)S(1)}, u32[]{:S(2)}, u32[]{:S(2)}) collective-permute-start(bf16[16,4]{0,1:T(4,128)(2,1)S(1)} %convert_bitcast_fusion), channel_id=1, source_target_pairs={{0,16},{16,0},{1,17},{17,1},{2,18},{18,2},{3,19},{19,3},{4,20},{20... | collective-permute-start | bytes 392 | tf_op jit(solution)/shard_map/ppermute | solution.py:10
  10.2 53.0 %collective-permute-start.4 = (bf16[128,64,128]{2,1,0:T(8,128)(2,1)}, bf16[128,64,128]{2,1,0:T(8,128)(2,1)}, u32[]{:S(2)}, u32[]{:S(2)}) collective-permute-start(bf16[128,64,128]{2,1,0:T(8,128)(2,1)} %bitcast.63), channel_id=1, source_target_pairs={{0,12},{4,0},{8,4},{12,8},{1,13},{5,1},{9,5},{13,9},{2,14},{6,2},{... | collective-permute-start | bytes 6291464 | tf_op jit(solution)/shard_map/ppermute | solution.py:10
  13.8 47.3 %collective-permute-start.5 = (bf16[16,64,256]{2,1,0:T(8,128)(2,1)}, bf16[16,64,256]{2,1,0:T(8,128)(2,1)}, u32[]{:S(2)}, u32[]{:S(2)}) collective-permute-start(bf16[16,64,256]{2,1,0:T(8,128)(2,1)} %bitcast.62), channel_id=1, source_target_pairs={{0,16},{16,0},{1,17},{17,1},{2,18},{18,2},{3,19},{19,3},{4,20},{20... | collective-permute-start | bytes 1572872 | tf_op jit(solution)/shard_map/ppermute | solution.py:10
  15.1 45.2 %collective-permute-start = (bf16[128,2]{1,0:T(8,128)(2,1)S(1)}, bf16[128,2]{1,0:T(8,128)(2,1)S(1)}, u32[]{:S(2)}, u32[]{:S(2)}) collective-permute-start(bf16[128,2]{1,0:T(8,128)(2,1)S(1)} %bitcast_convert_fusion.2), channel_id=1, source_target_pairs={{0,12},{4,0},{8,4},{12,8},{1,13},{5,1},{9,5},{13,9},{2,14},{6,2},{... | collective-permute-start | bytes 1544 | tf_op jit(solution)/shard_map/ppermute | solution.py:10
  16.3 15.6 %collective-permute-start.2 = (bf16[16]{0:T(256)(128)(2,1)S(1)}, bf16[16]{0:T(256)(128)(2,1)S(1)}, u32[]{:S(2)}, u32[]{:S(2)}) collective-permute-start(bf16[16]{0:T(256)(128)(2,1)S(1)} %bitcast_convert_fusion.1), channel_id=1, source_target_pairs={{0,16},{16,0},{1,17},{17,1},{2,18},{18,2},{3,19},{19,3},{4,20},{20... | collective-permute-start | bytes 104 | tf_op jit(solution)/shard_map/ppermute | solution.py:10
  26.3 4.5 %copy-start.1 = (s32[1,1,1,128]{3,2,1,0:T(1,128)S(1)}, s32[1,1,1,128]{3,2,1,0:T(1,128)}, u32[]{:S(2)}) copy-start(s32[1,1,1,128]{3,2,1,0:T(1,128)} %param.13) | copy-start | bytes 1540
  26.3 5.5 %copy-start.2 = (s32[1,1,1,16]{3,2,1,0:T(1,128)S(1)}, s32[1,1,1,16]{3,2,1,0:T(1,128)}, u32[]{:S(2)}) copy-start(s32[1,1,1,16]{3,2,1,0:T(1,128)} %param.10) | copy-start | bytes 196
  26.4 6.2 %copy-start.3 = (s32[1,1,16]{2,1,0:T(1,128)S(1)}, s32[1,1,16]{2,1,0:T(1,128)}, u32[]{:S(2)}) copy-start(s32[1,1,16]{2,1,0:T(1,128)} %param.15) | copy-start | bytes 196
  31.9 27.5 %collective-permute-start.3 = (bf16[128]{0:T(256)(128)(2,1)S(1)}, bf16[128]{0:T(256)(128)(2,1)S(1)}, u32[]{:S(2)}, u32[]{:S(2)}) collective-permute-start(bf16[128]{0:T(256)(128)(2,1)S(1)} %bitcast_convert_fusion), channel_id=1, source_target_pairs={{0,12},{4,0},{8,4},{12,8},{1,13},{5,1},{9,5},{13,9},{2,14},{6,2},{... | collective-permute-start | bytes 776 | tf_op jit(solution)/shard_map/ppermute | solution.py:10
  71.8 8.9 %copy-start = (f32[16,4,64,2,64]{4,3,2,1,0:T(2,128)S(1)}, f32[16,4,64,2,64]{4,3,2,1,0:T(2,128)}, u32[]{:S(2)}) copy-start(f32[16,4,64,2,64]{4,3,2,1,0:T(2,128)} %reshape.114) | copy-start | bytes 6291460
Sparse Core Ops, SparseCore 0:
  88.2 22.6 reduce-scatter.1
where the time goes:
time: 118 us
  waiting for transfers between devices  49.4 us (42%)
  local copies, waits for them, and re-layouts  24.6 us (21%)
  matrix products  18 us (15%)
  between operations  13.5 us (11%)
  starting transfers between devices  9.75 us (8%)
  other arithmetic  2.39 us (2%)
    ppermute x6, waiting for transfers between devices, shifted(): return lax.ppermute(value, axis, pairs)  26.6 us
    reduce_scatter x1, waiting for transfers between devices, local(): lax.psum_scatter(partial_value.astype(jnp.bfloat16), 'depth', scatter_dim...  22.8 us
    dot_general x2, matrix products, block_product(): jnp.einsum('iapjq,iajm->ipmq', products, matched.astype(jnp.float32), pre...  14.7 us
    ppermute x6, starting transfers between devices, shifted(): return lax.ppermute(value, axis, pairs)  9.75 us
    reshape x2, local copies, waits for them, and re-layouts, block_product(): products.reshape(row_count, a_slots, block_size, b_slots, block_size)  7.39 us
    gather x2, local copies, waits for them, and re-layouts, block_product(): b_rows = b_panel[a_cols]  6.51 us
    dot_general x2, matrix products, block_product(): jnp.einsum('ipak,iakq->iapq', a_split, b_rows, preferred_element_type=jnp...  3.28 us
  transfers between devices with their start and end apart: 7, of which 2 were waited for; matrix products, arithmetic and copies ran while one was open for 17% of the time, Pallas kernels for 0%

commit v1 on v0

v1 whole, which is shorter than its diff:
```python
import functools

import jax
import jax.numpy as jnp
from jax import lax
from jax.experimental import pallas as pl
from jax.experimental.pallas import tpu as pltpu
from jax.sharding import PartitionSpec as P

SMEM = pltpu.SMEM
VMEM = pltpu.VMEM


def select_row(i, b_ref, lists, sel_ref):
    a_col, a_cnt, b_col, b_cnt, c_col, c_cnt = lists
    block, width = b_ref.shape[1:]
    a_slots, c_slots = a_col.shape[0], c_col.shape[0]
    left = lax.broadcasted_iota(jnp.int32, (1, width), 1) < block
    target = [jnp.where(m < c_cnt[0, i], c_col[m, i], -1) for m in range(c_slots)]
    pairs = [jnp.where(left, target[m], target[m + 1]) for m in range(0, c_slots, 2)]
    for a in range(a_slots):
        k = a_col[a, i]
        live = jnp.where(a < a_cnt[0, i], b_cnt[0, k], 0)
        first = jnp.where(0 < live, b_col[0, k], -2)
        second = jnp.where(1 < live, b_col[1, k], -2)
        straight = jnp.where(left, first, second)
        crossed = jnp.where(left, second, first)
        rows = b_ref[k]
        swapped = jnp.concatenate([rows[:, block:], rows[:, :block]], axis=1)
        for p, wanted in enumerate(pairs):
            keep = (straight == wanted).astype(jnp.float32).astype(rows.dtype)
            swap = (crossed == wanted).astype(jnp.float32).astype(rows.dtype)
            sel_ref[a * block : (a + 1) * block, p * width : (p + 1) * width] = rows * keep + swapped * swap


def chunk_rows(total, parts):
    return total // parts


def own_kernel(parts, a_ref, b_ref, a_col, a_cnt, b_col, b_cnt, c_col, c_cnt, *rest):
    outs, sel = rest[:parts], rest[parts]
    lists = (a_col, a_cnt, b_col, b_cnt, c_col, c_cnt)
    me = lax.axis_index("depth")
    rows = a_ref.shape[0] // parts
    for n in range(parts):
        base = (me ^ n) * rows

        def body(j, carry, n=n, base=base):
            i = base + j
            select_row(i, b_ref, lists, sel.at[j % 2])
            got = jnp.dot(a_ref[i], sel[j % 2], preferred_element_type=jnp.float32)
            outs[n][j] = got.astype(outs[n].dtype)
            return carry

        lax.fori_loop(0, rows, body, 0, unroll=2)


def select_kernel(parts, b_ref, a_col, a_cnt, b_col, b_cnt, c_col, c_cnt, *outs):
    lists = (a_col, a_cnt, b_col, b_cnt, c_col, c_cnt)
    me = lax.axis_index("depth")
    rows = outs[0].shape[0]
    for n in range(parts):
        base = (me ^ n) * rows

        def body(j, carry, n=n, base=base):
            select_row(base + j, b_ref, lists, outs[n].at[j])
            return carry

        lax.fori_loop(0, rows, body, 0, unroll=2)


def far_kernel(order, a_ref, *refs):
    count = len(order)
    sels, outs = refs[:count], refs[count:]
    me = lax.axis_index("depth")
    rows = a_ref.shape[0] // count
    for sel, out, n in zip(sels, outs, order):
        base = ((me ^ n) % count) * rows
        for j in range(rows):
            got = jnp.dot(a_ref[base + j], sel[j], preferred_element_type=jnp.float32)
            out[j] = got.astype(out.dtype)


def sent(value, sizes, shift_row, shift_col, flip_depth):
    rows, cols, layers = sizes
    pairs = []
    for r in range(rows):
        for c in range(cols):
            for l in range(layers):
                here = (r * cols + c) * layers + l
                there = (((r + shift_row) % rows) * cols + (c + shift_col) % cols) * layers + (l ^ flip_depth)
                pairs.append((here, there))
    return lax.ppermute(value, ("row", "col", "depth"), pairs)


def local(sizes, a_blocks, a_columns, a_counts, b_blocks, b_columns, b_counts, c_columns, c_counts):
    layers = sizes[2]
    a = a_blocks[0, 0, 0]
    b = b_blocks[0, 0, 0]
    a_col, a_cnt = a_columns[0, 0, 0].T, a_counts[0, 0]
    b_col, b_cnt = b_columns[0, 0, 0].T, b_counts[0, 0]
    c_col, c_cnt = c_columns[0, 0].T, c_counts[0]
    total, block, width = a.shape
    rows = total // layers
    half = layers // 2
    out_width = c_col.shape[0] * block
    me = lax.axis_index("depth")
    spec = lambda space: pl.BlockSpec(memory_space=space)
    piece = jax.ShapeDtypeStruct((rows, block, out_width), a.dtype)

    far_a = []
    for side in (1, 0):
        start = ((me // half) ^ side) * (half * rows)
        part = lax.dynamic_slice_in_dim(a, start, half * rows, 0)
        far_a.append(sent(part, sizes, -1, 1, 0))
    far_a_col = sent(a_col, sizes, -1, 1, 0)
    far_a_cnt = sent(a_cnt, sizes, -1, 1, 0)
    far_c_col = sent(c_col, sizes, 0, 1, 0)
    far_c_cnt = sent(c_cnt, sizes, 0, 1, 0)

    own = pl.pallas_call(
        functools.partial(own_kernel, layers),
        out_shape=[piece] * layers,
        in_specs=[spec(VMEM)] * 2 + [spec(SMEM)] * 6,
        out_specs=[spec(VMEM)] * layers,
        scratch_shapes=[VMEM((2, width, out_width), a.dtype)],
        cost_estimate=pl.CostEstimate(flops=2 * total * block * width * out_width, bytes_accessed=4 << 20, transcendentals=0),
        name="own_product",
    )(a, b, a_col, a_cnt, b_col, b_cnt, c_col, c_cnt)
    pieces = [own[0]] + [sent(own[n], sizes, 0, 0, n) for n in range(1, layers)]

    chosen = pl.pallas_call(
        functools.partial(select_kernel, layers),
        out_shape=[jax.ShapeDtypeStruct((rows, width, out_width), a.dtype)] * layers,
        in_specs=[spec(VMEM)] + [spec(SMEM)] * 6,
        out_specs=[spec(VMEM)] * layers,
        cost_estimate=pl.CostEstimate(flops=0, bytes_accessed=4 << 20, transcendentals=0),
        name="far_select",
    )(b, far_a_col, far_a_cnt, b_col, b_cnt, far_c_col, far_c_cnt)
    for side, part in zip((1, 0), far_a):
        order = tuple(range(side * half, (side + 1) * half))
        got = pl.pallas_call(
            functools.partial(far_kernel, order),
            out_shape=[piece] * half,
            in_specs=[spec(VMEM)] * (1 + half),
            out_specs=[spec(VMEM)] * half,
            cost_estimate=pl.CostEstimate(flops=total * block * width * out_width, bytes_accessed=2 << 20, transcendentals=0),
            name="far_product",
        )(part, *[chosen[n] for n in order])
        pieces += [sent(one, sizes, 0, -1, n) for one, n in zip(got, order)]
    outcome = sum(one.astype(jnp.float32) for one in pieces)
    return outcome.astype(a.dtype)[None, None]


def solution(mesh):
    placed = (
        P("row", "col", "depth", None, None, None),
        P("row", "col", "depth", None, None),
        P("row", "col", "depth", None),
        P("row", "col", "depth", None, None, None),
        P("row", "col", "depth", None, None),
        P("row", "col", "depth", None),
        P("row", "col", None, None),
        P("row", "col", None),
    )
    sizes = (mesh.shape["row"], mesh.shape["col"], mesh.shape["depth"])
    return jax.shard_map(
        functools.partial(local, sizes),
        mesh=mesh,
        in_specs=placed,
        out_specs=P("row", "col", "depth", None, None),
        check_vma=False,
    )
```

time: 118 us -> 59.4 us (0.50)
  waiting for transfers between devices: 49.4 us -> 27.6 us
  local copies, waits for them, and re-layouts: 24.6 us -> 3.07 us
  matrix products: 18 us -> 0 us
  between operations: 13.5 us -> 0.06 us
  Pallas kernels: 0 us -> 13.4 us
  starting transfers between devices: 9.75 us -> 14.3 us
  other arithmetic: 2.39 us -> 0.79 us
    reduce_scatter x1 -> x0, waiting for transfers between devices: 22.8 us -> none  [local(): lax.psum_scatter(partial_value.astype(jnp.bfloat16), 'depth', scatter_dim...]
    dot_general x4 -> x0, matrix products: 18 us -> none  [the longest x2 14.7 us: block_product(): jnp.einsum('iapjq,iajm->ipmq', products, matched.astype(jnp.float32), pre...]
    pallas_call x0 -> x4, Pallas kernels: none -> 13.4 us  [the longest x1 4.96 us: local(): pl.pallas_call(functools.partial(own_kernel, layers), out_shape=[piece] *...]
    gather x10 -> x0, local copies, waits for them, and re-layouts: 9.8 us -> none  [the longest x2 6.51 us: block_product(): b_rows = b_panel[a_cols]]
    reshape x3 -> x0, local copies, waits for them, and re-layouts: 9.42 us -> none  [the longest x2 7.39 us: block_product(): products.reshape(row_count, a_slots, block_size, b_slots, block_size)]
    ppermute x6 -> x13, starting transfers between devices: 9.75 us -> 14.3 us  [sent(): return lax.ppermute(value, ('row', 'col', 'depth'), pairs)]
    another operation x1 -> x0, local copies, waits for them, and re-layouts: 2.03 us -> none  [block_product(): a_split = a_panel.reshape(row_count, block_size, a_slots, block_size)]
    convert_element_type x1 -> x0, local copies, waits for them, and re-layouts: 1.46 us -> none  [local(): partial_value.astype(jnp.bfloat16)]
  transfers between devices with their start and end apart: 7 -> 13, of which waited for: 2 -> 7; matrix products, arithmetic and copies ran while one was open for 17% -> 0% of each run, Pallas kernels for 0% -> 23%
where the time goes in v1:
time: 59.4 us; the launch traced here: 59.2 us
  waiting for transfers between devices  27.6 us (46%)
  starting transfers between devices  14.3 us (24%)
  Pallas kernels  13.4 us (23%)
  local copies, waits for them, and re-layouts  3.07 us (5%)
  other arithmetic  0.79 us (1%)
    ppermute x13, waiting for transfers between devices, sent(): return lax.ppermute(value, ('row', 'col', 'depth'), pairs)  27.6 us
    ppermute x13, starting transfers between devices, sent(): return lax.ppermute(value, ('row', 'col', 'depth'), pairs)  14.3 us
    pallas_call x1, Pallas kernels, local(): pl.pallas_call(functools.partial(own_kernel, layers), out_shape=[piece] *...  4.96 us
    pallas_call x2, Pallas kernels, local(): pl.pallas_call(functools.partial(far_kernel, order), out_shape=[piece] *...  4.45 us
    pallas_call x1, Pallas kernels, local(): pl.pallas_call(functools.partial(select_kernel, layers), out_shape=[jax.S...  3.96 us
    unnamed x22, local copies, waits for them, and re-layouts  1.95 us
  transfers between devices with their start and end apart: 13, of which 7 were waited for; matrix products, arithmetic and copies ran while one was open for 0% of the time, Pallas kernels for 23%

profile of v1, /device:TPU:0, one launch (start us, length us, event | category | flops | bytes accessed | tf_op | source)
XLA Modules:
  0.0 59.2 jit_solution(13875583522258877160)
XLA Ops:
  0.0 0.0 copy-start.3
  0.0 0.0 copy-start.4
  0.0 0.0 copy-start.7
  0.0 0.0 copy-start.8
  0.0 1.1 %dynamic-slice_bitcast_fusion.1 = (bf16[8,64,256]{2,1,0:T(8,128)(2,1)S(1)}, bf16[8,64,256]{2,1,0:T(8,128)(2,1)S(1)}) fusion(bf16[1,1,1,16,64,256]{5,4,3,2,1,0:T(8,128)(2,1)} %param.8, s32[]{:T(128)S(6)} %select_n.13, s32[]{:T(128)S(6)} %select_n.14), kind=kLoop, calls=%fused_computation.2 | loop fusion | bytes 1048584 | tf_op jit(solution)/shard_map/dynamic_slice | solution.py:114
  1.1 4.0 %collective-permute-start.3 = (bf16[8,64,256]{2,1,0:T(8,128)(2,1)S(1)}, bf16[8,64,256]{2,1,0:T(8,128)(2,1)S(1)}, u32[]{:S(2)}, u32[]{:S(2)}) collective-permute-start(bf16[8,64,256]{2,1,0:T(8,128)(2,1)S(1)} %get-tuple-element.29), channel_id=1, source_target_pairs={{0,20},{1,21},{2,22},{3,23},{4,24},{5,25},{6,26},{7,27},{8,28},{9,... | collective-permute-start | bytes 786440 | tf_op jit(solution)/shard_map/ppermute | solution.py:93
  5.2 1.5 %collective-permute-start.10 = (bf16[8,64,256]{2,1,0:T(8,128)(2,1)S(1)}, bf16[8,64,256]{2,1,0:T(8,128)(2,1)S(1)}, u32[]{:S(2)}, u32[]{:S(2)}) collective-permute-start(bf16[8,64,256]{2,1,0:T(8,128)(2,1)S(1)} %get-tuple-element.30), channel_id=1, source_target_pairs={{0,20},{1,21},{2,22},{3,23},{4,24},{5,25},{6,26},{7,27},{8,28},{9,... | collective-permute-start | bytes 786440 | tf_op jit(solution)/shard_map/ppermute | solution.py:93
  6.7 5.0 %own_product.1 = (bf16[4,64,256]{2,1,0:T(8,128)(2,1)}, bf16[4,64,256]{2,1,0:T(8,128)(2,1)}, bf16[4,64,256]{2,1,0:T(8,128)(2,1)}, bf16[4,64,256]{2,1,0:T(8,128)(2,1)}) custom-call(bf16[16,64,256]{2,1,0:T(8,128)(2,1)} %bitcast.22, bf16[128,64,128]{2,1,0:T(8,128)(2,1)} %bitcast.20, s32[4,16]{1,0:T(4,128)} %bitcast.25, s32[1,16]{1,0:T(1,128)} %bitcast.31, ...), custom_call_target="tpu_custom_call" | custom-call | flops 134217728 | bytes 4194304 | tf_op jit(solution)/shard_map/own_product/pallas_call | solution.py:121
  11.6 0.0 collective-permute-start
  11.6 1.5 %collective-permute-start.1 = (bf16[4,64,256]{2,1,0:T(8,128)(2,1)}, bf16[4,64,256]{2,1,0:T(8,128)(2,1)S(1)}, u32[]{:S(2)}, u32[]{:S(2)}) collective-permute-start(bf16[4,64,256]{2,1,0:T(8,128)(2,1)} %get-tuple-element.19), channel_id=1, source_target_pairs={{0,2},{1,3},{2,0},{3,1},{4,6},{5,7},{6,4},{7,5},{8,10},{9,11},{10,... | collective-permute-start | bytes 393224 | tf_op jit(solution)/shard_map/ppermute | solution.py:93
  13.2 0.0 copy-done.7
  13.2 2.5 %collective-permute-start.5 = (s32[1,16]{1,0:T(1,128)S(1)}, s32[1,16]{1,0:T(1,128)S(1)}, u32[]{:S(2)}, u32[]{:S(2)}) collective-permute-start(s32[1,16]{1,0:T(1,128)S(1)} %bitcast.32), channel_id=1, source_target_pairs={{0,20},{1,21},{2,22},{3,23},{4,24},{5,25},{6,26},{7,27},{8,28},{9,... | collective-permute-start | bytes 200 | tf_op jit(solution)/shard_map/ppermute | solution.py:93
  15.7 3.7 %collective-permute-done.5.a_cnt = s32[1,16]{1,0:T(1,128)S(1)} collective-permute-done((s32[1,16]{1,0:T(1,128)S(1)}, s32[1,16]{1,0:T(1,128)S(1)}, u32[]{:S(2)}, u32[]{:S(2)}) %collective-permute-start.5) | collective-permute-done | bytes 96 | tf_op jit(solution)/shard_map/ppermute | solution.py:93
  19.4 0.0 copy-done.8
  19.4 0.0 copy-start.9
  19.4 0.0 collective-permute-start.7
  19.4 5.3 %collective-permute-done.7.c_cnt = s32[1,16]{1,0:T(1,128)S(1)} collective-permute-done((s32[1,16]{1,0:T(1,128)S(1)}, s32[1,16]{1,0:T(1,128)S(1)}, u32[]{:S(2)}, u32[]{:S(2)}) %collective-permute-start.7) | collective-permute-done | bytes 96 | tf_op jit(solution)/shard_map/ppermute | solution.py:93
  24.8 0.0 copy-done.3
  24.8 0.0 copy-start.10
  24.8 0.0 collective-permute-start.4
  24.8 6.3 %collective-permute-done.4.a_col = s32[4,16]{1,0:T(4,128)S(1)} collective-permute-done((s32[4,16]{1,0:T(4,128)S(1)}, s32[4,16]{1,0:T(4,128)S(1)}, u32[]{:S(2)}, u32[]{:S(2)}) %collective-permute-start.4) | collective-permute-done | bytes 288 | tf_op jit(solution)/shard_map/ppermute | solution.py:93
  31.1 0.0 copy-done.4
  31.1 0.0 copy-start.5
  31.1 0.0 collective-permute-start.6
  31.1 5.4 %collective-permute-done.6.c_col = s32[4,16]{1,0:T(4,128)S(1)} collective-permute-done((s32[4,16]{1,0:T(4,128)S(1)}, s32[4,16]{1,0:T(4,128)S(1)}, u32[]{:S(2)}, u32[]{:S(2)}) %collective-permute-start.6) | collective-permute-done | bytes 288 | tf_op jit(solution)/shard_map/ppermute | solution.py:93
  36.4 0.0 copy-start.6
  36.4 0.0 copy-start.2
  36.4 0.0 collective-permute-start.2
  36.5 0.0 copy-done.9
  36.5 0.0 copy-done.10
  36.5 0.0 copy-done.5
  36.5 0.5 copy-done.6
  37.0 4.0 %far_select.1 = (bf16[4,256,256]{2,1,0:T(8,128)(2,1)}, bf16[4,256,256]{2,1,0:T(8,128)(2,1)}, bf16[4,256,256]{2,1,0:T(8,128)(2,1)}, bf16[4,256,256]{2,1,0:T(8,128)(2,1)}) custom-call(bf16[128,64,128]{2,1,0:T(8,128)(2,1)} %bitcast.21, s32[4,16]{1,0:T(4,128)} %copy-done.5, s32[1,16]{1,0:T(1,128)} %copy-done.9, s32[2,128]{1,0:T(2,128)} %bitcast.24, ...), custom_call_target="tpu_custom_call" | custom-call | bytes 4194304 | tf_op jit(solution)/shard_map/far_select/pallas_call | solution.py:132
  41.0 0.0 collective-permute-done.3.a_ref
  41.0 0.0 copy-start.1
  41.0 0.7 %copy-done.1 = bf16[8,64,256]{2,1,0:T(8,128)(2,1)} copy-done((bf16[8,64,256]{2,1,0:T(8,128)(2,1)}, bf16[8,64,256]{2,1,0:T(8,128)(2,1)S(1)}, u32[]{:S(2)}) %copy-start.1) | copy-done | bytes 262168
  41.7 2.2 %far_product.2 = (bf16[4,64,256]{2,1,0:T(8,128)(2,1)}, bf16[4,64,256]{2,1,0:T(8,128)(2,1)}) custom-call(bf16[8,64,256]{2,1,0:T(8,128)(2,1)} %copy-done.1, bf16[4,256,256]{2,1,0:T(8,128)(2,1)} %get-tuple-element.21.refs_0_, bf16[4,256,256]{2,1,0:T(8,128)(2,1)} %get-tuple-element.22.refs_1_), custom_call_target="tpu_custom_call" | custom-call | flops 67108864 | bytes 2097152 | tf_op jit(solution)/shard_map/far_product/pallas_call | solution.py:142
  43.9 0.4 collective-permute-start.8
  44.3 0.0 collective-permute-done.10.a_ref
  44.4 0.0 copy-start
  44.4 0.0 collective-permute-start.9
  44.4 0.7 %copy-done = bf16[8,64,256]{2,1,0:T(8,128)(2,1)} copy-done((bf16[8,64,256]{2,1,0:T(8,128)(2,1)}, bf16[8,64,256]{2,1,0:T(8,128)(2,1)S(1)}, u32[]{:S(2)}) %copy-start) | copy-done | bytes 262168
  45.1 2.2 %far_product.3 = (bf16[4,64,256]{2,1,0:T(8,128)(2,1)}, bf16[4,64,256]{2,1,0:T(8,128)(2,1)}) custom-call(bf16[8,64,256]{2,1,0:T(8,128)(2,1)} %copy-done, bf16[4,256,256]{2,1,0:T(8,128)(2,1)} %get-tuple-element.25.refs_0_, bf16[4,256,256]{2,1,0:T(8,128)(2,1)} %get-tuple-element.26.refs_1_), custom_call_target="tpu_custom_call" | custom-call | flops 67108864 | bytes 2097152 | tf_op jit(solution)/shard_map/far_product/pallas_call | solution.py:142
  47.3 0.0 collective-permute-done
  47.3 1.0 %collective-permute-start.11 = (bf16[4,64,256]{2,1,0:T(8,128)(2,1)}, bf16[4,64,256]{2,1,0:T(8,128)(2,1)S(1)}, u32[]{:S(2)}, u32[]{:S(2)}) collective-permute-start(bf16[4,64,256]{2,1,0:T(8,128)(2,1)} %get-tuple-element.27), channel_id=1, source_target_pairs={{0,12},{1,13},{2,14},{3,15},{4,0},{5,1},{6,2},{7,3},{8,4},{9,5},{1... | collective-permute-start | bytes 393224 | tf_op jit(solution)/shard_map/ppermute | solution.py:93
  48.3 0.0 collective-permute-done.1
  48.3 3.1 %collective-permute-start.12 = (bf16[4,64,256]{2,1,0:T(8,128)(2,1)}, bf16[4,64,256]{2,1,0:T(8,128)(2,1)S(1)}, u32[]{:S(2)}, u32[]{:S(2)}) collective-permute-start(bf16[4,64,256]{2,1,0:T(8,128)(2,1)} %get-tuple-element.28), channel_id=1, source_target_pairs={{0,13},{1,12},{2,15},{3,14},{4,1},{5,0},{6,3},{7,2},{8,5},{9,4},{1... | collective-permute-start | bytes 393224 | tf_op jit(solution)/shard_map/ppermute | solution.py:93
  51.4 0.0 collective-permute-done.2
  51.5 0.0 collective-permute-done.8
  51.5 2.4 %collective-permute-done.9 = bf16[4,64,256]{2,1,0:T(8,128)(2,1)S(1)} collective-permute-done((bf16[4,64,256]{2,1,0:T(8,128)(2,1)}, bf16[4,64,256]{2,1,0:T(8,128)(2,1)S(1)}, u32[]{:S(2)}, u32[]{:S(2)}) %collective-permute-start.9) | collective-permute-done | bytes 131104 | tf_op jit(solution)/shard_map/ppermute | solution.py:93
  53.9 2.9 %collective-permute-done.11 = bf16[4,64,256]{2,1,0:T(8,128)(2,1)S(1)} collective-permute-done((bf16[4,64,256]{2,1,0:T(8,128)(2,1)}, bf16[4,64,256]{2,1,0:T(8,128)(2,1)S(1)}, u32[]{:S(2)}, u32[]{:S(2)}) %collective-permute-start.11) | collective-permute-done | bytes 131104 | tf_op jit(solution)/shard_map/ppermute | solution.py:93
  56.7 1.7 %collective-permute-done.12 = bf16[4,64,256]{2,1,0:T(8,128)(2,1)S(1)} collective-permute-done((bf16[4,64,256]{2,1,0:T(8,128)(2,1)}, bf16[4,64,256]{2,1,0:T(8,128)(2,1)S(1)}, u32[]{:S(2)}, u32[]{:S(2)}) %collective-permute-start.12) | collective-permute-done | bytes 131104 | tf_op jit(solution)/shard_map/ppermute | solution.py:93
  58.4 0.0 copy-done.2
  58.4 0.8 %fusion = bf16[1,1,4,64,256]{4,3,2,1,0:T(8,128)(2,1)} fusion(bf16[4,64,256]{2,1,0:T(8,128)(2,1)S(1)} %collective-permute-done.12, bf16[4,64,256]{2,1,0:T(8,128)(2,1)S(1)} %collective-permute-done.11, bf16[4,64,256]{2,1,0:T(8,128)(2,1)S(1)} %collective-permute-done.9, bf16[4,64,256]{2,1,0:T(8,128)(2,1)S(1)} %collective-permute-done.8, ...), kind=kLoop, calls=%fused_computation.3 | loop fusion | flops 1048576 | bytes 1179648 | tf_op jit(solution)/shard_map/broadcast_in_dim | solution.py:152
Async XLA Ops:
  0.0 24.8 %copy-start.3 = (s32[1,1,1,16,4]{3,4,2,1,0:T(4,128)S(1)}, s32[1,1,1,16,4]{3,4,2,1,0:T(4,128)}, u32[]{:S(2)}) copy-start(s32[1,1,1,16,4]{3,4,2,1,0:T(4,128)} %param.9) | copy-start | bytes 772
  0.0 31.1 %copy-start.4 = (s32[1,1,16,4]{2,3,1,0:T(4,128)S(1)}, s32[1,1,16,4]{2,3,1,0:T(4,128)}, u32[]{:S(2)}) copy-start(s32[1,1,16,4]{2,3,1,0:T(4,128)} %param.14) | copy-start | bytes 772
  0.0 13.2 %copy-start.7 = (s32[1,1,1,16]{3,2,1,0:T(1,128)S(1)}, s32[1,1,1,16]{3,2,1,0:T(1,128)}, u32[]{:S(2)}) copy-start(s32[1,1,1,16]{3,2,1,0:T(1,128)} %param.10) | copy-start | bytes 196
  0.0 19.4 %copy-start.8 = (s32[1,1,16]{2,1,0:T(1,128)S(1)}, s32[1,1,16]{2,1,0:T(1,128)}, u32[]{:S(2)}) copy-start(s32[1,1,16]{2,1,0:T(1,128)} %param.15) | copy-start | bytes 196
  1.1 39.9 %collective-permute-start.3 = (bf16[8,64,256]{2,1,0:T(8,128)(2,1)S(1)}, bf16[8,64,256]{2,1,0:T(8,128)(2,1)S(1)}, u32[]{:S(2)}, u32[]{:S(2)}) collective-permute-start(bf16[8,64,256]{2,1,0:T(8,128)(2,1)S(1)} %get-tuple-element.29), channel_id=1, source_target_pairs={{0,20},{1,21},{2,22},{3,23},{4,24},{5,25},{6,26},{7,27},{8,28},{9,... | collective-permute-start | bytes 786440 | tf_op jit(solution)/shard_map/ppermute | solution.py:93
  5.2 39.2 %collective-permute-start.10 = (bf16[8,64,256]{2,1,0:T(8,128)(2,1)S(1)}, bf16[8,64,256]{2,1,0:T(8,128)(2,1)S(1)}, u32[]{:S(2)}, u32[]{:S(2)}) collective-permute-start(bf16[8,64,256]{2,1,0:T(8,128)(2,1)S(1)} %get-tuple-element.30), channel_id=1, source_target_pairs={{0,20},{1,21},{2,22},{3,23},{4,24},{5,25},{6,26},{7,27},{8,28},{9,... | collective-permute-start | bytes 786440 | tf_op jit(solution)/shard_map/ppermute | solution.py:93
  11.6 35.6 %collective-permute-start = (bf16[4,64,256]{2,1,0:T(8,128)(2,1)}, bf16[4,64,256]{2,1,0:T(8,128)(2,1)S(1)}, u32[]{:S(2)}, u32[]{:S(2)}) collective-permute-start(bf16[4,64,256]{2,1,0:T(8,128)(2,1)} %get-tuple-element.18), channel_id=1, source_target_pairs={{0,1},{1,0},{2,3},{3,2},{4,5},{5,4},{6,7},{7,6},{8,9},{9,8},{10,11... | collective-permute-start | bytes 393224 | tf_op jit(solution)/shard_map/ppermute | solution.py:93
  11.6 36.7 %collective-permute-start.1 = (bf16[4,64,256]{2,1,0:T(8,128)(2,1)}, bf16[4,64,256]{2,1,0:T(8,128)(2,1)S(1)}, u32[]{:S(2)}, u32[]{:S(2)}) collective-permute-start(bf16[4,64,256]{2,1,0:T(8,128)(2,1)} %get-tuple-element.19), channel_id=1, source_target_pairs={{0,2},{1,3},{2,0},{3,1},{4,6},{5,7},{6,4},{7,5},{8,10},{9,11},{10,... | collective-permute-start | bytes 393224 | tf_op jit(solution)/shard_map/ppermute | solution.py:93
  13.2 6.2 %collective-permute-start.5 = (s32[1,16]{1,0:T(1,128)S(1)}, s32[1,16]{1,0:T(1,128)S(1)}, u32[]{:S(2)}, u32[]{:S(2)}) collective-permute-start(s32[1,16]{1,0:T(1,128)S(1)} %bitcast.32), channel_id=1, source_target_pairs={{0,20},{1,21},{2,22},{3,23},{4,24},{5,25},{6,26},{7,27},{8,28},{9,... | collective-permute-start | bytes 200 | tf_op jit(solution)/shard_map/ppermute | solution.py:93
  19.4 17.0 %copy-start.9 = (s32[1,16]{1,0:T(1,128)}, s32[1,16]{1,0:T(1,128)S(1)}, u32[]{:S(2)}) copy-start(s32[1,16]{1,0:T(1,128)S(1)} %collective-permute-done.5.a_cnt) | copy-start | bytes 196
  19.4 5.3 %collective-permute-start.7 = (s32[1,16]{1,0:T(1,128)S(1)}, s32[1,16]{1,0:T(1,128)S(1)}, u32[]{:S(2)}, u32[]{:S(2)}) collective-permute-start(s32[1,16]{1,0:T(1,128)S(1)} %bitcast.34), channel_id=1, source_target_pairs={{0,4},{1,5},{2,6},{3,7},{4,8},{5,9},{6,10},{7,11},{8,12},{9,13},{1... | collective-permute-start | bytes 200 | tf_op jit(solution)/shard_map/ppermute | solution.py:93
  24.8 11.7 %copy-start.10 = (s32[1,16]{1,0:T(1,128)}, s32[1,16]{1,0:T(1,128)S(1)}, u32[]{:S(2)}) copy-start(s32[1,16]{1,0:T(1,128)S(1)} %collective-permute-done.7.c_cnt) | copy-start | bytes 196
  24.8 6.3 %collective-permute-start.4 = (s32[4,16]{1,0:T(4,128)S(1)}, s32[4,16]{1,0:T(4,128)S(1)}, u32[]{:S(2)}, u32[]{:S(2)}) collective-permute-start(s32[4,16]{1,0:T(4,128)S(1)} %bitcast.26), channel_id=1, source_target_pairs={{0,20},{1,21},{2,22},{3,23},{4,24},{5,25},{6,26},{7,27},{8,28},{9,... | collective-permute-start | bytes 776 | tf_op jit(solution)/shard_map/ppermute | solution.py:93
  31.1 5.4 %copy-start.5 = (s32[4,16]{1,0:T(4,128)}, s32[4,16]{1,0:T(4,128)S(1)}, u32[]{:S(2)}) copy-start(s32[4,16]{1,0:T(4,128)S(1)} %collective-permute-done.4.a_col) | copy-start | bytes 772
  31.1 5.4 %collective-permute-start.6 = (s32[4,16]{1,0:T(4,128)S(1)}, s32[4,16]{1,0:T(4,128)S(1)}, u32[]{:S(2)}, u32[]{:S(2)}) collective-permute-start(s32[4,16]{1,0:T(4,128)S(1)} %bitcast.28), channel_id=1, source_target_pairs={{0,4},{1,5},{2,6},{3,7},{4,8},{5,9},{6,10},{7,11},{8,12},{9,13},{1... | collective-permute-start | bytes 776 | tf_op jit(solution)/shard_map/ppermute | solution.py:93
  36.4 0.6 copy-start.6
  36.4 22.0 %copy-start.2 = (bf16[4,64,256]{2,1,0:T(8,128)(2,1)S(1)}, bf16[4,64,256]{2,1,0:T(8,128)(2,1)}, u32[]{:S(2)}) copy-start(bf16[4,64,256]{2,1,0:T(8,128)(2,1)} %get-tuple-element.17) | copy-start | bytes 393220
  36.4 15.0 %collective-permute-start.2 = (bf16[4,64,256]{2,1,0:T(8,128)(2,1)}, bf16[4,64,256]{2,1,0:T(8,128)(2,1)S(1)}, u32[]{:S(2)}, u32[]{:S(2)}) collective-permute-start(bf16[4,64,256]{2,1,0:T(8,128)(2,1)} %get-tuple-element.20), channel_id=1, source_target_pairs={{0,3},{1,2},{2,1},{3,0},{4,7},{5,6},{6,5},{7,4},{8,11},{9,10},{10,... | collective-permute-start | bytes 393224 | tf_op jit(solution)/shard_map/ppermute | solution.py:93
  41.0 0.7 %copy-start.1 = (bf16[8,64,256]{2,1,0:T(8,128)(2,1)}, bf16[8,64,256]{2,1,0:T(8,128)(2,1)S(1)}, u32[]{:S(2)}) copy-start(bf16[8,64,256]{2,1,0:T(8,128)(2,1)S(1)} %collective-permute-done.3.a_ref) | copy-start | bytes 786436
  43.9 7.5 %collective-permute-start.8 = (bf16[4,64,256]{2,1,0:T(8,128)(2,1)}, bf16[4,64,256]{2,1,0:T(8,128)(2,1)S(1)}, u32[]{:S(2)}, u32[]{:S(2)}) collective-permute-start(bf16[4,64,256]{2,1,0:T(8,128)(2,1)} %get-tuple-element.23), channel_id=1, source_target_pairs={{0,14},{1,15},{2,12},{3,13},{4,2},{5,3},{6,0},{7,1},{8,6},{9,7},{1... | collective-permute-start | bytes 393224 | tf_op jit(solution)/shard_map/ppermute | solution.py:93
  44.4 0.7 %copy-start = (bf16[8,64,256]{2,1,0:T(8,128)(2,1)}, bf16[8,64,256]{2,1,0:T(8,128)(2,1)S(1)}, u32[]{:S(2)}) copy-start(bf16[8,64,256]{2,1,0:T(8,128)(2,1)S(1)} %collective-permute-done.10.a_ref) | copy-start | bytes 786436
  44.4 9.5 %collective-permute-start.9 = (bf16[4,64,256]{2,1,0:T(8,128)(2,1)}, bf16[4,64,256]{2,1,0:T(8,128)(2,1)S(1)}, u32[]{:S(2)}, u32[]{:S(2)}) collective-permute-start(bf16[4,64,256]{2,1,0:T(8,128)(2,1)} %get-tuple-element.24), channel_id=1, source_target_pairs={{0,15},{1,14},{2,13},{3,12},{4,3},{5,2},{6,1},{7,0},{8,7},{9,6},{1... | collective-permute-start | bytes 393224 | tf_op jit(solution)/shard_map/ppermute | solution.py:93
  47.3 9.5 %collective-permute-start.11 = (bf16[4,64,256]{2,1,0:T(8,128)(2,1)}, bf16[4,64,256]{2,1,0:T(8,128)(2,1)S(1)}, u32[]{:S(2)}, u32[]{:S(2)}) collective-permute-start(bf16[4,64,256]{2,1,0:T(8,128)(2,1)} %get-tuple-element.27), channel_id=1, source_target_pairs={{0,12},{1,13},{2,14},{3,15},{4,0},{5,1},{6,2},{7,3},{8,4},{9,5},{1... | collective-permute-start | bytes 393224 | tf_op jit(solution)/shard_map/ppermute | solution.py:93
  48.3 10.1 %collective-permute-start.12 = (bf16[4,64,256]{2,1,0:T(8,128)(2,1)}, bf16[4,64,256]{2,1,0:T(8,128)(2,1)S(1)}, u32[]{:S(2)}, u32[]{:S(2)}) collective-permute-start(bf16[4,64,256]{2,1,0:T(8,128)(2,1)} %get-tuple-element.28), channel_id=1, source_target_pairs={{0,13},{1,12},{2,15},{3,14},{4,1},{5,0},{6,3},{7,2},{8,5},{9,4},{1... | collective-permute-start | bytes 393224 | tf_op jit(solution)/shard_map/ppermute | solution.py:93

commit v2 on v1

v2 whole, which is shorter than its diff:
```python
import functools

import jax
import jax.numpy as jnp
from jax import lax
from jax.experimental import pallas as pl
from jax.experimental.pallas import tpu as pltpu
from jax.sharding import PartitionSpec as P

ANY = pl.BlockSpec(memory_space=pl.ANY)
AXES = ("row", "col", "depth")


def select_row(i, b_ref, a_list, c_list, b_col, b_cnt, shape, sel_ref):
    a_slots, c_slots = shape
    block, width = b_ref.shape[1:]
    left = lax.broadcasted_iota(jnp.int32, (1, width), 1) < block
    target = [c_list[a_slots + m, i] for m in range(c_slots)]
    pairs = [jnp.where(left, target[m], target[m + 1]) for m in range(0, c_slots, 2)]
    for a in range(a_slots):
        listed = a_list[a, i]
        k = jnp.maximum(listed, 0)
        live = jnp.where(listed < 0, 0, b_cnt[0, k])
        first = jnp.where(0 < live, b_col[0, k], -2)
        second = jnp.where(1 < live, b_col[1, k], -2)
        straight = jnp.where(left, first, second)
        crossed = jnp.where(left, second, first)
        rows = b_ref[k]
        swapped = jnp.concatenate([rows[:, block:], rows[:, :block]], axis=1)
        for p, wanted in enumerate(pairs):
            keep = (straight == wanted).astype(jnp.float32).astype(rows.dtype)
            swap = (crossed == wanted).astype(jnp.float32).astype(rows.dtype)
            sel_ref[a * block : (a + 1) * block, p * width : (p + 1) * width] = rows * keep + swapped * swap


def product_kernel(shape, order, count, a_hbm, b_hbm, a_list_hbm, c_list_hbm, b_col_hbm, b_cnt_hbm, *rest):
    outs, (a_ref, b_ref, a_list, c_list, b_col, b_cnt, sel, sems) = rest[: len(order)], rest[len(order) :]
    pairs = ((a_list_hbm, a_list), (c_list_hbm, c_list), (b_col_hbm, b_col), (b_cnt_hbm, b_cnt), (a_hbm, a_ref), (b_hbm, b_ref))
    copies = [pltpu.make_async_copy(source, target, sems.at[at]) for at, (source, target) in enumerate(pairs)]
    for copy in copies:
        copy.start()
    me = lax.axis_index("depth")
    rows = a_ref.shape[0] // count
    for copy in copies:
        copy.wait()
    for n, out in zip(order, outs):
        slot = me ^ n
        first = slot * rows
        here = (slot % count) * rows
        for j in range(rows):
            select_row(first + j, b_ref, a_list, c_list, b_col, b_cnt, shape, sel.at[j])
        for j in range(rows):
            got = jnp.dot(a_ref[here + j], sel[j], preferred_element_type=jnp.float32)
            out[j] = got.astype(out.dtype)


def product(shape, order, count, a, b, a_list, c_list, b_col, b_cnt, name):
    total, block, width = a.shape
    rows = total // count
    out_width = shape[1] * block
    piece = jax.ShapeDtypeStruct((rows, block, out_width), a.dtype)
    operands = (a, b, a_list, c_list, b_col, b_cnt)
    smem = [pltpu.SMEM(x.shape, x.dtype) for x in operands[2:]]
    return pl.pallas_call(
        functools.partial(product_kernel, shape, order, count),
        out_shape=[piece] * len(order),
        in_specs=[ANY] * len(operands),
        out_specs=[pl.BlockSpec(memory_space=pltpu.VMEM)] * len(order),
        scratch_shapes=[pltpu.VMEM(a.shape, a.dtype), pltpu.VMEM(b.shape, b.dtype), *smem]
        + [pltpu.VMEM((rows, width, out_width), a.dtype), pltpu.SemaphoreType.DMA((len(operands),))],
        compiler_params=pltpu.CompilerParams(vmem_limit_bytes=16 << 20),
        cost_estimate=pl.CostEstimate(flops=2 * total * block * width * out_width, bytes_accessed=4 << 20, transcendentals=0),
        name=name,
    )(*operands)


def sent(value, sizes, shift_row, shift_col, flip_depth):
    rows, cols, layers = sizes
    pairs = []
    for r in range(rows):
        for c in range(cols):
            for l in range(layers):
                here = (r * cols + c) * layers + l
                there = (((r + shift_row) % rows) * cols + (c + shift_col) % cols) * layers + (l ^ flip_depth)
                pairs.append((here, there))
    return lax.ppermute(value, AXES, pairs)


def live_columns(columns, counts):
    slots = columns.shape[1]
    return jnp.where(jnp.arange(slots, dtype=jnp.int32)[:, None] < counts[None, :], columns.T, -1)


def local(sizes, a_blocks, a_columns, a_counts, b_blocks, b_columns, b_counts, c_columns, c_counts):
    layers = sizes[2]
    half = layers // 2
    a, b = a_blocks[0, 0, 0], b_blocks[0, 0, 0]
    b_col, b_cnt = b_columns[0, 0, 0].T, b_counts[0, 0]
    rows = a.shape[0] // layers
    shape = (a_columns.shape[-1], c_columns.shape[-1])
    me = lax.axis_index("depth")

    lists = jnp.concatenate([live_columns(a_columns[0, 0, 0], a_counts[0, 0, 0]), live_columns(c_columns[0, 0], c_counts[0, 0])])
    a_later, lists = lax.optimization_barrier((a, lists))
    far_a = []
    for side, source in ((1, a), (0, a_later)):
        start = ((me // half) ^ side) * (half * rows)
        part = lax.dynamic_slice_in_dim(source, start, half * rows, 0)
        far_a.append(sent(part, sizes, -1, 1, 0))
    far_a_list = sent(lists, sizes, -1, 1, 0)
    far_c_list = sent(lists, sizes, 0, 1, 0)

    own = product(shape, tuple(range(layers)), layers, a, b, lists, lists, b_col, b_cnt, "own_product")
    own, far_a_list, far_c_list = lax.optimization_barrier((own, far_a_list, far_c_list))
    pieces = [own[0]] + [sent(own[n], sizes, 0, 0, n) for n in range(1, layers)]
    for side, part in zip((1, 0), far_a):
        order = tuple(range(side * half, (side + 1) * half))
        if side == 0:
            part, got = lax.optimization_barrier((part, got))
            pieces[-half:] = [sent(one, sizes, 0, -1, n) for one, n in zip(got, range(half, layers))]
        got = product(shape, order, half, part, b, far_a_list, far_c_list, b_col, b_cnt, "far_product")
        pieces += [sent(one, sizes, 0, -1, n) for one, n in zip(got, order)]
    outcome = sum(one.astype(jnp.float32) for one in pieces)
    return outcome.astype(a.dtype)[None, None]


def solution(mesh):
    placed = (
        P("row", "col", "depth", None, None, None),
        P("row", "col", "depth", None, None),
        P("row", "col", "depth", None),
        P("row", "col", "depth", None, None, None),
        P("row", "col", "depth", None, None),
        P("row", "col", "depth", None),
        P("row", "col", None, None),
        P("row", "col", None),
    )
    sizes = tuple(mesh.shape[axis] for axis in AXES)
    return jax.shard_map(
        functools.partial(local, sizes),
        mesh=mesh,
        in_specs=placed,
        out_specs=P("row", "col", "depth", None, None),
        check_vma=False,
    )
```

time: 59.4 us -> 38 us (0.64)
  waiting for transfers between devices: 27.6 us -> 9.82 us
  Pallas kernels: 13.4 us -> 4.78 us
  local copies, waits for them, and re-layouts: 3.07 us -> 5.91 us
  starting transfers between devices: 14.3 us -> 15.6 us
  other arithmetic: 0.79 us -> 1.53 us
    ppermute x13 -> x11, waiting for transfers between devices: 27.6 us -> 9.82 us  [sent(): return lax.ppermute(value, AXES, pairs)]
    pallas_call x4 -> x3, Pallas kernels: 13.4 us -> 4.78 us  [product(): pl.pallas_call(functools.partial(product_kernel, shape, order, count), ou...]
    unnamed x22 -> x10, local copies, waits for them, and re-layouts: 1.95 us -> 3.97 us
    ppermute x13 -> x11, starting transfers between devices: 14.3 us -> 15.6 us  [sent(): return lax.ppermute(value, AXES, pairs)]
    dynamic_slice x1 -> x2, local copies, waits for them, and re-layouts: 1.12 us -> 1.94 us  [local(): part = lax.dynamic_slice_in_dim(source, start, half * rows, 0)]
    select_n x0 -> x1, other arithmetic: none -> 0.72 us  [live_columns(): jnp.where(jnp.arange(slots, dtype=jnp.int32)[:, None] < counts[None, :],...]
  transfers between devices with their start and end apart: 13 -> 11, of which waited for: 7 -> 5; matrix products, arithmetic and copies ran while one was open for 0% -> 5% of each run, Pallas kernels for 23% -> 13%
where the time goes in v2:
time: 38 us; the launch traced here: 37.7 us
  starting transfers between devices  15.6 us (41%)
  waiting for transfers between devices  9.82 us (26%)
  local copies, waits for them, and re-layouts  5.91 us (16%)
  Pallas kernels  4.78 us (13%)
  other arithmetic  1.53 us (4%)
    ppermute x11, starting transfers between devices, sent(): return lax.ppermute(value, AXES, pairs)  15.6 us
    ppermute x11, waiting for transfers between devices, sent(): return lax.ppermute(value, AXES, pairs)  9.82 us
    pallas_call x3, Pallas kernels, product(): pl.pallas_call(functools.partial(product_kernel, shape, order, count), ou...  4.78 us
    unnamed x10, local copies, waits for them, and re-layouts  3.97 us
    dynamic_slice x2, local copies, waits for them, and re-layouts, local(): part = lax.dynamic_slice_in_dim(source, start, half * rows, 0)  1.94 us
    broadcast_in_dim x1, other arithmetic, local(): return outcome.astype(a.dtype)[None, None]  0.8 us
  transfers between devices with their start and end apart: 11, of which 5 were waited for; matrix products, arithmetic and copies ran while one was open for 5% of the time, Pallas kernels for 13%

profile of v2, /device:TPU:0, one launch (start us, length us, event | category | flops | bytes accessed | tf_op | source)
XLA Modules:
  0.0 37.7 jit_solution(17626774454801093399)
XLA Ops:
  0.0 1.0 %dynamic-slice_bitcast_fusion = bf16[8,64,256]{2,1,0:T(8,128)(2,1)S(1)} fusion(bf16[1,1,1,16,64,256]{5,4,3,2,1,0:T(8,128)(2,1)} %param.8, s32[]{:T(128)S(6)} %select_n.23), kind=kLoop, calls=%fused_computation.1 | loop fusion | bytes 524292 | tf_op jit(solution)/shard_map/dynamic_slice | solution.py:108
  1.0 4.0 %collective-permute-start.6 = (bf16[8,64,256]{2,1,0:T(8,128)(2,1)S(1)}, bf16[8,64,256]{2,1,0:T(8,128)(2,1)S(1)}, u32[]{:S(2)}, u32[]{:S(2)}) collective-permute-start(bf16[8,64,256]{2,1,0:T(8,128)(2,1)S(1)} %dynamic-slice_bitcast_fusion), channel_id=1, source_target_pairs={{0,20},{1,21},{2,22},{3,23},{4,24},{5,25},{6,26},{7,27},{8,28},{9,... | collective-permute-start | bytes 786440 | tf_op jit(solution)/shard_map/ppermute | solution.py:86
  5.0 0.7 %bitcast_select_fusion = (s32[4,16]{1,0:T(4,128)S(1)}, s32[4,16]{1,0:T(4,128)S(1)}) fusion(s32[1,1,16,4]{2,3,1,0:T(4,128)} %param.14, s32[16]{0:T(128)} %bitcast.31, s32[1,1,1,16,4]{3,4,2,1,0:T(4,128)} %param.9, s32[16]{0:T(128)} %bitcast.32), kind=kLoop, calls=%fused_computation.4 | loop fusion | flops 256 | bytes 1152 | tf_op jit(solution)/shard_map/jit(_where)/select_n | solution.py:91
  5.7 1.0 %constant_dynamic-slice_fusion = bf16[8,64,256]{2,1,0:T(8,128)(2,1)S(1)} fusion(bf16[16,64,256]{2,1,0:T(8,128)(2,1)} %bitcast.23, s32[]{:T(128)S(6)} %select_n.22), kind=kLoop, calls=%fused_computation.8 | loop fusion | bytes 524292 | tf_op jit(solution)/shard_map/dynamic_slice | solution.py:108
  6.7 1.6 %collective-permute-start.5 = (bf16[8,64,256]{2,1,0:T(8,128)(2,1)S(1)}, bf16[8,64,256]{2,1,0:T(8,128)(2,1)S(1)}, u32[]{:S(2)}, u32[]{:S(2)}) collective-permute-start(bf16[8,64,256]{2,1,0:T(8,128)(2,1)S(1)} %constant_dynamic-slice_fusion), channel_id=1, source_target_pairs={{0,20},{1,21},{2,22},{3,23},{4,24},{5,25},{6,26},{7,27},{8,28},{9,... | collective-permute-start | bytes 786440 | tf_op jit(solution)/shard_map/ppermute | solution.py:86
  8.3 1.6 %collective-permute-start.1 = (s32[8,16]{1,0:T(8,128)S(1)}, s32[8,16]{1,0:T(8,128)S(1)}, u32[]{:S(2)}, u32[]{:S(2)}) collective-permute-start(s32[8,16]{1,0:T(8,128)S(1)} %pad_add_fusion.a_list_hbm.c_list_hbm), channel_id=1, source_target_pairs={{0,4},{1,5},{2,6},{3,7},{4,8},{5,9},{6,10},{7,11},{8,12},{9,13},{1... | collective-permute-start | bytes 1544 | tf_op jit(solution)/shard_map/ppermute | solution.py:86
  9.9 1.2 %collective-permute-start = (s32[8,16]{1,0:T(8,128)S(1)}, s32[8,16]{1,0:T(8,128)S(1)}, u32[]{:S(2)}, u32[]{:S(2)}) collective-permute-start(s32[8,16]{1,0:T(8,128)S(1)} %pad_add_fusion.a_list_hbm.c_list_hbm), channel_id=1, source_target_pairs={{0,20},{1,21},{2,22},{3,23},{4,24},{5,25},{6,26},{7,27},{8,28},{9,... | collective-permute-start | bytes 1544 | tf_op jit(solution)/shard_map/ppermute | solution.py:86
  11.0 0.0 copy-start
  11.0 1.6 %copy-done = bf16[1,1,1,128,64,128]{5,4,3,2,1,0:T(8,128)(2,1)S(1)} copy-done((bf16[1,1,1,128,64,128]{5,4,3,2,1,0:T(8,128)(2,1)S(1)}, bf16[1,1,1,128,64,128]{5,4,3,2,1,0:T(8,128)(2,1)}, u32[]{:S(2)}) %copy-start) | copy-done | bytes 2097176
  12.6 0.0 copy-start.2
  12.6 1.0 %copy-done.2 = bf16[1,1,1,16,64,256]{5,4,3,2,1,0:T(8,128)(2,1)S(1)} copy-done((bf16[1,1,1,16,64,256]{5,4,3,2,1,0:T(8,128)(2,1)S(1)}, bf16[1,1,1,16,64,256]{5,4,3,2,1,0:T(8,128)(2,1)}, u32[]{:S(2)}) %copy-start.2) | copy-done | bytes 524312
  13.7 0.0 copy-start.3
  13.7 0.7 %copy-done.3 = s32[1,1,1,128,2]{3,4,2,1,0:T(2,128)S(1)} copy-done((s32[1,1,1,128,2]{3,4,2,1,0:T(2,128)S(1)}, s32[1,1,1,128,2]{3,4,2,1,0:T(2,128)}, u32[]{:S(2)}) %copy-start.3) | copy-done | bytes 1048
  14.4 0.0 copy-start.4
  14.4 0.7 %copy-done.4 = s32[1,1,1,128]{3,2,1,0:T(1,128)S(1)} copy-done((s32[1,1,1,128]{3,2,1,0:T(1,128)S(1)}, s32[1,1,1,128]{3,2,1,0:T(1,128)}, u32[]{:S(2)}) %copy-start.4) | copy-done | bytes 536
  15.0 0.0 copy-start.1
  15.0 1.9 %own_product.1 = (bf16[4,64,256]{2,1,0:T(8,128)(2,1)S(1)}, bf16[4,64,256]{2,1,0:T(8,128)(2,1)S(1)}, bf16[4,64,256]{2,1,0:T(8,128)(2,1)S(1)}, bf16[4,64,256]{2,1,0:T(8,128)(2,1)S(1)}) custom-call(bf16[16,64,256]{2,1,0:T(8,128)(2,1)S(1)} %bitcast.24, bf16[128,64,128]{2,1,0:T(8,128)(2,1)S(1)} %bitcast.20, s32[8,16]{1,0:T(8,128)S(1)} %pad_add_fusion.a_list_hbm.c_list_hbm, ...), custom_call_target="tpu_custom_call" | custom-call | flops 134217728 | bytes 4194304 | tf_op jit(solution)/shard_map/own_product/pallas_call | solution.py:64
  17.0 2.1 %collective-permute-done.1.c_list_hbm = s32[8,16]{1,0:T(8,128)S(1)} collective-permute-done((s32[8,16]{1,0:T(8,128)S(1)}, s32[8,16]{1,0:T(8,128)S(1)}, u32[]{:S(2)}, u32[]{:S(2)}) %collective-permute-start.1) | collective-permute-done | bytes 544 | tf_op jit(solution)/shard_map/ppermute | solution.py:86
  19.0 0.1 collective-permute-done.a_list_hbm
  19.1 0.0 collective-permute-start.2
  19.1 1.5 %collective-permute-start.3 = (bf16[4,64,256]{2,1,0:T(8,128)(2,1)S(1)}, bf16[4,64,256]{2,1,0:T(8,128)(2,1)S(1)}, u32[]{:S(2)}, u32[]{:S(2)}) collective-permute-start(bf16[4,64,256]{2,1,0:T(8,128)(2,1)S(1)} %get-tuple-element.31), channel_id=1, source_target_pairs={{0,2},{1,3},{2,0},{3,1},{4,6},{5,7},{6,4},{7,5},{8,10},{9,11},{10,... | collective-permute-start | bytes 393224 | tf_op jit(solution)/shard_map/ppermute | solution.py:86
  20.6 0.4 collective-permute-start.4
  21.0 0.0 collective-permute-done.6.a_hbm
  21.0 1.4 %far_product.2 = (bf16[4,64,256]{2,1,0:T(8,128)(2,1)S(1)}, bf16[4,64,256]{2,1,0:T(8,128)(2,1)S(1)}) custom-call(bf16[8,64,256]{2,1,0:T(8,128)(2,1)S(1)} %collective-permute-done.6.a_hbm, bf16[128,64,128]{2,1,0:T(8,128)(2,1)S(1)} %bitcast.21, s32[8,16]{1,0:T(8,128)S(1)} %collective-permute-done.a_list_hbm, s32[8,16]{1,0:T(8,128)S(1)} %collective-permute-done.1.c_list_hbm, ...), custom_call_target="tpu_custom_call" | custom-call | flops 67108864 | bytes 4194304 | tf_op jit(solution)/shard_map/far_product/pallas_call | solution.py:64
  22.4 0.0 collective-permute-done.5.a_hbm
  22.4 2.7 %collective-permute-start.7 = (bf16[4,64,256]{2,1,0:T(8,128)(2,1)S(1)}, bf16[4,64,256]{2,1,0:T(8,128)(2,1)S(1)}, u32[]{:S(2)}, u32[]{:S(2)}) collective-permute-start(bf16[4,64,256]{2,1,0:T(8,128)(2,1)S(1)} %get-tuple-element.38), channel_id=1, source_target_pairs={{0,14},{1,15},{2,12},{3,13},{4,2},{5,3},{6,0},{7,1},{8,6},{9,7},{1... | collective-permute-start | bytes 393224 | tf_op jit(solution)/shard_map/ppermute | solution.py:86
  25.1 0.0 collective-permute-start.8
  25.2 0.0 copy-done.1
  25.2 1.4 %far_product.3 = (bf16[4,64,256]{2,1,0:T(8,128)(2,1)S(1)}, bf16[4,64,256]{2,1,0:T(8,128)(2,1)S(1)}) custom-call(bf16[8,64,256]{2,1,0:T(8,128)(2,1)S(1)} %collective-permute-done.5.a_hbm, bf16[128,64,128]{2,1,0:T(8,128)(2,1)S(1)} %bitcast.22, s32[8,16]{1,0:T(8,128)S(1)} %collective-permute-done.a_list_hbm, s32[8,16]{1,0:T(8,128)S(1)} %collective-permute-done.1.c_list_hbm, ...), custom_call_target="tpu_custom_call" | custom-call | flops 67108864 | bytes 4194304 | tf_op jit(solution)/shard_map/far_product/pallas_call | solution.py:64
  26.6 0.0 collective-permute-done.2
  26.6 0.5 %collective-permute-start.9 = (bf16[4,64,256]{2,1,0:T(8,128)(2,1)S(1)}, bf16[4,64,256]{2,1,0:T(8,128)(2,1)S(1)}, u32[]{:S(2)}, u32[]{:S(2)}) collective-permute-start(bf16[4,64,256]{2,1,0:T(8,128)(2,1)S(1)} %get-tuple-element.41), channel_id=1, source_target_pairs={{0,12},{1,13},{2,14},{3,15},{4,0},{5,1},{6,2},{7,3},{8,4},{9,5},{1... | collective-permute-start | bytes 393224 | tf_op jit(solution)/shard_map/ppermute | solution.py:86
  27.1 0.0 collective-permute-done.3
  27.1 2.2 %collective-permute-start.10 = (bf16[4,64,256]{2,1,0:T(8,128)(2,1)S(1)}, bf16[4,64,256]{2,1,0:T(8,128)(2,1)S(1)}, u32[]{:S(2)}, u32[]{:S(2)}) collective-permute-start(bf16[4,64,256]{2,1,0:T(8,128)(2,1)S(1)} %get-tuple-element.42), channel_id=1, source_target_pairs={{0,13},{1,12},{2,15},{3,14},{4,1},{5,0},{6,3},{7,2},{8,5},{9,4},{1... | collective-permute-start | bytes 393224 | tf_op jit(solution)/shard_map/ppermute | solution.py:86
  29.3 3.8 %collective-permute-done.4 = bf16[4,64,256]{2,1,0:T(8,128)(2,1)S(1)} collective-permute-done((bf16[4,64,256]{2,1,0:T(8,128)(2,1)S(1)}, bf16[4,64,256]{2,1,0:T(8,128)(2,1)S(1)}, u32[]{:S(2)}, u32[]{:S(2)}) %collective-permute-start.4) | collective-permute-done | bytes 131104 | tf_op jit(solution)/shard_map/ppermute | solution.py:86
  33.1 0.0 collective-permute-done.7
  33.1 0.0 collective-permute-done.8
  33.1 2.3 %collective-permute-done.9 = bf16[4,64,256]{2,1,0:T(8,128)(2,1)S(1)} collective-permute-done((bf16[4,64,256]{2,1,0:T(8,128)(2,1)S(1)}, bf16[4,64,256]{2,1,0:T(8,128)(2,1)S(1)}, u32[]{:S(2)}, u32[]{:S(2)}) %collective-permute-start.9) | collective-permute-done | bytes 131104 | tf_op jit(solution)/shard_map/ppermute | solution.py:86
  35.4 1.5 %collective-permute-done.10 = bf16[4,64,256]{2,1,0:T(8,128)(2,1)S(1)} collective-permute-done((bf16[4,64,256]{2,1,0:T(8,128)(2,1)S(1)}, bf16[4,64,256]{2,1,0:T(8,128)(2,1)S(1)}, u32[]{:S(2)}, u32[]{:S(2)}) %collective-permute-start.10) | collective-permute-done | bytes 131104 | tf_op jit(solution)/shard_map/ppermute | solution.py:86
  36.9 0.8 %fusion = bf16[1,1,4,64,256]{4,3,2,1,0:T(8,128)(2,1)} fusion(bf16[4,64,256]{2,1,0:T(8,128)(2,1)S(1)} %collective-permute-done.10, bf16[4,64,256]{2,1,0:T(8,128)(2,1)S(1)} %collective-permute-done.9, bf16[4,64,256]{2,1,0:T(8,128)(2,1)S(1)} %collective-permute-done.8, bf16[4,64,256]{2,1,0:T(8,128)(2,1)S(1)} %collective-permute-done.7, ...), kind=kLoop, calls=%fused_computation.2 | loop fusion | flops 1048576 | bytes 1179648 | tf_op jit(solution)/shard_map/broadcast_in_dim | solution.py:124
  (1 shorter events, 0.0 us)
Async XLA Ops:
  1.0 20.0 %collective-permute-start.6 = (bf16[8,64,256]{2,1,0:T(8,128)(2,1)S(1)}, bf16[8,64,256]{2,1,0:T(8,128)(2,1)S(1)}, u32[]{:S(2)}, u32[]{:S(2)}) collective-permute-start(bf16[8,64,256]{2,1,0:T(8,128)(2,1)S(1)} %dynamic-slice_bitcast_fusion), channel_id=1, source_target_pairs={{0,20},{1,21},{2,22},{3,23},{4,24},{5,25},{6,26},{7,27},{8,28},{9,... | collective-permute-start | bytes 786440 | tf_op jit(solution)/shard_map/ppermute | solution.py:86
  6.7 15.7 %collective-permute-start.5 = (bf16[8,64,256]{2,1,0:T(8,128)(2,1)S(1)}, bf16[8,64,256]{2,1,0:T(8,128)(2,1)S(1)}, u32[]{:S(2)}, u32[]{:S(2)}) collective-permute-start(bf16[8,64,256]{2,1,0:T(8,128)(2,1)S(1)} %constant_dynamic-slice_fusion), channel_id=1, source_target_pairs={{0,20},{1,21},{2,22},{3,23},{4,24},{5,25},{6,26},{7,27},{8,28},{9,... | collective-permute-start | bytes 786440 | tf_op jit(solution)/shard_map/ppermute | solution.py:86
  8.3 10.7 %collective-permute-start.1 = (s32[8,16]{1,0:T(8,128)S(1)}, s32[8,16]{1,0:T(8,128)S(1)}, u32[]{:S(2)}, u32[]{:S(2)}) collective-permute-start(s32[8,16]{1,0:T(8,128)S(1)} %pad_add_fusion.a_list_hbm.c_list_hbm), channel_id=1, source_target_pairs={{0,4},{1,5},{2,6},{3,7},{4,8},{5,9},{6,10},{7,11},{8,12},{9,13},{1... | collective-permute-start | bytes 1544 | tf_op jit(solution)/shard_map/ppermute | solution.py:86
  9.9 9.3 %collective-permute-start = (s32[8,16]{1,0:T(8,128)S(1)}, s32[8,16]{1,0:T(8,128)S(1)}, u32[]{:S(2)}, u32[]{:S(2)}) collective-permute-start(s32[8,16]{1,0:T(8,128)S(1)} %pad_add_fusion.a_list_hbm.c_list_hbm), channel_id=1, source_target_pairs={{0,20},{1,21},{2,22},{3,23},{4,24},{5,25},{6,26},{7,27},{8,28},{9,... | collective-permute-start | bytes 1544 | tf_op jit(solution)/shard_map/ppermute | solution.py:86
  11.0 1.6 %copy-start = (bf16[1,1,1,128,64,128]{5,4,3,2,1,0:T(8,128)(2,1)S(1)}, bf16[1,1,1,128,64,128]{5,4,3,2,1,0:T(8,128)(2,1)}, u32[]{:S(2)}) copy-start(bf16[1,1,1,128,64,128]{5,4,3,2,1,0:T(8,128)(2,1)} %param.11) | copy-start | bytes 6291460
  12.6 1.0 %copy-start.2 = (bf16[1,1,1,16,64,256]{5,4,3,2,1,0:T(8,128)(2,1)S(1)}, bf16[1,1,1,16,64,256]{5,4,3,2,1,0:T(8,128)(2,1)}, u32[]{:S(2)}) copy-start(bf16[1,1,1,16,64,256]{5,4,3,2,1,0:T(8,128)(2,1)} %param.8) | copy-start | bytes 1572868
  13.7 0.7 %copy-start.3 = (s32[1,1,1,128,2]{3,4,2,1,0:T(2,128)S(1)}, s32[1,1,1,128,2]{3,4,2,1,0:T(2,128)}, u32[]{:S(2)}) copy-start(s32[1,1,1,128,2]{3,4,2,1,0:T(2,128)} %param.12) | copy-start | bytes 3076
  14.4 0.7 %copy-start.4 = (s32[1,1,1,128]{3,2,1,0:T(1,128)S(1)}, s32[1,1,1,128]{3,2,1,0:T(1,128)}, u32[]{:S(2)}) copy-start(s32[1,1,1,128]{3,2,1,0:T(1,128)} %param.13) | copy-start | bytes 1540
  15.0 10.2 %copy-start.1 = (bf16[1,1,1,128,64,128]{5,4,3,2,1,0:T(8,128)(2,1)S(1)}, bf16[1,1,1,128,64,128]{5,4,3,2,1,0:T(8,128)(2,1)}, u32[]{:S(2)}) copy-start(bf16[1,1,1,128,64,128]{5,4,3,2,1,0:T(8,128)(2,1)} %param.11) | copy-start | bytes 6291460
  19.1 7.5 %collective-permute-start.2 = (bf16[4,64,256]{2,1,0:T(8,128)(2,1)S(1)}, bf16[4,64,256]{2,1,0:T(8,128)(2,1)S(1)}, u32[]{:S(2)}, u32[]{:S(2)}) collective-permute-start(bf16[4,64,256]{2,1,0:T(8,128)(2,1)S(1)} %get-tuple-element.30), channel_id=1, source_target_pairs={{0,1},{1,0},{2,3},{3,2},{4,5},{5,4},{6,7},{7,6},{8,9},{9,8},{10,11... | collective-permute-start | bytes 393224 | tf_op jit(solution)/shard_map/ppermute | solution.py:86
  19.1 8.0 %collective-permute-start.3 = (bf16[4,64,256]{2,1,0:T(8,128)(2,1)S(1)}, bf16[4,64,256]{2,1,0:T(8,128)(2,1)S(1)}, u32[]{:S(2)}, u32[]{:S(2)}) collective-permute-start(bf16[4,64,256]{2,1,0:T(8,128)(2,1)S(1)} %get-tuple-element.31), channel_id=1, source_target_pairs={{0,2},{1,3},{2,0},{3,1},{4,6},{5,7},{6,4},{7,5},{8,10},{9,11},{10,... | collective-permute-start | bytes 393224 | tf_op jit(solution)/shard_map/ppermute | solution.py:86
  20.6 12.5 %collective-permute-start.4 = (bf16[4,64,256]{2,1,0:T(8,128)(2,1)S(1)}, bf16[4,64,256]{2,1,0:T(8,128)(2,1)S(1)}, u32[]{:S(2)}, u32[]{:S(2)}) collective-permute-start(bf16[4,64,256]{2,1,0:T(8,128)(2,1)S(1)} %get-tuple-element.32), channel_id=1, source_target_pairs={{0,3},{1,2},{2,1},{3,0},{4,7},{5,6},{6,5},{7,4},{8,11},{9,10},{10,... | collective-permute-start | bytes 393224 | tf_op jit(solution)/shard_map/ppermute | solution.py:86
  22.4 10.6 %collective-permute-start.7 = (bf16[4,64,256]{2,1,0:T(8,128)(2,1)S(1)}, bf16[4,64,256]{2,1,0:T(8,128)(2,1)S(1)}, u32[]{:S(2)}, u32[]{:S(2)}) collective-permute-start(bf16[4,64,256]{2,1,0:T(8,128)(2,1)S(1)} %get-tuple-element.38), channel_id=1, source_target_pairs={{0,14},{1,15},{2,12},{3,13},{4,2},{5,3},{6,0},{7,1},{8,6},{9,7},{1... | collective-permute-start | bytes 393224 | tf_op jit(solution)/shard_map/ppermute | solution.py:86
  25.1 8.0 %collective-permute-start.8 = (bf16[4,64,256]{2,1,0:T(8,128)(2,1)S(1)}, bf16[4,64,256]{2,1,0:T(8,128)(2,1)S(1)}, u32[]{:S(2)}, u32[]{:S(2)}) collective-permute-start(bf16[4,64,256]{2,1,0:T(8,128)(2,1)S(1)} %get-tuple-element.39), channel_id=1, source_target_pairs={{0,15},{1,14},{2,13},{3,12},{4,3},{5,2},{6,1},{7,0},{8,7},{9,6},{1... | collective-permute-start | bytes 393224 | tf_op jit(solution)/shard_map/ppermute | solution.py:86
  26.6 8.8 %collective-permute-start.9 = (bf16[4,64,256]{2,1,0:T(8,128)(2,1)S(1)}, bf16[4,64,256]{2,1,0:T(8,128)(2,1)S(1)}, u32[]{:S(2)}, u32[]{:S(2)}) collective-permute-start(bf16[4,64,256]{2,1,0:T(8,128)(2,1)S(1)} %get-tuple-element.41), channel_id=1, source_target_pairs={{0,12},{1,13},{2,14},{3,15},{4,0},{5,1},{6,2},{7,3},{8,4},{9,5},{1... | collective-permute-start | bytes 393224 | tf_op jit(solution)/shard_map/ppermute | solution.py:86
  27.1 9.8 %collective-permute-start.10 = (bf16[4,64,256]{2,1,0:T(8,128)(2,1)S(1)}, bf16[4,64,256]{2,1,0:T(8,128)(2,1)S(1)}, u32[]{:S(2)}, u32[]{:S(2)}) collective-permute-start(bf16[4,64,256]{2,1,0:T(8,128)(2,1)S(1)} %get-tuple-element.42), channel_id=1, source_target_pairs={{0,13},{1,12},{2,15},{3,14},{4,1},{5,0},{6,3},{7,2},{8,5},{9,4},{1... | collective-permute-start | bytes 393224 | tf_op jit(solution)/shard_map/ppermute | solution.py:86

commit v3 on v2

v3 whole, which is shorter than its diff:
```python
import functools

import jax
import jax.numpy as jnp
from jax import lax
from jax.experimental import pallas as pl
from jax.experimental.pallas import tpu as pltpu
from jax.sharding import PartitionSpec as P

ANY = pl.BlockSpec(memory_space=pl.ANY)
HBM = pl.BlockSpec(memory_space=pltpu.HBM)
VMEM = pl.BlockSpec(memory_space=pltpu.VMEM)
DEAD_B, DEAD_C = -2, -1
OWN = 2
FAR = 100
AXES = ("row", "col", "depth")


def fill_b_list(b_list, b_col, b_cnt, block):
    slots, inner = b_col.shape
    width = b_list.shape[1]
    number = lax.broadcasted_iota(jnp.int32, (slots, inner), 0)
    live = jnp.where(number < b_cnt[...], b_col[...], DEAD_B)
    live = jnp.concatenate([live, jnp.full((8 - slots, inner), DEAD_B, jnp.int32)]).T
    first, second = (jnp.broadcast_to(live[:, slot : slot + 1], (inner, width)) for slot in range(2))
    left = lax.broadcasted_iota(jnp.int32, (inner, width), 1) < block
    half = b_list.shape[0] // 2
    b_list[:inner, :] = jnp.where(left, first, second)
    b_list[half : half + inner, :] = jnp.where(left, second, first)
    for start in (inner, half + inner):
        b_list[start : start + half - inner, :] = jnp.full((half - inner, width), DEAD_B, jnp.int32)


def select_row(i, b_ref, lists, b_list, sel_ref):
    inner, block, width = b_ref.shape
    a_slots, c_slots = sel_ref.shape[0] // block, sel_ref.shape[1] // block
    left = lax.broadcasted_iota(jnp.int32, (1, width), 1) < block
    listed = pltpu.roll(lists[...], lists.shape[1] - i, 1)
    target = [listed[a_slots + m, 0] for m in range(c_slots)]
    pairs = [jnp.where(left, target[m], target[m + 1]) for m in range(0, c_slots, 2)]
    for a in range(a_slots):
        k = listed[a, 0]
        straight = b_list[pl.ds(k, 1), :]
        crossed = b_list[pl.ds(k + b_list.shape[0] // 2, 1), :]
        rows = b_ref[jnp.minimum(k, inner - 1)]
        swapped = jnp.concatenate([rows[:, block:], rows[:, :block]], axis=1)
        for p, wanted in enumerate(pairs):
            keep = (straight == wanted).astype(jnp.float32).astype(rows.dtype)
            swap = (crossed == wanted).astype(jnp.float32).astype(rows.dtype)
            sel_ref[a * block : (a + 1) * block, p * width : (p + 1) * width] = rows * keep + swapped * swap


def product_kernel(groups, fills, *refs):
    a_ref, b_ref, a_list, c_list = refs[:4]
    if fills:
        b_col, b_cnt = refs[4:6]
        *outs, b_list, lists, sel = refs[6:]
        fill_b_list(b_list, b_col, b_cnt, b_ref.shape[1])
    else:
        b_list, *outs, lists, sel = refs[4:]
    a_slots, listed = a_list.shape
    lists[:a_slots, :listed] = a_list[...]
    lists[a_slots : a_slots + c_list.shape[0], :listed] = c_list[...]
    me = lax.axis_index("depth")
    rows = sel.shape[0]
    for group, out in zip(groups, outs):
        for at, n in enumerate(group):
            first = (me ^ n) * rows
            for j in range(rows):
                select_row(first + j, b_ref, lists, b_list, sel.at[j])
            for j in range(rows):
                got = jnp.dot(a_ref[first + j], sel[j], preferred_element_type=jnp.float32)
                out[at * rows + j] = got.astype(out.dtype)


def product(layers, groups, a, b, a_list, c_list, b_lists, name, limit, weight):
    total, block, width = a.shape
    inner, _, b_width = b.shape
    rows = total // layers
    out_width = c_list.shape[0] * block
    fills = len(b_lists) == 2
    outs = [jax.ShapeDtypeStruct((len(group) * rows, block, out_width), a.dtype) for group in groups]
    if fills:
        outs.append(jax.ShapeDtypeStruct((2 * (inner + 8), b_width), jnp.int32))
    return pl.pallas_call(
        functools.partial(product_kernel, groups, fills),
        out_shape=outs,
        in_specs=[VMEM] * (4 + len(b_lists)),
        out_specs=[VMEM] * len(outs),
        scratch_shapes=[pltpu.VMEM((8, 128), jnp.int32), pltpu.VMEM((rows, width, out_width), a.dtype)],
        compiler_params=pltpu.CompilerParams(vmem_limit_bytes=limit),
        cost_estimate=pl.CostEstimate(flops=weight * total * block * width * out_width, bytes_accessed=0, transcendentals=0),
        name=name,
    )(a, b, a_list, c_list, *b_lists)


def total_of(pieces, dtype):
    return sum(one.astype(jnp.float32) for one in pieces).astype(dtype)


def sent(value, sizes, shift_row, shift_col, flip_depth):
    rows, cols, layers = sizes
    shifts = [move if isinstance(move, tuple) else (move, move) for move in (shift_row, shift_col, flip_depth)]
    pairs = []
    for r in range(rows):
        for c in range(cols):
            for l in range(layers):
                by_row, by_col, flip = (move[l % 2] for move in shifts)
                here = (r * cols + c) * layers + l
                there = (((r + by_row) % rows) * cols + (c + by_col) % cols) * layers + (l ^ flip)
                pairs.append((here, there))
    return lax.ppermute(value, AXES, pairs)


def live_columns(columns, counts, dead):
    return jnp.where(jnp.arange(columns.shape[1], dtype=jnp.int32)[:, None] < counts[None, :], columns.T, dead)


def local(sizes, a_blocks, a_columns, a_counts, b_blocks, b_columns, b_counts, c_columns, c_counts):
    layers = sizes[2]
    a, b = a_blocks[0, 0, 0], b_blocks[0, 0, 0]
    rows = a.shape[0] // layers
    evens, odds = tuple(range(0, layers, 2)), tuple(range(1, layers, 2))

    far_a = sent(a, sizes, -1, 1, 0)
    a_list = live_columns(a_columns[0, 0, 0], a_counts[0, 0, 0], b.shape[0])
    c_list = live_columns(c_columns[0, 0], c_counts[0, 0], DEAD_C)
    far_a_list = sent(a_list, sizes, -1, 1, 0)
    far_c_list = sent(c_list, sizes, 0, 1, 0)

    def paired(passed, kept):
        met = sent(passed, sizes, 0, 0, 1)
        return [total_of((one, met[at * rows : (at + 1) * rows]), a.dtype) for at, one in enumerate(kept)]

    singles = tuple((n,) for n in evens)
    raw = (b_columns[0, 0, 0].T, b_counts[0, 0])
    passed, *kept, b_list = product(layers, (odds,) + singles, a, b, a_list, c_list, raw, "own_product", 8 << 20, OWN)
    own = paired(passed, kept)
    far_a, own = lax.optimization_barrier((far_a, own))
    (passed,) = product(layers, (odds,), far_a, b, far_a_list, far_c_list, (b_list,), "far_passed", 8 << 20, FAR)
    far_a, passed = lax.optimization_barrier((far_a, passed))
    kept = product(layers, singles, far_a, b, far_a_list, far_c_list, (b_list,), "far_kept", 8 << 20, FAR)
    far = paired(passed, kept)
    even = lax.axis_index("depth") % 2 == 0
    pieces = [own[0]]
    for own_piece, own_n, far_piece, far_n in zip(own[1:], evens[1:], far, evens):
        for own_side in (0, 1):
            moves = ((0, 0, own_n), (0, -1, far_n)) if own_side == 0 else ((0, -1, far_n), (0, 0, own_n))
            mixed = jnp.where(even == (own_side == 0), own_piece, far_piece)
            pieces.append(sent(mixed, sizes, *zip(*moves)))
    pieces.append(sent(far[-1], sizes, 0, -1, evens[-1]))
    return total_of(pieces, a.dtype)[None, None]


def solution(mesh):
    placed = (
        P("row", "col", "depth", None, None, None),
        P("row", "col", "depth", None, None),
        P("row", "col", "depth", None),
        P("row", "col", "depth", None, None, None),
        P("row", "col", "depth", None, None),
        P("row", "col", "depth", None),
        P("row", "col", None, None),
        P("row", "col", None),
    )
    sizes = tuple(mesh.shape[axis] for axis in AXES)
    return jax.shard_map(
        functools.partial(local, sizes),
        mesh=mesh,
        in_specs=placed,
        out_specs=P("row", "col", "depth", None, None),
        check_vma=False,
    )
```

time: 38 us -> 31 us (0.82)
  starting transfers between devices: 15.6 us -> 11 us
  local copies, waits for them, and re-layouts: 5.91 us -> 3.97 us
  Pallas kernels: 4.78 us -> 2.96 us
  other arithmetic: 1.53 us -> 3.24 us
  waiting for transfers between devices: 9.82 us -> 9.43 us
    ppermute x11 -> x8, starting transfers between devices: 15.6 us -> 11 us  [sent(): return lax.ppermute(value, AXES, pairs)]
    dynamic_slice x2 -> x0, local copies, waits for them, and re-layouts: 1.94 us -> none  [local(): part = lax.dynamic_slice_in_dim(source, start, half * rows, 0)]
    pallas_call x3, Pallas kernels: 4.78 us -> 2.96 us  [product(): pl.pallas_call(functools.partial(product_kernel, groups, fills), out_shap...]
    convert_element_type x0 -> x2, other arithmetic: none -> 1.07 us  [total_of(): return sum((one.astype(jnp.float32) for one in pieces)).astype(dtype)]
    select_n x1 -> x3, other arithmetic: 0.72 us -> 1.44 us  [the longest x2 1.37 us: live_columns(): jnp.where(jnp.arange(columns.shape[1], dtype=jnp.int32)[:, None] < counts...]
    ppermute x11 -> x8, waiting for transfers between devices: 9.82 us -> 9.43 us  [sent(): return lax.ppermute(value, AXES, pairs)]
  transfers between devices with their start and end apart: 11 -> 8, of which waited for: 5 -> 4; matrix products, arithmetic and copies ran while one was open for 5% -> 8% of each run, Pallas kernels for 13% -> 7%
where the time goes in v3:
time: 31 us; the launch traced here: 30.7 us
  starting transfers between devices  11 us (35%)
  waiting for transfers between devices  9.43 us (30%)
  local copies, waits for them, and re-layouts  3.97 us (13%)
  other arithmetic  3.24 us (10%)
  Pallas kernels  2.96 us (10%)
    ppermute x8, starting transfers between devices, sent(): return lax.ppermute(value, AXES, pairs)  11 us
    ppermute x8, waiting for transfers between devices, sent(): return lax.ppermute(value, AXES, pairs)  9.43 us
    unnamed x10, local copies, waits for them, and re-layouts  3.97 us
    pallas_call x3, Pallas kernels, product(): pl.pallas_call(functools.partial(product_kernel, groups, fills), out_shap...  2.96 us
    select_n x2, other arithmetic, live_columns(): jnp.where(jnp.arange(columns.shape[1], dtype=jnp.int32)[:, None] < counts...  1.37 us
    convert_element_type x2, other arithmetic, total_of(): return sum((one.astype(jnp.float32) for one in pieces)).astype(dtype)  1.07 us
    broadcast_in_dim x1, other arithmetic, local(): return total_of(pieces, a.dtype)[None, None]  0.73 us
  transfers between devices with their start and end apart: 8, of which 4 were waited for; matrix products, arithmetic and copies ran while one was open for 8% of the time, Pallas kernels for 7%

profile of v3, /device:TPU:0, one launch (start us, length us, event | category | flops | bytes accessed | tf_op | source)
XLA Modules:
  0.0 30.7 jit_solution(4474096394115022073)
XLA Ops:
  0.0 4.0 %collective-permute-start = (bf16[16,64,256]{2,1,0:T(8,128)(2,1)}, bf16[16,64,256]{2,1,0:T(8,128)(2,1)S(1)}, u32[]{:S(2)}, u32[]{:S(2)}) collective-permute-start(bf16[16,64,256]{2,1,0:T(8,128)(2,1)} %bitcast.21), channel_id=1, source_target_pairs={{0,20},{1,21},{2,22},{3,23},{4,24},{5,25},{6,26},{7,27},{8,28},{9,... | collective-permute-start | bytes 1572872 | tf_op jit(solution)/shard_map/ppermute | solution.py:112
  4.0 0.7 %bitcast_select_fusion.1.refs_2_ = s32[4,16]{1,0:T(4,128)S(1)} fusion(s32[1,1,1,16,4]{3,4,2,1,0:T(4,128)} %param.9, s32[16]{0:T(128)} %bitcast.25), kind=kLoop, calls=%fused_computation.9 | loop fusion | flops 128 | bytes 576 | tf_op jit(solution)/shard_map/jit(_where)/select_n | solution.py:116
  4.7 0.7 %bitcast_select_fusion.refs_3_ = s32[4,16]{1,0:T(4,128)S(1)} fusion(s32[1,1,16,4]{2,3,1,0:T(4,128)} %param.14, s32[16]{0:T(128)} %bitcast.26), kind=kLoop, calls=%fused_computation.8 | loop fusion | flops 128 | bytes 576 | tf_op jit(solution)/shard_map/jit(_where)/select_n | solution.py:116
  5.4 0.0 copy-start
  5.4 1.6 %copy-done = bf16[1,1,1,128,64,128]{5,4,3,2,1,0:T(8,128)(2,1)S(1)} copy-done((bf16[1,1,1,128,64,128]{5,4,3,2,1,0:T(8,128)(2,1)S(1)}, bf16[1,1,1,128,64,128]{5,4,3,2,1,0:T(8,128)(2,1)}, u32[]{:S(2)}) %copy-start) | copy-done | bytes 2097176
  6.9 0.0 copy-start.2
  7.0 1.0 %copy-done.2 = bf16[1,1,1,16,64,256]{5,4,3,2,1,0:T(8,128)(2,1)S(1)} copy-done((bf16[1,1,1,16,64,256]{5,4,3,2,1,0:T(8,128)(2,1)S(1)}, bf16[1,1,1,16,64,256]{5,4,3,2,1,0:T(8,128)(2,1)}, u32[]{:S(2)}) %copy-start.2) | copy-done | bytes 524312
  8.0 0.0 copy-start.3
  8.0 0.7 %copy-done.3 = s32[1,1,1,128,2]{3,4,2,1,0:T(2,128)S(1)} copy-done((s32[1,1,1,128,2]{3,4,2,1,0:T(2,128)S(1)}, s32[1,1,1,128,2]{3,4,2,1,0:T(2,128)}, u32[]{:S(2)}) %copy-start.3) | copy-done | bytes 1048
  8.7 0.0 copy-start.4
  8.7 0.7 %copy-done.4 = s32[1,1,1,128]{3,2,1,0:T(1,128)S(1)} copy-done((s32[1,1,1,128]{3,2,1,0:T(1,128)S(1)}, s32[1,1,1,128]{3,2,1,0:T(1,128)}, u32[]{:S(2)}) %copy-start.4) | copy-done | bytes 536
  9.3 0.0 copy-start.1
  9.3 1.4 %own_product.1 = (bf16[8,64,256]{2,1,0:T(8,128)(2,1)S(1)}, bf16[4,64,256]{2,1,0:T(8,128)(2,1)S(1)}, bf16[4,64,256]{2,1,0:T(8,128)(2,1)S(1)}, s32[272,128]{1,0:T(8,128)S(1)}) custom-call(bf16[16,64,256]{2,1,0:T(8,128)(2,1)S(1)} %bitcast.22, bf16[128,64,128]{2,1,0:T(8,128)(2,1)S(1)} %bitcast.18, s32[4,16]{1,0:T(4,128)S(1)} %bitcast_select_fusion.1.refs_2_, ...), custom_call_target="tpu_custom_call" | custom-call | flops 134217728 | tf_op jit(solution)/shard_map/own_product/pallas_call | solution.py:85
  10.7 0.1 collective-permute-start.1
  10.8 1.6 %collective-permute-start.2 = (s32[4,16]{1,0:T(4,128)S(1)}, s32[4,16]{1,0:T(4,128)S(1)}, u32[]{:S(2)}, u32[]{:S(2)}) collective-permute-start(s32[4,16]{1,0:T(4,128)S(1)} %bitcast_select_fusion.1.refs_2_), channel_id=1, source_target_pairs={{0,20},{1,21},{2,22},{3,23},{4,24},{5,25},{6,26},{7,27},{8,28},{9,... | collective-permute-start | bytes 776 | tf_op jit(solution)/shard_map/ppermute | solution.py:112
  12.4 1.6 %collective-permute-start.3 = (s32[4,16]{1,0:T(4,128)S(1)}, s32[4,16]{1,0:T(4,128)S(1)}, u32[]{:S(2)}, u32[]{:S(2)}) collective-permute-start(s32[4,16]{1,0:T(4,128)S(1)} %bitcast_select_fusion.refs_3_), channel_id=1, source_target_pairs={{0,4},{1,5},{2,6},{3,7},{4,8},{5,9},{6,10},{7,11},{8,12},{9,13},{1... | collective-permute-start | bytes 776 | tf_op jit(solution)/shard_map/ppermute | solution.py:112
  14.0 0.0 collective-permute-done.1
  14.0 1.0 %add_convert_fusion.3 = (bf16[4,64,256]{2,1,0:T(8,128)(2,1)S(1)}, bf16[4,64,256]{2,1,0:T(8,128)(2,1)S(1)}) fusion(bf16[4,64,256]{2,1,0:T(8,128)(2,1)S(1)} %get-tuple-element.18, bf16[8,64,256]{2,1,0:T(8,128)(2,1)} %collective-permute-done.1, bf16[4,64,256]{2,1,0:T(8,128)(2,1)S(1)} %get-tuple-element.16), kind=kLoop, calls=%fused_computation.3 | loop fusion | flops 524288 | bytes 786432 | tf_op jit(solution)/shard_map/convert_element_type | solution.py:98
  15.0 3.2 %collective-permute-done.refs_0_ = bf16[16,64,256]{2,1,0:T(8,128)(2,1)S(1)} collective-permute-done((bf16[16,64,256]{2,1,0:T(8,128)(2,1)}, bf16[16,64,256]{2,1,0:T(8,128)(2,1)S(1)}, u32[]{:S(2)}, u32[]{:S(2)}) %collective-permute-start) | collective-permute-done | bytes 524320 | tf_op jit(solution)/shard_map/ppermute | solution.py:112
  18.2 0.0 collective-permute-done.2.refs_2_
  18.2 0.0 collective-permute-done.3.refs_3_
  18.2 0.0 copy-done.1
  18.2 0.8 %far_passed.1 = bf16[8,64,256]{2,1,0:T(8,128)(2,1)S(1)} custom-call(bf16[16,64,256]{2,1,0:T(8,128)(2,1)S(1)} %collective-permute-done.refs_0_, bf16[128,64,128]{2,1,0:T(8,128)(2,1)S(1)} %bitcast.19, s32[4,16]{1,0:T(4,128)S(1)} %collective-permute-done.2.refs_2_, s32[4,16]{1,0:T(4,128)S(1)} %collective-permute-done.3.refs_3_, ...), custom_call_target="tpu_custom_call" | custom-call | flops 6710886400 | tf_op jit(solution)/shard_map/far_passed/pallas_call | solution.py:85
  19.0 0.1 collective-permute-start.4
  19.1 0.8 %far_kept.1 = (bf16[4,64,256]{2,1,0:T(8,128)(2,1)S(1)}, bf16[4,64,256]{2,1,0:T(8,128)(2,1)S(1)}) custom-call(bf16[16,64,256]{2,1,0:T(8,128)(2,1)S(1)} %collective-permute-done.refs_0_, bf16[128,64,128]{2,1,0:T(8,128)(2,1)S(1)} %bitcast.20, s32[4,16]{1,0:T(4,128)S(1)} %collective-permute-done.2.refs_2_, s32[4,16]{1,0:T(4,128)S(1)} %collective-permute-done.3.refs_3_, ...), custom_call_target="tpu_custom_call" | custom-call | flops 6710886400 | tf_op jit(solution)/shard_map/far_kept/pallas_call | solution.py:85
  19.8 0.7 %collective-permute-done.4 = bf16[8,64,256]{2,1,0:T(8,128)(2,1)S(1)} collective-permute-done((bf16[8,64,256]{2,1,0:T(8,128)(2,1)S(1)}, bf16[8,64,256]{2,1,0:T(8,128)(2,1)S(1)}, u32[]{:S(2)}, u32[]{:S(2)}) %collective-permute-start.4) | collective-permute-done | bytes 262176 | tf_op jit(solution)/shard_map/ppermute | solution.py:112
  20.6 2.7 %collective-permute-start.7 = (bf16[4,64,256]{2,1,0:T(8,128)(2,1)S(1)}, bf16[4,64,256]{2,1,0:T(8,128)(2,1)S(1)}, u32[]{:S(2)}, u32[]{:S(2)}) collective-permute-start(bf16[4,64,256]{2,1,0:T(8,128)(2,1)S(1)} %add_convert_fusion.1), channel_id=1, source_target_pairs={{0,14},{1,15},{2,12},{3,13},{4,2},{5,3},{6,0},{7,1},{8,6},{9,7},{1... | collective-permute-start | bytes 393224 | tf_op jit(solution)/shard_map/ppermute | solution.py:112
  23.4 0.1 broadcast_select_fusion.1
  23.4 0.5 %collective-permute-start.6 = (bf16[4,64,256]{2,1,0:T(8,128)(2,1)S(1)}, bf16[4,64,256]{2,1,0:T(8,128)(2,1)S(1)}, u32[]{:S(2)}, u32[]{:S(2)}) collective-permute-start(bf16[4,64,256]{2,1,0:T(8,128)(2,1)S(1)} %get-tuple-element.28), channel_id=1, source_target_pairs={{0,12},{1,3},{2,14},{3,1},{4,0},{5,7},{6,2},{7,5},{8,4},{9,11},{10... | collective-permute-start | bytes 393224 | tf_op jit(solution)/shard_map/ppermute | solution.py:112
  23.9 0.5 %collective-permute-start.5 = (bf16[4,64,256]{2,1,0:T(8,128)(2,1)S(1)}, bf16[4,64,256]{2,1,0:T(8,128)(2,1)S(1)}, u32[]{:S(2)}, u32[]{:S(2)}) collective-permute-start(bf16[4,64,256]{2,1,0:T(8,128)(2,1)S(1)} %get-tuple-element.27), channel_id=1, source_target_pairs={{0,2},{1,13},{2,0},{3,15},{4,6},{5,1},{6,4},{7,3},{8,10},{9,5},{10... | collective-permute-start | bytes 393224 | tf_op jit(solution)/shard_map/ppermute | solution.py:112
  24.5 2.8 %collective-permute-done.7 = bf16[4,64,256]{2,1,0:T(8,128)(2,1)S(1)} collective-permute-done((bf16[4,64,256]{2,1,0:T(8,128)(2,1)S(1)}, bf16[4,64,256]{2,1,0:T(8,128)(2,1)S(1)}, u32[]{:S(2)}, u32[]{:S(2)}) %collective-permute-start.7) | collective-permute-done | bytes 131104 | tf_op jit(solution)/shard_map/ppermute | solution.py:112
  27.2 2.7 %collective-permute-done.6 = bf16[4,64,256]{2,1,0:T(8,128)(2,1)S(1)} collective-permute-done((bf16[4,64,256]{2,1,0:T(8,128)(2,1)S(1)}, bf16[4,64,256]{2,1,0:T(8,128)(2,1)S(1)}, u32[]{:S(2)}, u32[]{:S(2)}) %collective-permute-start.6) | collective-permute-done | bytes 131104 | tf_op jit(solution)/shard_map/ppermute | solution.py:112
  29.9 0.0 collective-permute-done.5
  30.0 0.7 %fusion = bf16[1,1,4,64,256]{4,3,2,1,0:T(8,128)(2,1)} fusion(bf16[4,64,256]{2,1,0:T(8,128)(2,1)S(1)} %collective-permute-done.7, bf16[4,64,256]{2,1,0:T(8,128)(2,1)S(1)} %collective-permute-done.6, bf16[4,64,256]{2,1,0:T(8,128)(2,1)S(1)} %collective-permute-done.5, bf16[4,64,256]{2,1,0:T(8,128)(2,1)S(1)} %get-tuple-element.19), kind=kLoop, calls=%fused_computation.5 | loop fusion | flops 524288 | bytes 655360 | tf_op jit(solution)/shard_map/broadcast_in_dim | solution.py:152
  (1 shorter events, 0.0 us)
Async XLA Ops:
  0.0 18.2 %collective-permute-start = (bf16[16,64,256]{2,1,0:T(8,128)(2,1)}, bf16[16,64,256]{2,1,0:T(8,128)(2,1)S(1)}, u32[]{:S(2)}, u32[]{:S(2)}) collective-permute-start(bf16[16,64,256]{2,1,0:T(8,128)(2,1)} %bitcast.21), channel_id=1, source_target_pairs={{0,20},{1,21},{2,22},{3,23},{4,24},{5,25},{6,26},{7,27},{8,28},{9,... | collective-permute-start | bytes 1572872 | tf_op jit(solution)/shard_map/ppermute | solution.py:112
  5.4 1.6 %copy-start = (bf16[1,1,1,128,64,128]{5,4,3,2,1,0:T(8,128)(2,1)S(1)}, bf16[1,1,1,128,64,128]{5,4,3,2,1,0:T(8,128)(2,1)}, u32[]{:S(2)}) copy-start(bf16[1,1,1,128,64,128]{5,4,3,2,1,0:T(8,128)(2,1)} %param.11) | copy-start | bytes 6291460
  6.9 1.0 %copy-start.2 = (bf16[1,1,1,16,64,256]{5,4,3,2,1,0:T(8,128)(2,1)S(1)}, bf16[1,1,1,16,64,256]{5,4,3,2,1,0:T(8,128)(2,1)}, u32[]{:S(2)}) copy-start(bf16[1,1,1,16,64,256]{5,4,3,2,1,0:T(8,128)(2,1)} %param.8) | copy-start | bytes 1572868
  8.0 0.7 %copy-start.3 = (s32[1,1,1,128,2]{3,4,2,1,0:T(2,128)S(1)}, s32[1,1,1,128,2]{3,4,2,1,0:T(2,128)}, u32[]{:S(2)}) copy-start(s32[1,1,1,128,2]{3,4,2,1,0:T(2,128)} %param.12) | copy-start | bytes 3076
  8.7 0.7 %copy-start.4 = (s32[1,1,1,128]{3,2,1,0:T(1,128)S(1)}, s32[1,1,1,128]{3,2,1,0:T(1,128)}, u32[]{:S(2)}) copy-start(s32[1,1,1,128]{3,2,1,0:T(1,128)} %param.13) | copy-start | bytes 1540
  9.3 8.9 %copy-start.1 = (bf16[1,1,1,128,64,128]{5,4,3,2,1,0:T(8,128)(2,1)S(1)}, bf16[1,1,1,128,64,128]{5,4,3,2,1,0:T(8,128)(2,1)}, u32[]{:S(2)}) copy-start(bf16[1,1,1,128,64,128]{5,4,3,2,1,0:T(8,128)(2,1)} %param.11) | copy-start | bytes 6291460
  10.7 3.2 %collective-permute-start.1 = (bf16[8,64,256]{2,1,0:T(8,128)(2,1)S(1)}, bf16[8,64,256]{2,1,0:T(8,128)(2,1)}, u32[]{:S(2)}, u32[]{:S(2)}) collective-permute-start(bf16[8,64,256]{2,1,0:T(8,128)(2,1)S(1)} %get-tuple-element.17), channel_id=1, source_target_pairs={{0,1},{1,0},{2,3},{3,2},{4,5},{5,4},{6,7},{7,6},{8,9},{9,8},{10,11... | collective-permute-start | bytes 786440 | tf_op jit(solution)/shard_map/ppermute | solution.py:112
  10.8 7.4 %collective-permute-start.2 = (s32[4,16]{1,0:T(4,128)S(1)}, s32[4,16]{1,0:T(4,128)S(1)}, u32[]{:S(2)}, u32[]{:S(2)}) collective-permute-start(s32[4,16]{1,0:T(4,128)S(1)} %bitcast_select_fusion.1.refs_2_), channel_id=1, source_target_pairs={{0,20},{1,21},{2,22},{3,23},{4,24},{5,25},{6,26},{7,27},{8,28},{9,... | collective-permute-start | bytes 776 | tf_op jit(solution)/shard_map/ppermute | solution.py:112
  12.4 5.8 %collective-permute-start.3 = (s32[4,16]{1,0:T(4,128)S(1)}, s32[4,16]{1,0:T(4,128)S(1)}, u32[]{:S(2)}, u32[]{:S(2)}) collective-permute-start(s32[4,16]{1,0:T(4,128)S(1)} %bitcast_select_fusion.refs_3_), channel_id=1, source_target_pairs={{0,4},{1,5},{2,6},{3,7},{4,8},{5,9},{6,10},{7,11},{8,12},{9,13},{1... | collective-permute-start | bytes 776 | tf_op jit(solution)/shard_map/ppermute | solution.py:112
  19.0 1.6 %collective-permute-start.4 = (bf16[8,64,256]{2,1,0:T(8,128)(2,1)S(1)}, bf16[8,64,256]{2,1,0:T(8,128)(2,1)S(1)}, u32[]{:S(2)}, u32[]{:S(2)}) collective-permute-start(bf16[8,64,256]{2,1,0:T(8,128)(2,1)S(1)} %far_passed.1), channel_id=1, source_target_pairs={{0,1},{1,0},{2,3},{3,2},{4,5},{5,4},{6,7},{7,6},{8,9},{9,8},{10,11... | collective-permute-start | bytes 786440 | tf_op jit(solution)/shard_map/ppermute | solution.py:112
  20.6 6.6 %collective-permute-start.7 = (bf16[4,64,256]{2,1,0:T(8,128)(2,1)S(1)}, bf16[4,64,256]{2,1,0:T(8,128)(2,1)S(1)}, u32[]{:S(2)}, u32[]{:S(2)}) collective-permute-start(bf16[4,64,256]{2,1,0:T(8,128)(2,1)S(1)} %add_convert_fusion.1), channel_id=1, source_target_pairs={{0,14},{1,15},{2,12},{3,13},{4,2},{5,3},{6,0},{7,1},{8,6},{9,7},{1... | collective-permute-start | bytes 393224 | tf_op jit(solution)/shard_map/ppermute | solution.py:112
  23.4 6.5 %collective-permute-start.6 = (bf16[4,64,256]{2,1,0:T(8,128)(2,1)S(1)}, bf16[4,64,256]{2,1,0:T(8,128)(2,1)S(1)}, u32[]{:S(2)}, u32[]{:S(2)}) collective-permute-start(bf16[4,64,256]{2,1,0:T(8,128)(2,1)S(1)} %get-tuple-element.28), channel_id=1, source_target_pairs={{0,12},{1,3},{2,14},{3,1},{4,0},{5,7},{6,2},{7,5},{8,4},{9,11},{10... | collective-permute-start | bytes 393224 | tf_op jit(solution)/shard_map/ppermute | solution.py:112
  23.9 6.0 %collective-permute-start.5 = (bf16[4,64,256]{2,1,0:T(8,128)(2,1)S(1)}, bf16[4,64,256]{2,1,0:T(8,128)(2,1)S(1)}, u32[]{:S(2)}, u32[]{:S(2)}) collective-permute-start(bf16[4,64,256]{2,1,0:T(8,128)(2,1)S(1)} %get-tuple-element.27), channel_id=1, source_target_pairs={{0,2},{1,13},{2,0},{3,15},{4,6},{5,1},{6,4},{7,3},{8,10},{9,5},{10... | collective-permute-start | bytes 393224 | tf_op jit(solution)/shard_map/ppermute | solution.py:112

commit v4 on v3

--- a/solution.py
+++ b/solution.py
@@ -10,19 +10,18 @@
 ANY = pl.BlockSpec(memory_space=pl.ANY)
 HBM = pl.BlockSpec(memory_space=pltpu.HBM)
 VMEM = pl.BlockSpec(memory_space=pltpu.VMEM)
-DEAD_B, DEAD_C = -2, -1
+DEAD_B = -1
 OWN = 2
+SLICE = 10000
 FAR = 100
 AXES = ("row", "col", "depth")
 
 
-def fill_b_list(b_list, b_col, b_cnt, block):
-    slots, inner = b_col.shape
+def fill_b_list(b_list, live, block):
+    slots, inner = live.shape
     width = b_list.shape[1]
-    number = lax.broadcasted_iota(jnp.int32, (slots, inner), 0)
-    live = jnp.where(number < b_cnt[...], b_col[...], DEAD_B)
-    live = jnp.concatenate([live, jnp.full((8 - slots, inner), DEAD_B, jnp.int32)]).T
-    first, second = (jnp.broadcast_to(live[:, slot : slot + 1], (inner, width)) for slot in range(2))
+    columns = jnp.concatenate([live[...], jnp.full((8 - slots, inner), DEAD_B, jnp.int32)]).T
+    first, second = (jnp.broadcast_to(columns[:, slot : slot + 1], (inner, width)) for slot in range(2))
     left = lax.broadcasted_iota(jnp.int32, (inner, width), 1) < block
     half = b_list.shape[0] // 2
     b_list[:inner, :] = jnp.where(left, first, second)
@@ -50,14 +49,11 @@
             sel_ref[a * block : (a + 1) * block, p * width : (p + 1) * width] = rows * keep + swapped * swap
 
 
-def product_kernel(groups, fills, *refs):
-    a_ref, b_ref, a_list, c_list = refs[:4]
+def product_kernel(groups, count, fills, *refs):
+    a_ref, b_ref, a_list, c_list, b_list, *outs, lists, sel = refs
     if fills:
-        b_col, b_cnt = refs[4:6]
-        *outs, b_list, lists, sel = refs[6:]
-        fill_b_list(b_list, b_col, b_cnt, b_ref.shape[1])
-    else:
-        b_list, *outs, lists, sel = refs[4:]
+        live, b_list = b_list, outs.pop()
+        fill_b_list(b_list, live, b_ref.shape[1])
     a_slots, listed = a_list.shape
     lists[:a_slots, :listed] = a_list[...]
     lists[a_slots : a_slots + c_list.shape[0], :listed] = c_list[...]
@@ -65,33 +61,50 @@
     rows = sel.shape[0]
     for group, out in zip(groups, outs):
         for at, n in enumerate(group):
-            first = (me ^ n) * rows
+            slot = me ^ n
+            first, here = slot * rows, slot % count * rows
             for j in range(rows):
                 select_row(first + j, b_ref, lists, b_list, sel.at[j])
             for j in range(rows):
-                got = jnp.dot(a_ref[first + j], sel[j], preferred_element_type=jnp.float32)
+                got = jnp.dot(a_ref[here + j], sel[j], preferred_element_type=jnp.float32)
                 out[at * rows + j] = got.astype(out.dtype)
 
 
-def product(layers, groups, a, b, a_list, c_list, b_lists, name, limit, weight):
+def product(count, groups, a, b, a_list, c_list, b_list, name, weight):
     total, block, width = a.shape
     inner, _, b_width = b.shape
-    rows = total // layers
+    rows = total // count
     out_width = c_list.shape[0] * block
-    fills = len(b_lists) == 2
+    fills = b_list.shape[0] < inner
     outs = [jax.ShapeDtypeStruct((len(group) * rows, block, out_width), a.dtype) for group in groups]
     if fills:
         outs.append(jax.ShapeDtypeStruct((2 * (inner + 8), b_width), jnp.int32))
     return pl.pallas_call(
-        functools.partial(product_kernel, groups, fills),
+        functools.partial(product_kernel, groups, count, fills),
         out_shape=outs,
-        in_specs=[VMEM] * (4 + len(b_lists)),
+        in_specs=[VMEM] * 5,
         out_specs=[VMEM] * len(outs),
         scratch_shapes=[pltpu.VMEM((8, 128), jnp.int32), pltpu.VMEM((rows, width, out_width), a.dtype)],
-        compiler_params=pltpu.CompilerParams(vmem_limit_bytes=limit),
+        compiler_params=pltpu.CompilerParams(vmem_limit_bytes=8 << 20),
         cost_estimate=pl.CostEstimate(flops=weight * total * block * width * out_width, bytes_accessed=0, transcendentals=0),
         name=name,
-    )(a, b, a_list, c_list, *b_lists)
+    )(a, b, a_list, c_list, b_list)
+
+
+def slice_kernel(parts, a_ref, out):
+    out[...] = a_ref[pl.ds(lax.axis_index("depth") // (parts // 2) * out.shape[0], out.shape[0])]
+
+
+def near_half(a, parts):
+    return pl.pallas_call(
+        functools.partial(slice_kernel, parts),
+        out_shape=jax.ShapeDtypeStruct((a.shape[0] // 2, *a.shape[1:]), a.dtype),
+        in_specs=[VMEM],
+        out_specs=VMEM,
+        compiler_params=pltpu.CompilerParams(vmem_limit_bytes=8 << 20),
+        cost_estimate=pl.CostEstimate(flops=SLICE * a.size, bytes_accessed=0, transcendentals=0),
+        name="near_half",
+    )(a)
 
 
 def total_of(pieces, dtype):
@@ -122,34 +135,47 @@
     rows = a.shape[0] // layers
     evens, odds = tuple(range(0, layers, 2)), tuple(range(1, layers, 2))
 
-    far_a = sent(a, sizes, -1, 1, 0)
+    half = layers // 2
+    side = lax.axis_index("depth") // half
+    first = lax.dynamic_slice_in_dim(a, (1 - side) * (half * rows), half * rows, 0)
+    far_first = sent(first, sizes, -1, 1, 0)
+    first, a_counts, c_list = lax.optimization_barrier((first, a_counts, c_columns[0, 0].T))
     a_list = live_columns(a_columns[0, 0, 0], a_counts[0, 0, 0], b.shape[0])
-    c_list = live_columns(c_columns[0, 0], c_counts[0, 0], DEAD_C)
     far_a_list = sent(a_list, sizes, -1, 1, 0)
     far_c_list = sent(c_list, sizes, 0, 1, 0)
+    a_later, a_list = lax.optimization_barrier((a, a_list))
+    far_second = sent(near_half(a_later, layers), sizes, -1, 1, 0)
 
     def paired(passed, kept):
         met = sent(passed, sizes, 0, 0, 1)
         return [total_of((one, met[at * rows : (at + 1) * rows]), a.dtype) for at, one in enumerate(kept)]
 
-    singles = tuple((n,) for n in evens)
-    raw = (b_columns[0, 0, 0].T, b_counts[0, 0])
-    passed, *kept, b_list = product(layers, (odds,) + singles, a, b, a_list, c_list, raw, "own_product", 8 << 20, OWN)
+    def far_product(part, order, b_list):
+        order_odds, order_evens = tuple(n for n in order if n % 2), tuple((n,) for n in order if n % 2 == 0)
+        passed, *filled = product(half, (order_odds,), part, b, far_a_list, far_c_list, b_list, "far_passed", FAR)
+        b_list = filled[0] if filled else b_list
+        part, passed = lax.optimization_barrier((part, passed))
+        kept = product(half, order_evens, part, b, far_a_list, far_c_list, b_list, "far_kept", FAR)
+        return paired(passed, kept), b_list
+
+    b_list = live_columns(b_columns[0, 0, 0], b_counts[0, 0, 0], DEAD_B)
+    far, b_list = far_product(far_first, range(half, layers), b_list)
+    a_later, far = lax.optimization_barrier((a_later, far))
+    passed, *kept = product(layers, (odds,) + tuple((n,) for n in evens), a_later, b, a_list, c_list, b_list, "own_product", OWN)
+    far_second, passed = lax.optimization_barrier((far_second, passed))
     own = paired(passed, kept)
-    far_a, own = lax.optimization_barrier((far_a, own))
-    (passed,) = product(layers, (odds,), far_a, b, far_a_list, far_c_list, (b_list,), "far_passed", 8 << 20, FAR)
-    far_a, passed = lax.optimization_barrier((far_a, passed))
-    kept = product(layers, singles, far_a, b, far_a_list, far_c_list, (b_list,), "far_kept", 8 << 20, FAR)
-    far = paired(passed, kept)
+    far = far_product(far_second, range(half), b_list)[0] + far
     even = lax.axis_index("depth") % 2 == 0
-    pieces = [own[0]]
+    pieces = [own[0]] + [sent(one, sizes, 0, -1, n) for one, n in zip(far[len(evens) // 2 :], evens[len(evens) // 2 :])]
     for own_piece, own_n, far_piece, far_n in zip(own[1:], evens[1:], far, evens):
         for own_side in (0, 1):
             moves = ((0, 0, own_n), (0, -1, far_n)) if own_side == 0 else ((0, -1, far_n), (0, 0, own_n))
             mixed = jnp.where(even == (own_side == 0), own_piece, far_piece)
             pieces.append(sent(mixed, sizes, *zip(*moves)))
-    pieces.append(sent(far[-1], sizes, 0, -1, evens[-1]))
-    return total_of(pieces, a.dtype)[None, None]
+    counts = lax.dynamic_slice_in_dim(c_counts[0, 0], lax.axis_index("depth") * rows, rows, 0)
+    slot = jnp.arange(c_list.shape[0] * b.shape[1], dtype=jnp.int32) // b.shape[1]
+    live = slot[None, None, :] < counts[:, None, None]
+    return jnp.where(live, total_of(pieces, jnp.float32), 0).astype(a.dtype)[None, None]
 
 
 def solution(mesh):

time: 31 us -> 29.8 us (0.961)
  starting transfers between devices: 11 us -> 14.5 us
  local copies, waits for them, and re-layouts: 3.97 us -> 2.12 us
  waiting for transfers between devices: 9.43 us -> 7.77 us
  other arithmetic: 3.24 us -> 1.64 us
  Pallas kernels: 2.96 us -> 3.48 us
    ppermute x8 -> x10, starting transfers between devices: 11 us -> 14.5 us  [sent(): return lax.ppermute(value, AXES, pairs)]
    unnamed x10 -> x14, local copies, waits for them, and re-layouts: 3.97 us -> 1.07 us
    ppermute x8 -> x10, waiting for transfers between devices: 9.43 us -> 7.77 us  [sent(): return lax.ppermute(value, AXES, pairs)]
    convert_element_type x2 -> x1, other arithmetic: 1.07 us -> 0.03 us  [total_of(): return sum((one.astype(jnp.float32) for one in pieces)).astype(dtype)]
    dynamic_slice x0 -> x1, local copies, waits for them, and re-layouts: none -> 0.98 us  [local(): lax.dynamic_slice_in_dim(a, (1 - side) * (half * rows), half * rows, 0)]
    select_n x2, other arithmetic: 1.37 us -> 0.69 us  [live_columns(): jnp.where(jnp.arange(columns.shape[1], dtype=jnp.int32)[:, None] < counts...]
    pallas_call x3 -> x6, Pallas kernels: 2.96 us -> 3.48 us  [the longest x5 3.47 us: product(): pl.pallas_call(functools.partial(product_kernel, groups, count, fills), o...]
  transfers between devices with their start and end apart: 8 -> 10, of which waited for: 4 -> 6; matrix products, arithmetic and copies ran while one was open for 8% -> 3% of each run, Pallas kernels for 7% -> 12%
where the time goes in v4:
time: 29.8 us; the launch traced here: 29.6 us
  starting transfers between devices  14.5 us (49%)
  waiting for transfers between devices  7.77 us (26%)
  Pallas kernels  3.48 us (12%)
  local copies, waits for them, and re-layouts  2.12 us (7%)
  other arithmetic  1.64 us (6%)
    ppermute x10, starting transfers between devices, sent(): return lax.ppermute(value, AXES, pairs)  14.5 us
    ppermute x10, waiting for transfers between devices, sent(): return lax.ppermute(value, AXES, pairs)  7.77 us
    pallas_call x5, Pallas kernels, product(): pl.pallas_call(functools.partial(product_kernel, groups, count, fills), o...  3.47 us
    unnamed x14, local copies, waits for them, and re-layouts  1.07 us
    dynamic_slice x1, local copies, waits for them, and re-layouts, local(): lax.dynamic_slice_in_dim(a, (1 - side) * (half * rows), half * rows, 0)  0.98 us
    broadcast_in_dim x1, other arithmetic, local(): jnp.where(live, total_of(pieces, jnp.float32), 0).astype(a.dtype)  0.76 us
    select_n x2, other arithmetic, live_columns(): jnp.where(jnp.arange(columns.shape[1], dtype=jnp.int32)[:, None] < counts...  0.69 us
  transfers between devices with their start and end apart: 10, of which 6 were waited for; matrix products, arithmetic and copies ran while one was open for 3% of the time, Pallas kernels for 12%

profile of v4, /device:TPU:0, one launch (start us, length us, event | category | flops | bytes accessed | tf_op | source)
XLA Modules:
  0.0 29.6 jit_solution(16432979396899715000)
XLA Ops:
  0.0 0.0 copy-start
  0.0 1.0 %dynamic-slice_bitcast_fusion = bf16[8,64,256]{2,1,0:T(8,128)(2,1)S(1)} fusion(bf16[1,1,1,16,64,256]{5,4,3,2,1,0:T(8,128)(2,1)} %param.8, s32[]{:T(128)S(6)} %select_n.55), kind=kLoop, calls=%fused_computation.5 | loop fusion | bytes 524292 | tf_op jit(solution)/shard_map/dynamic_slice | solution.py:140
  1.0 4.0 %collective-permute-start = (bf16[8,64,256]{2,1,0:T(8,128)(2,1)S(1)}, bf16[8,64,256]{2,1,0:T(8,128)(2,1)S(1)}, u32[]{:S(2)}, u32[]{:S(2)}) collective-permute-start(bf16[8,64,256]{2,1,0:T(8,128)(2,1)S(1)} %dynamic-slice_bitcast_fusion), channel_id=1, source_target_pairs={{0,20},{1,21},{2,22},{3,23},{4,24},{5,25},{6,26},{7,27},{8,28},{9,... | collective-permute-start | bytes 786440 | tf_op jit(solution)/shard_map/ppermute | solution.py:125
  5.0 0.7 %bitcast_select_fusion.refs_2_ = s32[4,16]{1,0:T(4,128)S(1)} fusion(s32[1,1,1,16,4]{3,4,2,1,0:T(4,128)} %param.9, s32[16]{0:T(128)} %bitcast.30), kind=kLoop, calls=%fused_computation.9 | loop fusion | flops 128 | bytes 576 | tf_op jit(solution)/shard_map/jit(_where)/select_n | solution.py:129
  5.7 1.5 %collective-permute-start.1 = (s32[4,16]{1,0:T(4,128)S(1)}, s32[4,16]{1,0:T(4,128)S(1)}, u32[]{:S(2)}, u32[]{:S(2)}) collective-permute-start(s32[4,16]{1,0:T(4,128)S(1)} %bitcast_select_fusion.refs_2_), channel_id=1, source_target_pairs={{0,20},{1,21},{2,22},{3,23},{4,24},{5,25},{6,26},{7,27},{8,28},{9,... | collective-permute-start | bytes 776 | tf_op jit(solution)/shard_map/ppermute | solution.py:125
  7.2 1.6 %collective-permute-start.2 = (s32[4,16]{1,0:T(4,128)}, s32[4,16]{1,0:T(4,128)S(1)}, u32[]{:S(2)}, u32[]{:S(2)}) collective-permute-start(s32[4,16]{1,0:T(4,128)} %bitcast.28), channel_id=1, source_target_pairs={{0,4},{1,5},{2,6},{3,7},{4,8},{5,9},{6,10},{7,11},{8,12},{9,13},{1... | collective-permute-start | bytes 776 | tf_op jit(solution)/shard_map/ppermute | solution.py:125
  8.8 0.0 copy-start.2
  8.8 1.0 %copy-done.2 = bf16[1,1,1,16,64,256]{5,4,3,2,1,0:T(8,128)(2,1)S(1)} copy-done((bf16[1,1,1,16,64,256]{5,4,3,2,1,0:T(8,128)(2,1)S(1)}, bf16[1,1,1,16,64,256]{5,4,3,2,1,0:T(8,128)(2,1)}, u32[]{:S(2)}) %copy-start.2) | copy-done | bytes 524312
  9.8 0.0 copy-start.5
  9.8 0.0 copy-start.6
  9.9 0.0 copy-start.1
  9.9 1.2 %collective-permute-start.4 = (bf16[8,64,256]{2,1,0:T(8,128)(2,1)S(1)}, bf16[8,64,256]{2,1,0:T(8,128)(2,1)S(1)}, u32[]{:S(2)}, u32[]{:S(2)}) collective-permute-start(bf16[8,64,256]{2,1,0:T(8,128)(2,1)S(1)} %near_half.1), channel_id=1, source_target_pairs={{0,20},{1,21},{2,22},{3,23},{4,24},{5,25},{6,26},{7,27},{8,28},{9,... | collective-permute-start | bytes 786440 | tf_op jit(solution)/shard_map/ppermute | solution.py:125
  11.1 0.0 copy-done
  11.1 0.1 dynamic-slice_bitcast_fusion.1
  11.2 0.0 copy-done.5
  11.2 0.0 copy-done.6
  11.2 2.2 %collective-permute-done.1.refs_2_ = s32[4,16]{1,0:T(4,128)S(1)} collective-permute-done((s32[4,16]{1,0:T(4,128)S(1)}, s32[4,16]{1,0:T(4,128)S(1)}, u32[]{:S(2)}, u32[]{:S(2)}) %collective-permute-start.1) | collective-permute-done | bytes 288 | tf_op jit(solution)/shard_map/ppermute | solution.py:125
  13.4 0.0 collective-permute-done.2.refs_3_
  13.4 0.0 collective-permute-done.refs_0_
  13.4 0.0 copy-done.1
  13.4 0.6 %far_passed.2 = (bf16[4,64,256]{2,1,0:T(8,128)(2,1)S(1)}, s32[272,128]{1,0:T(8,128)S(1)}) custom-call(bf16[8,64,256]{2,1,0:T(8,128)(2,1)S(1)} %collective-permute-done.refs_0_, bf16[128,64,128]{2,1,0:T(8,128)(2,1)S(1)} %bitcast.21, s32[4,16]{1,0:T(4,128)S(1)} %collective-permute-done.1.refs_2_, s32[4,16]{1,0:T(4,128)S(1)} %collective-permute-done.2.refs_3_, ...), custom_call_target="tpu_custom_call" | custom-call | flops 3355443200 | tf_op jit(solution)/shard_map/far_passed/pallas_call | solution.py:82
  14.0 0.1 collective-permute-start.3
  14.1 0.0 copy-start.3
  14.1 0.0 copy-start.4
  14.1 0.5 %far_kept.2 = bf16[4,64,256]{2,1,0:T(8,128)(2,1)S(1)} custom-call(bf16[8,64,256]{2,1,0:T(8,128)(2,1)S(1)} %collective-permute-done.refs_0_, bf16[128,64,128]{2,1,0:T(8,128)(2,1)S(1)} %bitcast.22, s32[4,16]{1,0:T(4,128)S(1)} %collective-permute-done.1.refs_2_, s32[4,16]{1,0:T(4,128)S(1)} %collective-permute-done.2.refs_3_, ...), custom_call_target="tpu_custom_call" | custom-call | flops 3355443200 | tf_op jit(solution)/shard_map/far_kept/pallas_call | solution.py:82
  14.7 0.8 %collective-permute-done.3 = bf16[4,64,256]{2,1,0:T(8,128)(2,1)S(1)} collective-permute-done((bf16[4,64,256]{2,1,0:T(8,128)(2,1)S(1)}, bf16[4,64,256]{2,1,0:T(8,128)(2,1)S(1)}, u32[]{:S(2)}, u32[]{:S(2)}) %collective-permute-start.3) | collective-permute-done | bytes 131104 | tf_op jit(solution)/shard_map/ppermute | solution.py:125
  15.5 3.1 %collective-permute-start.6 = (bf16[4,64,256]{2,1,0:T(8,128)(2,1)S(1)}, bf16[4,64,256]{2,1,0:T(8,128)(2,1)S(1)}, u32[]{:S(2)}, u32[]{:S(2)}) collective-permute-start(bf16[4,64,256]{2,1,0:T(8,128)(2,1)S(1)} %add_convert_fusion.3), channel_id=1, source_target_pairs={{0,14},{1,15},{2,12},{3,13},{4,2},{5,3},{6,0},{7,1},{8,6},{9,7},{1... | collective-permute-start | bytes 393224 | tf_op jit(solution)/shard_map/ppermute | solution.py:125
  18.6 0.0 copy-done.3
  18.6 0.0 copy-done.4
  18.6 1.3 %own_product.1 = (bf16[8,64,256]{2,1,0:T(8,128)(2,1)S(1)}, bf16[4,64,256]{2,1,0:T(8,128)(2,1)S(1)}, bf16[4,64,256]{2,1,0:T(8,128)(2,1)S(1)}) custom-call(bf16[16,64,256]{2,1,0:T(8,128)(2,1)S(1)} %bitcast.27, bf16[128,64,128]{2,1,0:T(8,128)(2,1)S(1)} %bitcast.23, s32[4,16]{1,0:T(4,128)S(1)} %bitcast_select_fusion.refs_2_, s32[4,16]{1,0:T(4,128)S(1)} %bitcast.29, ...), custom_call_target="tpu_custom_call" | custom-call | flops 134217728 | tf_op jit(solution)/shard_map/own_product/pallas_call | solution.py:82
  19.9 0.0 collective-permute-done.4.refs_0_
  19.9 0.5 %far_passed.3 = bf16[4,64,256]{2,1,0:T(8,128)(2,1)S(1)} custom-call(bf16[8,64,256]{2,1,0:T(8,128)(2,1)S(1)} %collective-permute-done.4.refs_0_, bf16[128,64,128]{2,1,0:T(8,128)(2,1)S(1)} %bitcast.24, s32[4,16]{1,0:T(4,128)S(1)} %collective-permute-done.1.refs_2_, s32[4,16]{1,0:T(4,128)S(1)} %collective-permute-done.2.refs_3_, ...), custom_call_target="tpu_custom_call" | custom-call | flops 3355443200 | tf_op jit(solution)/shard_map/far_passed/pallas_call | solution.py:82
  20.4 0.1 collective-permute-start.7
  20.5 0.5 %collective-permute-start.5 = (bf16[8,64,256]{2,1,0:T(8,128)(2,1)S(1)}, bf16[8,64,256]{2,1,0:T(8,128)(2,1)S(1)}, u32[]{:S(2)}, u32[]{:S(2)}) collective-permute-start(bf16[8,64,256]{2,1,0:T(8,128)(2,1)S(1)} %get-tuple-element.33), channel_id=1, source_target_pairs={{0,1},{1,0},{2,3},{3,2},{4,5},{5,4},{6,7},{7,6},{8,9},{9,8},{10,11... | collective-permute-start | bytes 786440 | tf_op jit(solution)/shard_map/ppermute | solution.py:125
  21.0 0.5 %far_kept.3 = bf16[4,64,256]{2,1,0:T(8,128)(2,1)S(1)} custom-call(bf16[8,64,256]{2,1,0:T(8,128)(2,1)S(1)} %collective-permute-done.4.refs_0_, bf16[128,64,128]{2,1,0:T(8,128)(2,1)S(1)} %bitcast.25, s32[4,16]{1,0:T(4,128)S(1)} %collective-permute-done.1.refs_2_, s32[4,16]{1,0:T(4,128)S(1)} %collective-permute-done.2.refs_3_, ...), custom_call_target="tpu_custom_call" | custom-call | flops 3355443200 | tf_op jit(solution)/shard_map/far_kept/pallas_call | solution.py:82
  21.6 0.3 %collective-permute-done.7 = bf16[4,64,256]{2,1,0:T(8,128)(2,1)S(1)} collective-permute-done((bf16[4,64,256]{2,1,0:T(8,128)(2,1)S(1)}, bf16[4,64,256]{2,1,0:T(8,128)(2,1)S(1)}, u32[]{:S(2)}, u32[]{:S(2)}) %collective-permute-start.7) | collective-permute-done | bytes 131104 | tf_op jit(solution)/shard_map/ppermute | solution.py:125
  21.9 0.4 %collective-permute-done.5 = bf16[8,64,256]{2,1,0:T(8,128)(2,1)S(1)} collective-permute-done((bf16[8,64,256]{2,1,0:T(8,128)(2,1)S(1)}, bf16[8,64,256]{2,1,0:T(8,128)(2,1)S(1)}, u32[]{:S(2)}, u32[]{:S(2)}) %collective-permute-start.5) | collective-permute-done | bytes 262176 | tf_op jit(solution)/shard_map/ppermute | solution.py:125
  22.2 0.1 broadcast_select_fusion.1
  22.3 1.6 %collective-permute-start.8 = (bf16[4,64,256]{2,1,0:T(8,128)(2,1)S(1)}, bf16[4,64,256]{2,1,0:T(8,128)(2,1)S(1)}, u32[]{:S(2)}, u32[]{:S(2)}) collective-permute-start(bf16[4,64,256]{2,1,0:T(8,128)(2,1)S(1)} %get-tuple-element.39), channel_id=1, source_target_pairs={{0,2},{1,13},{2,0},{3,15},{4,6},{5,1},{6,4},{7,3},{8,10},{9,5},{10... | collective-permute-start | bytes 393224 | tf_op jit(solution)/shard_map/ppermute | solution.py:125
  23.9 0.8 %collective-permute-start.9 = (bf16[4,64,256]{2,1,0:T(8,128)(2,1)S(1)}, bf16[4,64,256]{2,1,0:T(8,128)(2,1)S(1)}, u32[]{:S(2)}, u32[]{:S(2)}) collective-permute-start(bf16[4,64,256]{2,1,0:T(8,128)(2,1)S(1)} %get-tuple-element.40), channel_id=1, source_target_pairs={{0,12},{1,3},{2,14},{3,1},{4,0},{5,7},{6,2},{7,5},{8,4},{9,11},{10... | collective-permute-start | bytes 393224 | tf_op jit(solution)/shard_map/ppermute | solution.py:125
  24.7 0.1 broadcast_compare_fusion
  24.8 0.0 collective-permute-done.6
  24.8 3.9 %collective-permute-done.8 = bf16[4,64,256]{2,1,0:T(8,128)(2,1)S(1)} collective-permute-done((bf16[4,64,256]{2,1,0:T(8,128)(2,1)S(1)}, bf16[4,64,256]{2,1,0:T(8,128)(2,1)S(1)}, u32[]{:S(2)}, u32[]{:S(2)}) %collective-permute-start.8) | collective-permute-done | bytes 131104 | tf_op jit(solution)/shard_map/ppermute | solution.py:125
  28.7 0.2 collective-permute-done.9
  28.9 0.8 %fusion = bf16[1,1,4,64,256]{4,3,2,1,0:T(8,128)(2,1)} fusion(bf16[4,64,256]{2,1,0:T(8,128)(2,1)S(1)} %collective-permute-done.9, bf16[4,64,256]{2,1,0:T(8,128)(2,1)S(1)} %collective-permute-done.8, bf16[4,64,256]{2,1,0:T(8,128)(2,1)S(1)} %collective-permute-done.6, bf16[4,64,256]{2,1,0:T(8,128)(2,1)S(1)} %get-tuple-element.31, ...), kind=kLoop, calls=%fused_computation.6 | loop fusion | flops 851968 | bytes 787456 | tf_op jit(solution)/shard_map/broadcast_in_dim | solution.py:178
  (4 shorter events, 0.1 us)
Async XLA Ops:
  0.0 11.1 %copy-start = (s32[1,1,16]{2,1,0:T(1,128)S(1)}, s32[1,1,16]{2,1,0:T(1,128)}, u32[]{:S(2)}) copy-start(s32[1,1,16]{2,1,0:T(1,128)} %param.15) | copy-start | bytes 196
  1.0 12.4 %collective-permute-start = (bf16[8,64,256]{2,1,0:T(8,128)(2,1)S(1)}, bf16[8,64,256]{2,1,0:T(8,128)(2,1)S(1)}, u32[]{:S(2)}, u32[]{:S(2)}) collective-permute-start(bf16[8,64,256]{2,1,0:T(8,128)(2,1)S(1)} %dynamic-slice_bitcast_fusion), channel_id=1, source_target_pairs={{0,20},{1,21},{2,22},{3,23},{4,24},{5,25},{6,26},{7,27},{8,28},{9,... | collective-permute-start | bytes 786440 | tf_op jit(solution)/shard_map/ppermute | solution.py:125
  5.7 7.7 %collective-permute-start.1 = (s32[4,16]{1,0:T(4,128)S(1)}, s32[4,16]{1,0:T(4,128)S(1)}, u32[]{:S(2)}, u32[]{:S(2)}) collective-permute-start(s32[4,16]{1,0:T(4,128)S(1)} %bitcast_select_fusion.refs_2_), channel_id=1, source_target_pairs={{0,20},{1,21},{2,22},{3,23},{4,24},{5,25},{6,26},{7,27},{8,28},{9,... | collective-permute-start | bytes 776 | tf_op jit(solution)/shard_map/ppermute | solution.py:125
  7.2 6.2 %collective-permute-start.2 = (s32[4,16]{1,0:T(4,128)}, s32[4,16]{1,0:T(4,128)S(1)}, u32[]{:S(2)}, u32[]{:S(2)}) collective-permute-start(s32[4,16]{1,0:T(4,128)} %bitcast.28), channel_id=1, source_target_pairs={{0,4},{1,5},{2,6},{3,7},{4,8},{5,9},{6,10},{7,11},{8,12},{9,13},{1... | collective-permute-start | bytes 776 | tf_op jit(solution)/shard_map/ppermute | solution.py:125
  8.8 1.0 %copy-start.2 = (bf16[1,1,1,16,64,256]{5,4,3,2,1,0:T(8,128)(2,1)S(1)}, bf16[1,1,1,16,64,256]{5,4,3,2,1,0:T(8,128)(2,1)}, u32[]{:S(2)}) copy-start(bf16[1,1,1,16,64,256]{5,4,3,2,1,0:T(8,128)(2,1)} %param.8) | copy-start | bytes 1572868
  9.8 1.3 %copy-start.5 = (s32[1,1,1,128,2]{3,4,2,1,0:T(2,128)S(1)}, s32[1,1,1,128,2]{3,4,2,1,0:T(2,128)}, u32[]{:S(2)}) copy-start(s32[1,1,1,128,2]{3,4,2,1,0:T(2,128)} %param.12) | copy-start | bytes 3076
  9.8 1.3 %copy-start.6 = (s32[1,1,1,128]{3,2,1,0:T(1,128)S(1)}, s32[1,1,1,128]{3,2,1,0:T(1,128)}, u32[]{:S(2)}) copy-start(s32[1,1,1,128]{3,2,1,0:T(1,128)} %param.13) | copy-start | bytes 1540
  9.9 3.6 %copy-start.1 = (bf16[1,1,1,128,64,128]{5,4,3,2,1,0:T(8,128)(2,1)S(1)}, bf16[1,1,1,128,64,128]{5,4,3,2,1,0:T(8,128)(2,1)}, u32[]{:S(2)}) copy-start(bf16[1,1,1,128,64,128]{5,4,3,2,1,0:T(8,128)(2,1)} %param.11) | copy-start | bytes 6291460
  9.9 10.0 %collective-permute-start.4 = (bf16[8,64,256]{2,1,0:T(8,128)(2,1)S(1)}, bf16[8,64,256]{2,1,0:T(8,128)(2,1)S(1)}, u32[]{:S(2)}, u32[]{:S(2)}) collective-permute-start(bf16[8,64,256]{2,1,0:T(8,128)(2,1)S(1)} %near_half.1), channel_id=1, source_target_pairs={{0,20},{1,21},{2,22},{3,23},{4,24},{5,25},{6,26},{7,27},{8,28},{9,... | collective-permute-start | bytes 786440 | tf_op jit(solution)/shard_map/ppermute | solution.py:125
  14.0 1.4 %collective-permute-start.3 = (bf16[4,64,256]{2,1,0:T(8,128)(2,1)S(1)}, bf16[4,64,256]{2,1,0:T(8,128)(2,1)S(1)}, u32[]{:S(2)}, u32[]{:S(2)}) collective-permute-start(bf16[4,64,256]{2,1,0:T(8,128)(2,1)S(1)} %get-tuple-element.28), channel_id=1, source_target_pairs={{0,1},{1,0},{2,3},{3,2},{4,5},{5,4},{6,7},{7,6},{8,9},{9,8},{10,11... | collective-permute-start | bytes 393224 | tf_op jit(solution)/shard_map/ppermute | solution.py:125
  14.1 4.5 %copy-start.3 = (bf16[1,1,1,16,64,256]{5,4,3,2,1,0:T(8,128)(2,1)S(1)}, bf16[1,1,1,16,64,256]{5,4,3,2,1,0:T(8,128)(2,1)}, u32[]{:S(2)}) copy-start(bf16[1,1,1,16,64,256]{5,4,3,2,1,0:T(8,128)(2,1)} %param.8) | copy-start | bytes 1572868
  14.1 4.5 %copy-start.4 = (s32[1,1,16,4]{2,3,1,0:T(4,128)S(1)}, s32[1,1,16,4]{2,3,1,0:T(4,128)}, u32[]{:S(2)}) copy-start(s32[1,1,16,4]{2,3,1,0:T(4,128)} %param.14) | copy-start | bytes 772
  15.5 9.3 %collective-permute-start.6 = (bf16[4,64,256]{2,1,0:T(8,128)(2,1)S(1)}, bf16[4,64,256]{2,1,0:T(8,128)(2,1)S(1)}, u32[]{:S(2)}, u32[]{:S(2)}) collective-permute-start(bf16[4,64,256]{2,1,0:T(8,128)(2,1)S(1)} %add_convert_fusion.3), channel_id=1, source_target_pairs={{0,14},{1,15},{2,12},{3,13},{4,2},{5,3},{6,0},{7,1},{8,6},{9,7},{1... | collective-permute-start | bytes 393224 | tf_op jit(solution)/shard_map/ppermute | solution.py:125
  20.4 1.4 %collective-permute-start.7 = (bf16[4,64,256]{2,1,0:T(8,128)(2,1)S(1)}, bf16[4,64,256]{2,1,0:T(8,128)(2,1)S(1)}, u32[]{:S(2)}, u32[]{:S(2)}) collective-permute-start(bf16[4,64,256]{2,1,0:T(8,128)(2,1)S(1)} %far_passed.3), channel_id=1, source_target_pairs={{0,1},{1,0},{2,3},{3,2},{4,5},{5,4},{6,7},{7,6},{8,9},{9,8},{10,11... | collective-permute-start | bytes 393224 | tf_op jit(solution)/shard_map/ppermute | solution.py:125
  20.5 1.7 %collective-permute-start.5 = (bf16[8,64,256]{2,1,0:T(8,128)(2,1)S(1)}, bf16[8,64,256]{2,1,0:T(8,128)(2,1)S(1)}, u32[]{:S(2)}, u32[]{:S(2)}) collective-permute-start(bf16[8,64,256]{2,1,0:T(8,128)(2,1)S(1)} %get-tuple-element.33), channel_id=1, source_target_pairs={{0,1},{1,0},{2,3},{3,2},{4,5},{5,4},{6,7},{7,6},{8,9},{9,8},{10,11... | collective-permute-start | bytes 786440 | tf_op jit(solution)/shard_map/ppermute | solution.py:125
  22.3 6.3 %collective-permute-start.8 = (bf16[4,64,256]{2,1,0:T(8,128)(2,1)S(1)}, bf16[4,64,256]{2,1,0:T(8,128)(2,1)S(1)}, u32[]{:S(2)}, u32[]{:S(2)}) collective-permute-start(bf16[4,64,256]{2,1,0:T(8,128)(2,1)S(1)} %get-tuple-element.39), channel_id=1, source_target_pairs={{0,2},{1,13},{2,0},{3,15},{4,6},{5,1},{6,4},{7,3},{8,10},{9,5},{10... | collective-permute-start | bytes 393224 | tf_op jit(solution)/shard_map/ppermute | solution.py:125
  23.9 5.0 %collective-permute-start.9 = (bf16[4,64,256]{2,1,0:T(8,128)(2,1)S(1)}, bf16[4,64,256]{2,1,0:T(8,128)(2,1)S(1)}, u32[]{:S(2)}, u32[]{:S(2)}) collective-permute-start(bf16[4,64,256]{2,1,0:T(8,128)(2,1)S(1)} %get-tuple-element.40), channel_id=1, source_target_pairs={{0,12},{1,3},{2,14},{3,1},{4,0},{5,7},{6,2},{7,5},{8,4},{9,11},{10... | collective-permute-start | bytes 393224 | tf_op jit(solution)/shard_map/ppermute | solution.py:125

commit v5 on v4

--- a/solution.py
+++ b/solution.py
@@ -12,7 +12,9 @@
 VMEM = pl.BlockSpec(memory_space=pltpu.VMEM)
 DEAD_B = -1
 OWN = 2
-SLICE = 10000
+GATE = 5 << 30
+TURN = 5 << 30
+LIMIT = 8 << 20
 FAR = 100
 AXES = ("row", "col", "depth")
 
@@ -85,26 +87,46 @@
         in_specs=[VMEM] * 5,
         out_specs=[VMEM] * len(outs),
         scratch_shapes=[pltpu.VMEM((8, 128), jnp.int32), pltpu.VMEM((rows, width, out_width), a.dtype)],
-        compiler_params=pltpu.CompilerParams(vmem_limit_bytes=8 << 20),
+        compiler_params=pltpu.CompilerParams(vmem_limit_bytes=LIMIT),
         cost_estimate=pl.CostEstimate(flops=weight * total * block * width * out_width, bytes_accessed=0, transcendentals=0),
         name=name,
     )(a, b, a_list, c_list, b_list)
 
 
-def slice_kernel(parts, a_ref, out):
-    out[...] = a_ref[pl.ds(lax.axis_index("depth") // (parts // 2) * out.shape[0], out.shape[0])]
-
-
-def near_half(a, parts):
+def halves_kernel(parts, a_ref, far, near):
+    place = lax.axis_index("depth") // (parts // 2)
+    rows = near.shape[0]
+    far[...] = a_ref[pl.ds((1 - place) * rows, rows)]
+    near[...] = a_ref[pl.ds(place * rows, rows)]
+
+
+def halves_of(a, parts):
+    half = jax.ShapeDtypeStruct((a.shape[0] // 2, *a.shape[1:]), a.dtype)
     return pl.pallas_call(
-        functools.partial(slice_kernel, parts),
-        out_shape=jax.ShapeDtypeStruct((a.shape[0] // 2, *a.shape[1:]), a.dtype),
+        functools.partial(halves_kernel, parts),
+        out_shape=[half, half],
         in_specs=[VMEM],
+        out_specs=[VMEM, VMEM],
+        compiler_params=pltpu.CompilerParams(vmem_limit_bytes=LIMIT),
+        cost_estimate=pl.CostEstimate(flops=0, bytes_accessed=0, transcendentals=0),
+        name="halves_of_rows",
+    )(a)
+
+
+def after_kernel(value, earlier, out):
+    out[...] = value[...]
+
+
+def after(value, earlier, weight):
+    return pl.pallas_call(
+        after_kernel,
+        out_shape=jax.ShapeDtypeStruct(value.shape, value.dtype),
+        in_specs=[VMEM, VMEM],
         out_specs=VMEM,
-        compiler_params=pltpu.CompilerParams(vmem_limit_bytes=8 << 20),
-        cost_estimate=pl.CostEstimate(flops=SLICE * a.size, bytes_accessed=0, transcendentals=0),
-        name="near_half",
-    )(a)
+        compiler_params=pltpu.CompilerParams(vmem_limit_bytes=LIMIT),
+        cost_estimate=pl.CostEstimate(flops=weight, bytes_accessed=0, transcendentals=0),
+        name="after_lists",
+    )(value, earlier)
 
 
 def total_of(pieces, dtype):
@@ -136,35 +158,33 @@
     evens, odds = tuple(range(0, layers, 2)), tuple(range(1, layers, 2))
 
     half = layers // 2
-    side = lax.axis_index("depth") // half
-    first = lax.dynamic_slice_in_dim(a, (1 - side) * (half * rows), half * rows, 0)
+    first, second = halves_of(a, layers)
     far_first = sent(first, sizes, -1, 1, 0)
     first, a_counts, c_list = lax.optimization_barrier((first, a_counts, c_columns[0, 0].T))
     a_list = live_columns(a_columns[0, 0, 0], a_counts[0, 0, 0], b.shape[0])
     far_a_list = sent(a_list, sizes, -1, 1, 0)
     far_c_list = sent(c_list, sizes, 0, 1, 0)
-    a_later, a_list = lax.optimization_barrier((a, a_list))
-    far_second = sent(near_half(a_later, layers), sizes, -1, 1, 0)
+    far_second = sent(after(second, a_list, GATE), sizes, -1, 1, 0)
 
     def paired(passed, kept):
         met = sent(passed, sizes, 0, 0, 1)
         return [total_of((one, met[at * rows : (at + 1) * rows]), a.dtype) for at, one in enumerate(kept)]
 
-    def far_product(part, order, b_list):
+    def far_product(part, order, far_a_list, b_list):
         order_odds, order_evens = tuple(n for n in order if n % 2), tuple((n,) for n in order if n % 2 == 0)
         passed, *filled = product(half, (order_odds,), part, b, far_a_list, far_c_list, b_list, "far_passed", FAR)
         b_list = filled[0] if filled else b_list
         part, passed = lax.optimization_barrier((part, passed))
-        kept = product(half, order_evens, part, b, far_a_list, far_c_list, b_list, "far_kept", FAR)
-        return paired(passed, kept), b_list
-
-    b_list = live_columns(b_columns[0, 0, 0], b_counts[0, 0, 0], DEAD_B)
-    far, b_list = far_product(far_first, range(half, layers), b_list)
-    a_later, far = lax.optimization_barrier((a_later, far))
-    passed, *kept = product(layers, (odds,) + tuple((n,) for n in evens), a_later, b, a_list, c_list, b_list, "own_product", OWN)
-    far_second, passed = lax.optimization_barrier((far_second, passed))
+        return paired(passed, product(half, order_evens, part, b, far_a_list, far_c_list, b_list, "far_kept", FAR)), b_list
+
+    b_live = live_columns(b_columns[0, 0, 0], b_counts[0, 0, 0], DEAD_B)
+    passed, *kept, _ = product(layers, (odds,) + tuple((n,) for n in evens), a, b, a_list, c_list, b_live, "own_product", OWN)
     own = paired(passed, kept)
-    far = far_product(far_second, range(half), b_list)[0] + far
+    far_first, passed = lax.optimization_barrier((far_first, passed))
+    far, b_list = far_product(far_first, range(half, layers), far_a_list, b_live)
+    far_a_list = after(far_a_list, far[-1], TURN)
+    far_second, own, far_a_list = lax.optimization_barrier((far_second, own, far_a_list))
+    far = far_product(far_second, range(half), far_a_list, b_list)[0] + far
     even = lax.axis_index("depth") % 2 == 0
     pieces = [own[0]] + [sent(one, sizes, 0, -1, n) for one, n in zip(far[len(evens) // 2 :], evens[len(evens) // 2 :])]
     for own_piece, own_n, far_piece, far_n in zip(own[1:], evens[1:], far, evens):

time: 29.8 us -> 29.1 us (0.977)
  waiting for transfers between devices: 7.77 us -> 5.3 us
  other arithmetic: 1.64 us -> 2.64 us
  Pallas kernels: 3.48 us -> 4.26 us
  starting transfers between devices: 14.5 us -> 15 us
  local copies, waits for them, and re-layouts: 2.12 us -> 1.64 us
    ppermute x10, waiting for transfers between devices: 7.77 us -> 5.3 us  [sent(): return lax.ppermute(value, AXES, pairs)]
    convert_element_type x1 -> x2, other arithmetic: 0.03 us -> 1.07 us  [total_of(): return sum((one.astype(jnp.float32) for one in pieces)).astype(dtype)]
    dynamic_slice x1 -> x0, local copies, waits for them, and re-layouts: 0.98 us -> none  [local(): lax.dynamic_slice_in_dim(a, (1 - side) * (half * rows), half * rows, 0)]
    pallas_call x5, Pallas kernels: 3.47 us -> 4.21 us  [product(): pl.pallas_call(functools.partial(product_kernel, groups, count, fills), o...]
    unnamed x14, local copies, waits for them, and re-layouts: 1.07 us -> 1.57 us
    ppermute x10, starting transfers between devices: 14.5 us -> 15 us  [sent(): return lax.ppermute(value, AXES, pairs)]
  transfers between devices with their start and end apart: 10 -> 10, of which waited for: 6 -> 3; matrix products, arithmetic and copies ran while one was open for 3% -> 7% of each run, Pallas kernels for 12% -> 15%
where the time goes in v5:
time: 29.1 us; the launch traced here: 28.9 us
  starting transfers between devices  15 us (52%)
  waiting for transfers between devices  5.3 us (18%)
  Pallas kernels  4.26 us (15%)
  other arithmetic  2.64 us (9%)
  local copies, waits for them, and re-layouts  1.64 us (6%)
    ppermute x10, starting transfers between devices, sent(): return lax.ppermute(value, AXES, pairs)  15 us
    ppermute x10, waiting for transfers between devices, sent(): return lax.ppermute(value, AXES, pairs)  5.3 us
    pallas_call x5, Pallas kernels, product(): pl.pallas_call(functools.partial(product_kernel, groups, count, fills), o...  4.21 us
    unnamed x14, local copies, waits for them, and re-layouts  1.57 us
    convert_element_type x2, other arithmetic, total_of(): return sum((one.astype(jnp.float32) for one in pieces)).astype(dtype)  1.07 us
    broadcast_in_dim x1, other arithmetic, local(): jnp.where(live, total_of(pieces, jnp.float32), 0).astype(a.dtype)  0.74 us
    select_n x2, other arithmetic, live_columns(): jnp.where(jnp.arange(columns.shape[1], dtype=jnp.int32)[:, None] < counts...  0.69 us
  transfers between devices with their start and end apart: 10, of which 3 were waited for; matrix products, arithmetic and copies ran while one was open for 7% of the time, Pallas kernels for 15%

profile of v5, /device:TPU:0, one launch (start us, length us, event | category | flops | bytes accessed | tf_op | source)
XLA Modules:
  0.0 28.9 jit_solution(9551446798890313517)
XLA Ops:
  0.0 0.0 copy-start
  0.0 0.0 copy-start.1
  0.0 1.1 %copy-done.1 = bf16[1,1,1,16,64,256]{5,4,3,2,1,0:T(8,128)(2,1)S(1)} copy-done((bf16[1,1,1,16,64,256]{5,4,3,2,1,0:T(8,128)(2,1)S(1)}, bf16[1,1,1,16,64,256]{5,4,3,2,1,0:T(8,128)(2,1)}, u32[]{:S(2)}) %copy-start.1) | copy-done | bytes 524312
  1.1 4.0 %collective-permute-start.3 = (bf16[8,64,256]{2,1,0:T(8,128)(2,1)S(1)}, bf16[8,64,256]{2,1,0:T(8,128)(2,1)S(1)}, u32[]{:S(2)}, u32[]{:S(2)}) collective-permute-start(bf16[8,64,256]{2,1,0:T(8,128)(2,1)S(1)} %get-tuple-element.24), channel_id=1, source_target_pairs={{0,20},{1,21},{2,22},{3,23},{4,24},{5,25},{6,26},{7,27},{8,28},{9,... | collective-permute-start | bytes 786440 | tf_op jit(solution)/shard_map/ppermute | solution.py:147
  5.1 0.7 %bitcast_select_fusion.earlier.refs_2_ = s32[4,16]{1,0:T(4,128)S(1)} fusion(s32[1,1,1,16,4]{3,4,2,1,0:T(4,128)} %param.9, s32[16]{0:T(128)} %bitcast.28), kind=kLoop, calls=%fused_computation.8 | loop fusion | flops 128 | bytes 576 | tf_op jit(solution)/shard_map/jit(_where)/select_n | solution.py:151
  5.8 1.5 %collective-permute-start.2 = (s32[4,16]{1,0:T(4,128)S(1)}, s32[4,16]{1,0:T(4,128)S(1)}, u32[]{:S(2)}, u32[]{:S(2)}) collective-permute-start(s32[4,16]{1,0:T(4,128)S(1)} %bitcast_select_fusion.earlier.refs_2_), channel_id=1, source_target_pairs={{0,20},{1,21},{2,22},{3,23},{4,24},{5,25},{6,26},{7,27},{8,28},{9,... | collective-permute-start | bytes 776 | tf_op jit(solution)/shard_map/ppermute | solution.py:147
  7.3 1.6 %collective-permute-start.4 = (s32[4,16]{1,0:T(4,128)}, s32[4,16]{1,0:T(4,128)S(1)}, u32[]{:S(2)}, u32[]{:S(2)}) collective-permute-start(s32[4,16]{1,0:T(4,128)} %bitcast.26), channel_id=1, source_target_pairs={{0,4},{1,5},{2,6},{3,7},{4,8},{5,9},{6,10},{7,11},{8,12},{9,13},{1... | collective-permute-start | bytes 776 | tf_op jit(solution)/shard_map/ppermute | solution.py:147
  8.9 0.0 copy-start.5
  8.9 0.0 copy-start.6
  8.9 0.0 copy-start.2
  8.9 0.0 copy-start.3
  8.9 0.0 copy-start.4
  9.0 1.2 %collective-permute-start = (bf16[8,64,256]{2,1,0:T(8,128)(2,1)S(1)}, bf16[8,64,256]{2,1,0:T(8,128)(2,1)S(1)}, u32[]{:S(2)}, u32[]{:S(2)}) collective-permute-start(bf16[8,64,256]{2,1,0:T(8,128)(2,1)S(1)} %after_lists.2), channel_id=1, source_target_pairs={{0,20},{1,21},{2,22},{3,23},{4,24},{5,25},{6,26},{7,27},{8,28},{9,... | collective-permute-start | bytes 786440 | tf_op jit(solution)/shard_map/ppermute | solution.py:147
  10.2 0.0 copy-done.5
  10.2 0.0 copy-done.6
  10.2 0.0 copy-done.2
  10.2 0.5 %copy-done.3 = bf16[1,1,1,128,64,128]{5,4,3,2,1,0:T(8,128)(2,1)S(1)} copy-done((bf16[1,1,1,128,64,128]{5,4,3,2,1,0:T(8,128)(2,1)S(1)}, bf16[1,1,1,128,64,128]{5,4,3,2,1,0:T(8,128)(2,1)}, u32[]{:S(2)}) %copy-start.3) | copy-done | bytes 2097176
  10.7 0.0 copy-done.4
  10.7 2.0 %own_product.1 = (bf16[8,64,256]{2,1,0:T(8,128)(2,1)}, bf16[4,64,256]{2,1,0:T(8,128)(2,1)S(1)}, bf16[4,64,256]{2,1,0:T(8,128)(2,1)S(1)}, s32[272,128]{1,0:T(8,128)}) custom-call(bf16[16,64,256]{2,1,0:T(8,128)(2,1)S(1)} %bitcast.20, bf16[128,64,128]{2,1,0:T(8,128)(2,1)S(1)} %bitcast.21, s32[4,16]{1,0:T(4,128)S(1)} %bitcast_select_fusion.earlier.refs_2_, ...), custom_call_target="tpu_custom_call" | custom-call | flops 134217728 | tf_op jit(solution)/shard_map/own_product/pallas_call | solution.py:84
  12.7 0.0 collective-permute-start.1
  12.8 0.0 copy-done
  12.8 0.1 dynamic-slice_bitcast_fusion
  12.8 0.8 %collective-permute-done.3.refs_0_ = bf16[8,64,256]{2,1,0:T(8,128)(2,1)S(1)} collective-permute-done((bf16[8,64,256]{2,1,0:T(8,128)(2,1)S(1)}, bf16[8,64,256]{2,1,0:T(8,128)(2,1)S(1)}, u32[]{:S(2)}, u32[]{:S(2)}) %collective-permute-start.3) | collective-permute-done | bytes 262176 | tf_op jit(solution)/shard_map/ppermute | solution.py:147
  13.6 0.0 collective-permute-done.2.refs_2_.value
  13.7 0.0 collective-permute-done.4.refs_3_
  13.7 0.6 %far_passed.2 = (bf16[4,64,256]{2,1,0:T(8,128)(2,1)S(1)}, s32[272,128]{1,0:T(8,128)S(1)}) custom-call(bf16[8,64,256]{2,1,0:T(8,128)(2,1)S(1)} %collective-permute-done.3.refs_0_, bf16[128,64,128]{2,1,0:T(8,128)(2,1)S(1)} %bitcast.22, s32[4,16]{1,0:T(4,128)S(1)} %collective-permute-done.2.refs_2_.value, s32[4,16]{1,0:T(4,128)S(1)} %collective-permute-done.4.refs_3_, ...), custom_call_target="tpu_custom_call" | custom-call | flops 3355443200 | tf_op jit(solution)/shard_map/far_passed/pallas_call | solution.py:84
  14.3 0.1 collective-permute-start.5
  14.4 0.5 %far_kept.2 = bf16[4,64,256]{2,1,0:T(8,128)(2,1)S(1)} custom-call(bf16[8,64,256]{2,1,0:T(8,128)(2,1)S(1)} %collective-permute-done.3.refs_0_, bf16[128,64,128]{2,1,0:T(8,128)(2,1)S(1)} %bitcast.23, s32[4,16]{1,0:T(4,128)S(1)} %collective-permute-done.2.refs_2_.value, s32[4,16]{1,0:T(4,128)S(1)} %collective-permute-done.4.refs_3_, ...), custom_call_target="tpu_custom_call" | custom-call | flops 3355443200 | tf_op jit(solution)/shard_map/far_kept/pallas_call | solution.py:84
  14.9 0.0 collective-permute-done.1
  14.9 1.0 %add_convert_fusion.2 = (bf16[4,64,256]{2,1,0:T(8,128)(2,1)S(1)}, bf16[4,64,256]{2,1,0:T(8,128)(2,1)S(1)}) fusion(bf16[4,64,256]{2,1,0:T(8,128)(2,1)S(1)} %get-tuple-element.29, bf16[8,64,256]{2,1,0:T(8,128)(2,1)} %collective-permute-done.1, bf16[4,64,256]{2,1,0:T(8,128)(2,1)S(1)} %get-tuple-element.27), kind=kLoop, calls=%fused_computation.3 | loop fusion | flops 524288 | bytes 786432 | tf_op jit(solution)/shard_map/convert_element_type | solution.py:133
  15.9 0.0 collective-permute-done.5
  16.0 3.9 %collective-permute-start.6 = (bf16[4,64,256]{2,1,0:T(8,128)(2,1)S(1)}, bf16[4,64,256]{2,1,0:T(8,128)(2,1)S(1)}, u32[]{:S(2)}, u32[]{:S(2)}) collective-permute-start(bf16[4,64,256]{2,1,0:T(8,128)(2,1)S(1)} %add_convert_fusion.1.earlier), channel_id=1, source_target_pairs={{0,14},{1,15},{2,12},{3,13},{4,2},{5,3},{6,0},{7,1},{8,6},{9,7},{1... | collective-permute-start | bytes 393224 | tf_op jit(solution)/shard_map/ppermute | solution.py:147
  19.9 0.0 collective-permute-done.refs_0_
  19.9 0.5 %far_passed.3 = bf16[4,64,256]{2,1,0:T(8,128)(2,1)S(1)} custom-call(bf16[8,64,256]{2,1,0:T(8,128)(2,1)S(1)} %collective-permute-done.refs_0_, bf16[128,64,128]{2,1,0:T(8,128)(2,1)S(1)} %bitcast.24, s32[4,16]{1,0:T(4,128)S(1)} %after_lists.3.refs_2_, s32[4,16]{1,0:T(4,128)S(1)} %collective-permute-done.4.refs_3_, s32[272,128]{1,0:T(8,128)S(1)} %get-tuple-element.33.refs_4_), custom_call_target="tpu_custom_call" | custom-call | flops 3355443200 | tf_op jit(solution)/shard_map/far_passed/pallas_call | solution.py:84
  20.4 0.1 collective-permute-start.7
  20.5 0.5 %far_kept.3 = bf16[4,64,256]{2,1,0:T(8,128)(2,1)S(1)} custom-call(bf16[8,64,256]{2,1,0:T(8,128)(2,1)S(1)} %collective-permute-done.refs_0_, bf16[128,64,128]{2,1,0:T(8,128)(2,1)S(1)} %bitcast.25, s32[4,16]{1,0:T(4,128)S(1)} %after_lists.3.refs_2_, s32[4,16]{1,0:T(4,128)S(1)} %collective-permute-done.4.refs_3_, s32[272,128]{1,0:T(8,128)S(1)} %get-tuple-element.33.refs_4_), custom_call_target="tpu_custom_call" | custom-call | flops 3355443200 | tf_op jit(solution)/shard_map/far_kept/pallas_call | solution.py:84
  21.1 0.7 %collective-permute-done.7 = bf16[4,64,256]{2,1,0:T(8,128)(2,1)S(1)} collective-permute-done((bf16[4,64,256]{2,1,0:T(8,128)(2,1)S(1)}, bf16[4,64,256]{2,1,0:T(8,128)(2,1)S(1)}, u32[]{:S(2)}, u32[]{:S(2)}) %collective-permute-start.7) | collective-permute-done | bytes 131104 | tf_op jit(solution)/shard_map/ppermute | solution.py:147
  21.8 0.1 broadcast_select_fusion.1
  21.9 0.8 %collective-permute-start.8 = (bf16[4,64,256]{2,1,0:T(8,128)(2,1)S(1)}, bf16[4,64,256]{2,1,0:T(8,128)(2,1)S(1)}, u32[]{:S(2)}, u32[]{:S(2)}) collective-permute-start(bf16[4,64,256]{2,1,0:T(8,128)(2,1)S(1)} %get-tuple-element.41), channel_id=1, source_target_pairs={{0,2},{1,13},{2,0},{3,15},{4,6},{5,1},{6,4},{7,3},{8,10},{9,5},{10... | collective-permute-start | bytes 393224 | tf_op jit(solution)/shard_map/ppermute | solution.py:147
  22.7 1.7 %collective-permute-start.9 = (bf16[4,64,256]{2,1,0:T(8,128)(2,1)S(1)}, bf16[4,64,256]{2,1,0:T(8,128)(2,1)S(1)}, u32[]{:S(2)}, u32[]{:S(2)}) collective-permute-start(bf16[4,64,256]{2,1,0:T(8,128)(2,1)S(1)} %get-tuple-element.42), channel_id=1, source_target_pairs={{0,12},{1,3},{2,14},{3,1},{4,0},{5,7},{6,2},{7,5},{8,4},{9,11},{10... | collective-permute-start | bytes 393224 | tf_op jit(solution)/shard_map/ppermute | solution.py:147
  24.4 0.1 broadcast_compare_fusion
  24.5 0.0 collective-permute-done.6
  24.5 3.7 %collective-permute-done.8 = bf16[4,64,256]{2,1,0:T(8,128)(2,1)S(1)} collective-permute-done((bf16[4,64,256]{2,1,0:T(8,128)(2,1)S(1)}, bf16[4,64,256]{2,1,0:T(8,128)(2,1)S(1)}, u32[]{:S(2)}, u32[]{:S(2)}) %collective-permute-start.8) | collective-permute-done | bytes 131104 | tf_op jit(solution)/shard_map/ppermute | solution.py:147
  28.2 0.0 collective-permute-done.9
  28.2 0.7 %fusion = bf16[1,1,4,64,256]{4,3,2,1,0:T(8,128)(2,1)} fusion(bf16[4,64,256]{2,1,0:T(8,128)(2,1)S(1)} %collective-permute-done.9, bf16[4,64,256]{2,1,0:T(8,128)(2,1)S(1)} %collective-permute-done.8, bf16[4,64,256]{2,1,0:T(8,128)(2,1)S(1)} %collective-permute-done.6, bf16[4,64,256]{2,1,0:T(8,128)(2,1)S(1)} %get-tuple-element.35, ...), kind=kLoop, calls=%fused_computation.5 | loop fusion | flops 589824 | bytes 656384 | tf_op jit(solution)/shard_map/broadcast_in_dim | solution.py:198
  (6 shorter events, 0.1 us)
Async XLA Ops:
  0.0 12.8 %copy-start = (s32[1,1,16]{2,1,0:T(1,128)S(1)}, s32[1,1,16]{2,1,0:T(1,128)}, u32[]{:S(2)}) copy-start(s32[1,1,16]{2,1,0:T(1,128)} %param.15) | copy-start | bytes 196
  0.0 1.1 %copy-start.1 = (bf16[1,1,1,16,64,256]{5,4,3,2,1,0:T(8,128)(2,1)S(1)}, bf16[1,1,1,16,64,256]{5,4,3,2,1,0:T(8,128)(2,1)}, u32[]{:S(2)}) copy-start(bf16[1,1,1,16,64,256]{5,4,3,2,1,0:T(8,128)(2,1)} %param.8) | copy-start | bytes 1572868
  1.1 12.5 %collective-permute-start.3 = (bf16[8,64,256]{2,1,0:T(8,128)(2,1)S(1)}, bf16[8,64,256]{2,1,0:T(8,128)(2,1)S(1)}, u32[]{:S(2)}, u32[]{:S(2)}) collective-permute-start(bf16[8,64,256]{2,1,0:T(8,128)(2,1)S(1)} %get-tuple-element.24), channel_id=1, source_target_pairs={{0,20},{1,21},{2,22},{3,23},{4,24},{5,25},{6,26},{7,27},{8,28},{9,... | collective-permute-start | bytes 786440 | tf_op jit(solution)/shard_map/ppermute | solution.py:147
  5.8 7.9 %collective-permute-start.2 = (s32[4,16]{1,0:T(4,128)S(1)}, s32[4,16]{1,0:T(4,128)S(1)}, u32[]{:S(2)}, u32[]{:S(2)}) collective-permute-start(s32[4,16]{1,0:T(4,128)S(1)} %bitcast_select_fusion.earlier.refs_2_), channel_id=1, source_target_pairs={{0,20},{1,21},{2,22},{3,23},{4,24},{5,25},{6,26},{7,27},{8,28},{9,... | collective-permute-start | bytes 776 | tf_op jit(solution)/shard_map/ppermute | solution.py:147
  7.3 6.4 %collective-permute-start.4 = (s32[4,16]{1,0:T(4,128)}, s32[4,16]{1,0:T(4,128)S(1)}, u32[]{:S(2)}, u32[]{:S(2)}) collective-permute-start(s32[4,16]{1,0:T(4,128)} %bitcast.26), channel_id=1, source_target_pairs={{0,4},{1,5},{2,6},{3,7},{4,8},{5,9},{6,10},{7,11},{8,12},{9,13},{1... | collective-permute-start | bytes 776 | tf_op jit(solution)/shard_map/ppermute | solution.py:147
  8.9 1.3 %copy-start.5 = (s32[1,1,1,128,2]{3,4,2,1,0:T(2,128)S(1)}, s32[1,1,1,128,2]{3,4,2,1,0:T(2,128)}, u32[]{:S(2)}) copy-start(s32[1,1,1,128,2]{3,4,2,1,0:T(2,128)} %param.12) | copy-start | bytes 3076
  8.9 1.3 %copy-start.6 = (s32[1,1,1,128]{3,2,1,0:T(1,128)S(1)}, s32[1,1,1,128]{3,2,1,0:T(1,128)}, u32[]{:S(2)}) copy-start(s32[1,1,1,128]{3,2,1,0:T(1,128)} %param.13) | copy-start | bytes 1540
  8.9 1.3 %copy-start.2 = (bf16[1,1,1,16,64,256]{5,4,3,2,1,0:T(8,128)(2,1)S(1)}, bf16[1,1,1,16,64,256]{5,4,3,2,1,0:T(8,128)(2,1)}, u32[]{:S(2)}) copy-start(bf16[1,1,1,16,64,256]{5,4,3,2,1,0:T(8,128)(2,1)} %param.8) | copy-start | bytes 1572868
  8.9 1.8 %copy-start.3 = (bf16[1,1,1,128,64,128]{5,4,3,2,1,0:T(8,128)(2,1)S(1)}, bf16[1,1,1,128,64,128]{5,4,3,2,1,0:T(8,128)(2,1)}, u32[]{:S(2)}) copy-start(bf16[1,1,1,128,64,128]{5,4,3,2,1,0:T(8,128)(2,1)} %param.11) | copy-start | bytes 6291460
  8.9 1.8 %copy-start.4 = (s32[1,1,16,4]{2,3,1,0:T(4,128)S(1)}, s32[1,1,16,4]{2,3,1,0:T(4,128)}, u32[]{:S(2)}) copy-start(s32[1,1,16,4]{2,3,1,0:T(4,128)} %param.14) | copy-start | bytes 772
  9.0 10.9 %collective-permute-start = (bf16[8,64,256]{2,1,0:T(8,128)(2,1)S(1)}, bf16[8,64,256]{2,1,0:T(8,128)(2,1)S(1)}, u32[]{:S(2)}, u32[]{:S(2)}) collective-permute-start(bf16[8,64,256]{2,1,0:T(8,128)(2,1)S(1)} %after_lists.2), channel_id=1, source_target_pairs={{0,20},{1,21},{2,22},{3,23},{4,24},{5,25},{6,26},{7,27},{8,28},{9,... | collective-permute-start | bytes 786440 | tf_op jit(solution)/shard_map/ppermute | solution.py:147
  12.7 2.1 %collective-permute-start.1 = (bf16[8,64,256]{2,1,0:T(8,128)(2,1)}, bf16[8,64,256]{2,1,0:T(8,128)(2,1)}, u32[]{:S(2)}, u32[]{:S(2)}) collective-permute-start(bf16[8,64,256]{2,1,0:T(8,128)(2,1)} %get-tuple-element.28), channel_id=1, source_target_pairs={{0,1},{1,0},{2,3},{3,2},{4,5},{5,4},{6,7},{7,6},{8,9},{9,8},{10,11... | collective-permute-start | bytes 786440 | tf_op jit(solution)/shard_map/ppermute | solution.py:147
  14.3 1.7 %collective-permute-start.5 = (bf16[4,64,256]{2,1,0:T(8,128)(2,1)S(1)}, bf16[4,64,256]{2,1,0:T(8,128)(2,1)S(1)}, u32[]{:S(2)}, u32[]{:S(2)}) collective-permute-start(bf16[4,64,256]{2,1,0:T(8,128)(2,1)S(1)} %get-tuple-element.34), channel_id=1, source_target_pairs={{0,1},{1,0},{2,3},{3,2},{4,5},{5,4},{6,7},{7,6},{8,9},{9,8},{10,11... | collective-permute-start | bytes 393224 | tf_op jit(solution)/shard_map/ppermute | solution.py:147
  16.0 8.5 %collective-permute-start.6 = (bf16[4,64,256]{2,1,0:T(8,128)(2,1)S(1)}, bf16[4,64,256]{2,1,0:T(8,128)(2,1)S(1)}, u32[]{:S(2)}, u32[]{:S(2)}) collective-permute-start(bf16[4,64,256]{2,1,0:T(8,128)(2,1)S(1)} %add_convert_fusion.1.earlier), channel_id=1, source_target_pairs={{0,14},{1,15},{2,12},{3,13},{4,2},{5,3},{6,0},{7,1},{8,6},{9,7},{1... | collective-permute-start | bytes 393224 | tf_op jit(solution)/shard_map/ppermute | solution.py:147
  20.4 1.4 %collective-permute-start.7 = (bf16[4,64,256]{2,1,0:T(8,128)(2,1)S(1)}, bf16[4,64,256]{2,1,0:T(8,128)(2,1)S(1)}, u32[]{:S(2)}, u32[]{:S(2)}) collective-permute-start(bf16[4,64,256]{2,1,0:T(8,128)(2,1)S(1)} %far_passed.3), channel_id=1, source_target_pairs={{0,1},{1,0},{2,3},{3,2},{4,5},{5,4},{6,7},{7,6},{8,9},{9,8},{10,11... | collective-permute-start | bytes 393224 | tf_op jit(solution)/shard_map/ppermute | solution.py:147
  21.9 6.3 %collective-permute-start.8 = (bf16[4,64,256]{2,1,0:T(8,128)(2,1)S(1)}, bf16[4,64,256]{2,1,0:T(8,128)(2,1)S(1)}, u32[]{:S(2)}, u32[]{:S(2)}) collective-permute-start(bf16[4,64,256]{2,1,0:T(8,128)(2,1)S(1)} %get-tuple-element.41), channel_id=1, source_target_pairs={{0,2},{1,13},{2,0},{3,15},{4,6},{5,1},{6,4},{7,3},{8,10},{9,5},{10... | collective-permute-start | bytes 393224 | tf_op jit(solution)/shard_map/ppermute | solution.py:147
  22.7 5.5 %collective-permute-start.9 = (bf16[4,64,256]{2,1,0:T(8,128)(2,1)S(1)}, bf16[4,64,256]{2,1,0:T(8,128)(2,1)S(1)}, u32[]{:S(2)}, u32[]{:S(2)}) collective-permute-start(bf16[4,64,256]{2,1,0:T(8,128)(2,1)S(1)} %get-tuple-element.42), channel_id=1, source_target_pairs={{0,12},{1,3},{2,14},{3,1},{4,0},{5,7},{6,2},{7,5},{8,4},{9,11},{10... | collective-permute-start | bytes 393224 | tf_op jit(solution)/shard_map/ppermute | solution.py:147

commit v6 on v5

--- a/solution.py
+++ b/solution.py
@@ -185,13 +185,8 @@
     far_a_list = after(far_a_list, far[-1], TURN)
     far_second, own, far_a_list = lax.optimization_barrier((far_second, own, far_a_list))
     far = far_product(far_second, range(half), far_a_list, b_list)[0] + far
-    even = lax.axis_index("depth") % 2 == 0
-    pieces = [own[0]] + [sent(one, sizes, 0, -1, n) for one, n in zip(far[len(evens) // 2 :], evens[len(evens) // 2 :])]
-    for own_piece, own_n, far_piece, far_n in zip(own[1:], evens[1:], far, evens):
-        for own_side in (0, 1):
-            moves = ((0, 0, own_n), (0, -1, far_n)) if own_side == 0 else ((0, -1, far_n), (0, 0, own_n))
-            mixed = jnp.where(even == (own_side == 0), own_piece, far_piece)
-            pieces.append(sent(mixed, sizes, *zip(*moves)))
+    pieces = [own[0]] + [sent(one, sizes, 0, 0, n) for one, n in zip(own[1:], evens[1:])]
+    pieces += [sent(one, sizes, 0, -1, n) for one, n in zip(far, evens)]
     counts = lax.dynamic_slice_in_dim(c_counts[0, 0], lax.axis_index("depth") * rows, rows, 0)
     slot = jnp.arange(c_list.shape[0] * b.shape[1], dtype=jnp.int32) // b.shape[1]
     live = slot[None, None, :] < counts[:, None, None]

time: 29.1 us -> 28.5 us (0.979)
  waiting for transfers between devices: 5.3 us -> 4.67 us
    ppermute x10, waiting for transfers between devices: 5.3 us -> 4.67 us  [sent(): return lax.ppermute(value, AXES, pairs)]
    convert_element_type x2 -> x3, other arithmetic: 1.07 us -> 1.11 us  [total_of(): return sum((one.astype(jnp.float32) for one in pieces)).astype(dtype)]
where the time goes in v6:
time: 28.5 us; the launch traced here: 28.3 us
  starting transfers between devices  15 us (53%)
  waiting for transfers between devices  4.67 us (16%)
  Pallas kernels  4.27 us (15%)
  other arithmetic  2.61 us (9%)
  local copies, waits for them, and re-layouts  1.64 us (6%)
    ppermute x10, starting transfers between devices, sent(): return lax.ppermute(value, AXES, pairs)  15 us
    ppermute x10, waiting for transfers between devices, sent(): return lax.ppermute(value, AXES, pairs)  4.67 us
    pallas_call x5, Pallas kernels, product(): pl.pallas_call(functools.partial(product_kernel, groups, count, fills), o...  4.21 us
    unnamed x14, local copies, waits for them, and re-layouts  1.57 us
    convert_element_type x3, other arithmetic, total_of(): return sum((one.astype(jnp.float32) for one in pieces)).astype(dtype)  1.11 us
    broadcast_in_dim x1, other arithmetic, local(): jnp.where(live, total_of(pieces, jnp.float32), 0).astype(a.dtype)  0.74 us
    select_n x2, other arithmetic, live_columns(): jnp.where(jnp.arange(columns.shape[1], dtype=jnp.int32)[:, None] < counts...  0.69 us
  transfers between devices with their start and end apart: 10, of which 3 were waited for; matrix products, arithmetic and copies ran while one was open for 7% of the time, Pallas kernels for 15%

profile of v6, /device:TPU:0, one launch (start us, length us, event | category | flops | bytes accessed | tf_op | source)
XLA Modules:
  0.0 28.3 jit_solution(13722956700966042424)
XLA Ops:
  0.0 0.0 copy-start
  0.0 0.0 copy-start.1
  0.0 1.1 %copy-done.1 = bf16[1,1,1,16,64,256]{5,4,3,2,1,0:T(8,128)(2,1)S(1)} copy-done((bf16[1,1,1,16,64,256]{5,4,3,2,1,0:T(8,128)(2,1)S(1)}, bf16[1,1,1,16,64,256]{5,4,3,2,1,0:T(8,128)(2,1)}, u32[]{:S(2)}) %copy-start.1) | copy-done | bytes 524312
  1.1 4.0 %collective-permute-start.3 = (bf16[8,64,256]{2,1,0:T(8,128)(2,1)S(1)}, bf16[8,64,256]{2,1,0:T(8,128)(2,1)S(1)}, u32[]{:S(2)}, u32[]{:S(2)}) collective-permute-start(bf16[8,64,256]{2,1,0:T(8,128)(2,1)S(1)} %get-tuple-element.24), channel_id=1, source_target_pairs={{0,20},{1,21},{2,22},{3,23},{4,24},{5,25},{6,26},{7,27},{8,28},{9,... | collective-permute-start | bytes 786440 | tf_op jit(solution)/shard_map/ppermute | solution.py:147
  5.1 0.7 %bitcast_select_fusion.earlier.refs_2_ = s32[4,16]{1,0:T(4,128)S(1)} fusion(s32[1,1,1,16,4]{3,4,2,1,0:T(4,128)} %param.9, s32[16]{0:T(128)} %bitcast.28), kind=kLoop, calls=%fused_computation.6 | loop fusion | flops 128 | bytes 576 | tf_op jit(solution)/shard_map/jit(_where)/select_n | solution.py:151
  5.8 1.5 %collective-permute-start.2 = (s32[4,16]{1,0:T(4,128)S(1)}, s32[4,16]{1,0:T(4,128)S(1)}, u32[]{:S(2)}, u32[]{:S(2)}) collective-permute-start(s32[4,16]{1,0:T(4,128)S(1)} %bitcast_select_fusion.earlier.refs_2_), channel_id=1, source_target_pairs={{0,20},{1,21},{2,22},{3,23},{4,24},{5,25},{6,26},{7,27},{8,28},{9,... | collective-permute-start | bytes 776 | tf_op jit(solution)/shard_map/ppermute | solution.py:147
  7.3 1.6 %collective-permute-start.4 = (s32[4,16]{1,0:T(4,128)}, s32[4,16]{1,0:T(4,128)S(1)}, u32[]{:S(2)}, u32[]{:S(2)}) collective-permute-start(s32[4,16]{1,0:T(4,128)} %bitcast.26), channel_id=1, source_target_pairs={{0,4},{1,5},{2,6},{3,7},{4,8},{5,9},{6,10},{7,11},{8,12},{9,13},{1... | collective-permute-start | bytes 776 | tf_op jit(solution)/shard_map/ppermute | solution.py:147
  8.9 0.0 copy-start.5
  8.9 0.0 copy-start.6
  8.9 0.0 copy-start.2
  8.9 0.0 copy-start.3
  8.9 0.0 copy-start.4
  9.0 1.2 %collective-permute-start = (bf16[8,64,256]{2,1,0:T(8,128)(2,1)S(1)}, bf16[8,64,256]{2,1,0:T(8,128)(2,1)S(1)}, u32[]{:S(2)}, u32[]{:S(2)}) collective-permute-start(bf16[8,64,256]{2,1,0:T(8,128)(2,1)S(1)} %after_lists.2), channel_id=1, source_target_pairs={{0,20},{1,21},{2,22},{3,23},{4,24},{5,25},{6,26},{7,27},{8,28},{9,... | collective-permute-start | bytes 786440 | tf_op jit(solution)/shard_map/ppermute | solution.py:147
  10.2 0.0 copy-done.5
  10.2 0.0 copy-done.6
  10.2 0.0 copy-done.2
  10.2 0.5 %copy-done.3 = bf16[1,1,1,128,64,128]{5,4,3,2,1,0:T(8,128)(2,1)S(1)} copy-done((bf16[1,1,1,128,64,128]{5,4,3,2,1,0:T(8,128)(2,1)S(1)}, bf16[1,1,1,128,64,128]{5,4,3,2,1,0:T(8,128)(2,1)}, u32[]{:S(2)}) %copy-start.3) | copy-done | bytes 2097176
  10.7 0.0 copy-done.4
  10.7 2.0 %own_product.1 = (bf16[8,64,256]{2,1,0:T(8,128)(2,1)}, bf16[4,64,256]{2,1,0:T(8,128)(2,1)S(1)}, bf16[4,64,256]{2,1,0:T(8,128)(2,1)S(1)}, s32[272,128]{1,0:T(8,128)}) custom-call(bf16[16,64,256]{2,1,0:T(8,128)(2,1)S(1)} %bitcast.20, bf16[128,64,128]{2,1,0:T(8,128)(2,1)S(1)} %bitcast.21, s32[4,16]{1,0:T(4,128)S(1)} %bitcast_select_fusion.earlier.refs_2_, ...), custom_call_target="tpu_custom_call" | custom-call | flops 134217728 | tf_op jit(solution)/shard_map/own_product/pallas_call | solution.py:84
  12.8 0.0 collective-permute-start.1
  12.8 0.0 copy-done
  12.8 0.1 dynamic-slice_bitcast_fusion
  12.8 0.8 %collective-permute-done.3.refs_0_ = bf16[8,64,256]{2,1,0:T(8,128)(2,1)S(1)} collective-permute-done((bf16[8,64,256]{2,1,0:T(8,128)(2,1)S(1)}, bf16[8,64,256]{2,1,0:T(8,128)(2,1)S(1)}, u32[]{:S(2)}, u32[]{:S(2)}) %collective-permute-start.3) | collective-permute-done | bytes 262176 | tf_op jit(solution)/shard_map/ppermute | solution.py:147
  13.6 0.0 collective-permute-done.2.refs_2_.value
  13.7 0.0 collective-permute-done.4.refs_3_
  13.7 0.6 %far_passed.2 = (bf16[4,64,256]{2,1,0:T(8,128)(2,1)S(1)}, s32[272,128]{1,0:T(8,128)S(1)}) custom-call(bf16[8,64,256]{2,1,0:T(8,128)(2,1)S(1)} %collective-permute-done.3.refs_0_, bf16[128,64,128]{2,1,0:T(8,128)(2,1)S(1)} %bitcast.22, s32[4,16]{1,0:T(4,128)S(1)} %collective-permute-done.2.refs_2_.value, s32[4,16]{1,0:T(4,128)S(1)} %collective-permute-done.4.refs_3_, ...), custom_call_target="tpu_custom_call" | custom-call | flops 3355443200 | tf_op jit(solution)/shard_map/far_passed/pallas_call | solution.py:84
  14.3 0.1 collective-permute-start.5
  14.3 0.5 %far_kept.2 = bf16[4,64,256]{2,1,0:T(8,128)(2,1)S(1)} custom-call(bf16[8,64,256]{2,1,0:T(8,128)(2,1)S(1)} %collective-permute-done.3.refs_0_, bf16[128,64,128]{2,1,0:T(8,128)(2,1)S(1)} %bitcast.23, s32[4,16]{1,0:T(4,128)S(1)} %collective-permute-done.2.refs_2_.value, s32[4,16]{1,0:T(4,128)S(1)} %collective-permute-done.4.refs_3_, ...), custom_call_target="tpu_custom_call" | custom-call | flops 3355443200 | tf_op jit(solution)/shard_map/far_kept/pallas_call | solution.py:84
  14.9 0.0 collective-permute-done.1
  14.9 1.0 %add_convert_fusion.2 = (bf16[4,64,256]{2,1,0:T(8,128)(2,1)S(1)}, bf16[4,64,256]{2,1,0:T(8,128)(2,1)S(1)}) fusion(bf16[4,64,256]{2,1,0:T(8,128)(2,1)S(1)} %get-tuple-element.29, bf16[8,64,256]{2,1,0:T(8,128)(2,1)} %collective-permute-done.1, bf16[4,64,256]{2,1,0:T(8,128)(2,1)S(1)} %get-tuple-element.27), kind=kLoop, calls=%fused_computation.3 | loop fusion | flops 524288 | bytes 786432 | tf_op jit(solution)/shard_map/convert_element_type | solution.py:133
  15.9 0.0 collective-permute-done.5
  16.0 3.9 %collective-permute-start.9 = (bf16[4,64,256]{2,1,0:T(8,128)(2,1)S(1)}, bf16[4,64,256]{2,1,0:T(8,128)(2,1)S(1)}, u32[]{:S(2)}, u32[]{:S(2)}) collective-permute-start(bf16[4,64,256]{2,1,0:T(8,128)(2,1)S(1)} %add_convert_fusion.1.earlier), channel_id=1, source_target_pairs={{0,14},{1,15},{2,12},{3,13},{4,2},{5,3},{6,0},{7,1},{8,6},{9,7},{1... | collective-permute-start | bytes 393224 | tf_op jit(solution)/shard_map/ppermute | solution.py:147
  19.9 0.0 collective-permute-done.refs_0_
  19.9 0.5 %far_passed.3 = bf16[4,64,256]{2,1,0:T(8,128)(2,1)S(1)} custom-call(bf16[8,64,256]{2,1,0:T(8,128)(2,1)S(1)} %collective-permute-done.refs_0_, bf16[128,64,128]{2,1,0:T(8,128)(2,1)S(1)} %bitcast.24, s32[4,16]{1,0:T(4,128)S(1)} %after_lists.3.refs_2_, s32[4,16]{1,0:T(4,128)S(1)} %collective-permute-done.4.refs_3_, s32[272,128]{1,0:T(8,128)S(1)} %get-tuple-element.33.refs_4_), custom_call_target="tpu_custom_call" | custom-call | flops 3355443200 | tf_op jit(solution)/shard_map/far_passed/pallas_call | solution.py:84
  20.4 0.1 collective-permute-start.7
  20.5 0.8 %collective-permute-start.6 = (bf16[4,64,256]{2,1,0:T(8,128)(2,1)S(1)}, bf16[4,64,256]{2,1,0:T(8,128)(2,1)S(1)}, u32[]{:S(2)}, u32[]{:S(2)}) collective-permute-start(bf16[4,64,256]{2,1,0:T(8,128)(2,1)S(1)} %get-tuple-element.36), channel_id=1, source_target_pairs={{0,2},{1,3},{2,0},{3,1},{4,6},{5,7},{6,4},{7,5},{8,10},{9,11},{10,... | collective-permute-start | bytes 393224 | tf_op jit(solution)/shard_map/ppermute | solution.py:147
  21.3 0.5 %far_kept.3 = bf16[4,64,256]{2,1,0:T(8,128)(2,1)S(1)} custom-call(bf16[8,64,256]{2,1,0:T(8,128)(2,1)S(1)} %collective-permute-done.refs_0_, bf16[128,64,128]{2,1,0:T(8,128)(2,1)S(1)} %bitcast.25, s32[4,16]{1,0:T(4,128)S(1)} %after_lists.3.refs_2_, s32[4,16]{1,0:T(4,128)S(1)} %collective-permute-done.4.refs_3_, s32[272,128]{1,0:T(8,128)S(1)} %get-tuple-element.33.refs_4_), custom_call_target="tpu_custom_call" | custom-call | flops 3355443200 | tf_op jit(solution)/shard_map/far_kept/pallas_call | solution.py:84
  21.9 0.0 collective-permute-done.7
  21.9 1.7 %collective-permute-start.8 = (bf16[4,64,256]{2,1,0:T(8,128)(2,1)S(1)}, bf16[4,64,256]{2,1,0:T(8,128)(2,1)S(1)}, u32[]{:S(2)}, u32[]{:S(2)}) collective-permute-start(bf16[4,64,256]{2,1,0:T(8,128)(2,1)S(1)} %add_convert_fusion), channel_id=1, source_target_pairs={{0,12},{1,13},{2,14},{3,15},{4,0},{5,1},{6,2},{7,3},{8,4},{9,5},{1... | collective-permute-start | bytes 393224 | tf_op jit(solution)/shard_map/ppermute | solution.py:147
  23.7 0.1 broadcast_compare_fusion
  23.7 0.0 collective-permute-done.9
  23.7 2.6 %collective-permute-done.6 = bf16[4,64,256]{2,1,0:T(8,128)(2,1)S(1)} collective-permute-done((bf16[4,64,256]{2,1,0:T(8,128)(2,1)S(1)}, bf16[4,64,256]{2,1,0:T(8,128)(2,1)S(1)}, u32[]{:S(2)}, u32[]{:S(2)}) %collective-permute-start.6) | collective-permute-done | bytes 131104 | tf_op jit(solution)/shard_map/ppermute | solution.py:147
  26.4 1.2 %collective-permute-done.8 = bf16[4,64,256]{2,1,0:T(8,128)(2,1)S(1)} collective-permute-done((bf16[4,64,256]{2,1,0:T(8,128)(2,1)S(1)}, bf16[4,64,256]{2,1,0:T(8,128)(2,1)S(1)}, u32[]{:S(2)}, u32[]{:S(2)}) %collective-permute-start.8) | collective-permute-done | bytes 131104 | tf_op jit(solution)/shard_map/ppermute | solution.py:147
  27.6 0.7 %fusion = bf16[1,1,4,64,256]{4,3,2,1,0:T(8,128)(2,1)} fusion(bf16[4,64,256]{2,1,0:T(8,128)(2,1)S(1)} %collective-permute-done.9, bf16[4,64,256]{2,1,0:T(8,128)(2,1)S(1)} %collective-permute-done.8, bf16[4,64,256]{2,1,0:T(8,128)(2,1)S(1)} %collective-permute-done.6, bf16[4,64,256]{2,1,0:T(8,128)(2,1)S(1)} %get-tuple-element.35, ...), kind=kLoop, calls=%fused_computation.5 | loop fusion | flops 589824 | bytes 656384 | tf_op jit(solution)/shard_map/broadcast_in_dim | solution.py:193
  (7 shorter events, 0.1 us)
Async XLA Ops:
  0.0 12.8 %copy-start = (s32[1,1,16]{2,1,0:T(1,128)S(1)}, s32[1,1,16]{2,1,0:T(1,128)}, u32[]{:S(2)}) copy-start(s32[1,1,16]{2,1,0:T(1,128)} %param.15) | copy-start | bytes 196
  0.0 1.1 %copy-start.1 = (bf16[1,1,1,16,64,256]{5,4,3,2,1,0:T(8,128)(2,1)S(1)}, bf16[1,1,1,16,64,256]{5,4,3,2,1,0:T(8,128)(2,1)}, u32[]{:S(2)}) copy-start(bf16[1,1,1,16,64,256]{5,4,3,2,1,0:T(8,128)(2,1)} %param.8) | copy-start | bytes 1572868
  1.1 12.5 %collective-permute-start.3 = (bf16[8,64,256]{2,1,0:T(8,128)(2,1)S(1)}, bf16[8,64,256]{2,1,0:T(8,128)(2,1)S(1)}, u32[]{:S(2)}, u32[]{:S(2)}) collective-permute-start(bf16[8,64,256]{2,1,0:T(8,128)(2,1)S(1)} %get-tuple-element.24), channel_id=1, source_target_pairs={{0,20},{1,21},{2,22},{3,23},{4,24},{5,25},{6,26},{7,27},{8,28},{9,... | collective-permute-start | bytes 786440 | tf_op jit(solution)/shard_map/ppermute | solution.py:147
  5.8 7.9 %collective-permute-start.2 = (s32[4,16]{1,0:T(4,128)S(1)}, s32[4,16]{1,0:T(4,128)S(1)}, u32[]{:S(2)}, u32[]{:S(2)}) collective-permute-start(s32[4,16]{1,0:T(4,128)S(1)} %bitcast_select_fusion.earlier.refs_2_), channel_id=1, source_target_pairs={{0,20},{1,21},{2,22},{3,23},{4,24},{5,25},{6,26},{7,27},{8,28},{9,... | collective-permute-start | bytes 776 | tf_op jit(solution)/shard_map/ppermute | solution.py:147
  7.3 6.4 %collective-permute-start.4 = (s32[4,16]{1,0:T(4,128)}, s32[4,16]{1,0:T(4,128)S(1)}, u32[]{:S(2)}, u32[]{:S(2)}) collective-permute-start(s32[4,16]{1,0:T(4,128)} %bitcast.26), channel_id=1, source_target_pairs={{0,4},{1,5},{2,6},{3,7},{4,8},{5,9},{6,10},{7,11},{8,12},{9,13},{1... | collective-permute-start | bytes 776 | tf_op jit(solution)/shard_map/ppermute | solution.py:147
  8.9 1.3 %copy-start.5 = (s32[1,1,1,128,2]{3,4,2,1,0:T(2,128)S(1)}, s32[1,1,1,128,2]{3,4,2,1,0:T(2,128)}, u32[]{:S(2)}) copy-start(s32[1,1,1,128,2]{3,4,2,1,0:T(2,128)} %param.12) | copy-start | bytes 3076
  8.9 1.3 %copy-start.6 = (s32[1,1,1,128]{3,2,1,0:T(1,128)S(1)}, s32[1,1,1,128]{3,2,1,0:T(1,128)}, u32[]{:S(2)}) copy-start(s32[1,1,1,128]{3,2,1,0:T(1,128)} %param.13) | copy-start | bytes 1540
  8.9 1.3 %copy-start.2 = (bf16[1,1,1,16,64,256]{5,4,3,2,1,0:T(8,128)(2,1)S(1)}, bf16[1,1,1,16,64,256]{5,4,3,2,1,0:T(8,128)(2,1)}, u32[]{:S(2)}) copy-start(bf16[1,1,1,16,64,256]{5,4,3,2,1,0:T(8,128)(2,1)} %param.8) | copy-start | bytes 1572868
  8.9 1.8 %copy-start.3 = (bf16[1,1,1,128,64,128]{5,4,3,2,1,0:T(8,128)(2,1)S(1)}, bf16[1,1,1,128,64,128]{5,4,3,2,1,0:T(8,128)(2,1)}, u32[]{:S(2)}) copy-start(bf16[1,1,1,128,64,128]{5,4,3,2,1,0:T(8,128)(2,1)} %param.11) | copy-start | bytes 6291460
  8.9 1.8 %copy-start.4 = (s32[1,1,16,4]{2,3,1,0:T(4,128)S(1)}, s32[1,1,16,4]{2,3,1,0:T(4,128)}, u32[]{:S(2)}) copy-start(s32[1,1,16,4]{2,3,1,0:T(4,128)} %param.14) | copy-start | bytes 772
  9.0 10.9 %collective-permute-start = (bf16[8,64,256]{2,1,0:T(8,128)(2,1)S(1)}, bf16[8,64,256]{2,1,0:T(8,128)(2,1)S(1)}, u32[]{:S(2)}, u32[]{:S(2)}) collective-permute-start(bf16[8,64,256]{2,1,0:T(8,128)(2,1)S(1)} %after_lists.2), channel_id=1, source_target_pairs={{0,20},{1,21},{2,22},{3,23},{4,24},{5,25},{6,26},{7,27},{8,28},{9,... | collective-permute-start | bytes 786440 | tf_op jit(solution)/shard_map/ppermute | solution.py:147
  12.8 2.1 %collective-permute-start.1 = (bf16[8,64,256]{2,1,0:T(8,128)(2,1)}, bf16[8,64,256]{2,1,0:T(8,128)(2,1)}, u32[]{:S(2)}, u32[]{:S(2)}) collective-permute-start(bf16[8,64,256]{2,1,0:T(8,128)(2,1)} %get-tuple-element.28), channel_id=1, source_target_pairs={{0,1},{1,0},{2,3},{3,2},{4,5},{5,4},{6,7},{7,6},{8,9},{9,8},{10,11... | collective-permute-start | bytes 786440 | tf_op jit(solution)/shard_map/ppermute | solution.py:147
  14.3 1.7 %collective-permute-start.5 = (bf16[4,64,256]{2,1,0:T(8,128)(2,1)S(1)}, bf16[4,64,256]{2,1,0:T(8,128)(2,1)S(1)}, u32[]{:S(2)}, u32[]{:S(2)}) collective-permute-start(bf16[4,64,256]{2,1,0:T(8,128)(2,1)S(1)} %get-tuple-element.34), channel_id=1, source_target_pairs={{0,1},{1,0},{2,3},{3,2},{4,5},{5,4},{6,7},{7,6},{8,9},{9,8},{10,11... | collective-permute-start | bytes 393224 | tf_op jit(solution)/shard_map/ppermute | solution.py:147
  16.0 7.7 %collective-permute-start.9 = (bf16[4,64,256]{2,1,0:T(8,128)(2,1)S(1)}, bf16[4,64,256]{2,1,0:T(8,128)(2,1)S(1)}, u32[]{:S(2)}, u32[]{:S(2)}) collective-permute-start(bf16[4,64,256]{2,1,0:T(8,128)(2,1)S(1)} %add_convert_fusion.1.earlier), channel_id=1, source_target_pairs={{0,14},{1,15},{2,12},{3,13},{4,2},{5,3},{6,0},{7,1},{8,6},{9,7},{1... | collective-permute-start | bytes 393224 | tf_op jit(solution)/shard_map/ppermute | solution.py:147
  20.4 1.5 %collective-permute-start.7 = (bf16[4,64,256]{2,1,0:T(8,128)(2,1)S(1)}, bf16[4,64,256]{2,1,0:T(8,128)(2,1)S(1)}, u32[]{:S(2)}, u32[]{:S(2)}) collective-permute-start(bf16[4,64,256]{2,1,0:T(8,128)(2,1)S(1)} %far_passed.3), channel_id=1, source_target_pairs={{0,1},{1,0},{2,3},{3,2},{4,5},{5,4},{6,7},{7,6},{8,9},{9,8},{10,11... | collective-permute-start | bytes 393224 | tf_op jit(solution)/shard_map/ppermute | solution.py:147
  20.5 5.8 %collective-permute-start.6 = (bf16[4,64,256]{2,1,0:T(8,128)(2,1)S(1)}, bf16[4,64,256]{2,1,0:T(8,128)(2,1)S(1)}, u32[]{:S(2)}, u32[]{:S(2)}) collective-permute-start(bf16[4,64,256]{2,1,0:T(8,128)(2,1)S(1)} %get-tuple-element.36), channel_id=1, source_target_pairs={{0,2},{1,3},{2,0},{3,1},{4,6},{5,7},{6,4},{7,5},{8,10},{9,11},{10,... | collective-permute-start | bytes 393224 | tf_op jit(solution)/shard_map/ppermute | solution.py:147
  21.9 5.6 %collective-permute-start.8 = (bf16[4,64,256]{2,1,0:T(8,128)(2,1)S(1)}, bf16[4,64,256]{2,1,0:T(8,128)(2,1)S(1)}, u32[]{:S(2)}, u32[]{:S(2)}) collective-permute-start(bf16[4,64,256]{2,1,0:T(8,128)(2,1)S(1)} %add_convert_fusion), channel_id=1, source_target_pairs={{0,12},{1,13},{2,14},{3,15},{4,0},{5,1},{6,2},{7,3},{8,4},{9,5},{1... | collective-permute-start | bytes 393224 | tf_op jit(solution)/shard_map/ppermute | solution.py:147
